TPU v7x, 32 devices: a whole 2x2x4 slice. The times are simulated.
32 devices in a mesh: ctx: 8 (over y, x, core), ch: 4 (over z).
Axes of the slice: x: 2, y: 2, z: 4, core: 2. Of those that a mesh axis runs over, the one named last changes fastest.
Arguments:
- query_short: bfloat16 [1024, 8192], P('ctx', 'ch'), may hold values from -6 to 6
- key_short: bfloat16 [1024, 8192], P('ctx', 'ch'), may hold values from -6 to 6
- value_short: bfloat16 [1024, 8192], P('ctx', 'ch'), may hold values from -6 to 6
- short_taps: float32 [128, 8192], P(None, 'ch'), may hold values from -0.5 to 0.5
- query_long: bfloat16 [1024, 8192], P('ctx', 'ch'), may hold values from -6 to 6
- key_long: bfloat16 [1024, 8192], P('ctx', 'ch'), may hold values from -6 to 6
- long_residue: float32 [16, 8192], P(None, 'ch'), may hold values from -0.5 to 0.5
- long_rate: float32 [16, 8192], P(None, 'ch'), may hold values from 0.0009765625 to 0.05
- cotangent: bfloat16 [1024, 8192], P('ctx', 'ch'), may hold values from -6 to 6
Outputs:
- core_output: bfloat16 [1024, 8192], P('ctx', 'ch')
- query_short_grad: bfloat16 [1024, 8192], P('ctx', 'ch')
- key_short_grad: bfloat16 [1024, 8192], P('ctx', 'ch')
- value_short_grad: bfloat16 [1024, 8192], P('ctx', 'ch')
- query_long_grad: bfloat16 [1024, 8192], P('ctx', 'ch')
- key_long_grad: bfloat16 [1024, 8192], P('ctx', 'ch')
- taps_grad: float32 [128, 8192], P(None, 'ch')
All inputs are finite; a program needn't handle non-finite values.
Results may differ from a plain program's by a relative error of at most 0.0064.
Values may be sent and summed in bfloat16 or wider, within the bound.
No kernel may reach another device: no remote copies, remote signals or barrier semaphores. Data moves between devices by JAX's collectives and lax.ppermute only.
A program may use at most 128 MiB of HBM per device.

v0:
```python
import jax
import jax.numpy as jnp
import numpy as np
from jax import lax
from jax.experimental import pallas as pl
from jax.experimental.pallas import tpu as pltpu
from jax.sharding import PartitionSpec as P

ROWS = 8
LANES = 128
VMEM_BYTES = 48 * 1024 * 1024


def split_np(matrix):
    high = matrix.astype(jnp.bfloat16)
    low = (matrix - high.astype(np.float64)).astype(jnp.bfloat16)
    return high, low


def tables(block):
    length = 2 * block
    freq = np.pi * (2 * np.arange(block)[:, None] + 1) / length
    here = freq * np.arange(block)[None, :]
    after = freq * (np.arange(block)[None, :] + block)
    own = np.concatenate([np.cos(here), -np.sin(here)], axis=0)
    nxt = np.concatenate([np.cos(after), -np.sin(after)], axis=0)
    own_hi, own_lo = split_np(own)
    nxt_hi, nxt_lo = split_np(nxt)
    own_two = np.concatenate([own_hi, own_lo], axis=1)
    own_three = np.concatenate([own_hi, own_hi, own_lo], axis=1)
    nxt_two = np.concatenate([nxt_hi, nxt_lo], axis=1)
    back = np.concatenate([own_hi.T, own_lo.T], axis=0)
    return own_two, own_three, nxt_two, back


def mxu(matrix, data):
    return lax.dot_general(
        matrix, data, (((1,), (0,)), ((), ())), preferred_element_type=jnp.float32
    )


def split(value):
    high = value.astype(jnp.bfloat16)
    low = (value - high.astype(jnp.float32)).astype(jnp.bfloat16)
    return high, low


def dft_exact(matrix_two, data):
    return mxu(matrix_two, jnp.concatenate([data, data], axis=0))


def dft_full(matrix_three, data):
    high, low = split(data)
    return mxu(matrix_three, jnp.concatenate([high, low, high], axis=0))


def dft_back(back, spec_re, spec_im):
    block = spec_re.shape[0]
    high, low = split(jnp.concatenate([spec_re, spec_im], axis=0))
    both = mxu(back, high)
    return both[:block] + both[block:] + mxu(back[:block], low)


def halves(spec):
    block = spec.shape[0] // 2
    return spec[:block], spec[block:]


def times(left, right):
    left_re, left_im = halves(left)
    right_re, right_im = halves(right)
    return left_re * right_re - left_im * right_im, left_re * right_im + left_im * right_re


def times_conj(left, right):
    left_re, left_im = halves(left)
    right_re, right_im = halves(right)
    return left_re * right_re + left_im * right_im, left_im * right_re - left_re * right_im


def sublane(shape):
    return lax.broadcasted_iota(jnp.int32, shape, 0).astype(jnp.float32)


def spread(row):
    return jnp.broadcast_to(row, (ROWS, row.shape[1]))


def mode_sum(rate, weight, start, forward, block):
    sub = sublane((ROWS, rate.shape[1]))
    age = start + (sub if forward else ROWS - 1 - sub)
    waves, falls = [], []
    for mode in range(rate.shape[0]):
        pace = spread(rate[mode : mode + 1])
        waves.append(spread(weight[mode : mode + 1]) * jnp.exp(-pace * age))
        falls.append(jnp.exp(-ROWS * pace))
    tiles = []
    count = block // ROWS
    for step in range(count):
        total = waves[0]
        for wave in waves[1:]:
            total = total + wave
        tiles.append(total)
        if step < count - 1:
            waves = [wave * fall for wave, fall in zip(waves, falls)]
    if not forward:
        tiles = tiles[::-1]
    return jnp.concatenate(tiles, axis=0)


def mode_state(rate, data, forward, out_ref, lanes):
    block = data.shape[0]
    sub = sublane((ROWS, rate.shape[1]))
    age = (ROWS - 1 - sub) if forward else sub
    tiles = [data[t : t + ROWS] for t in range(0, block, ROWS)]
    if not forward:
        tiles = tiles[::-1]
    for mode in range(rate.shape[0]):
        pace = spread(rate[mode : mode + 1])
        fall = jnp.exp(-ROWS * pace)
        total = tiles[0]
        for tile in tiles[1:]:
            total = total * fall + tile
        out_ref[mode : mode + 1, lanes] = jnp.sum(total * jnp.exp(-pace * age), axis=0, keepdims=True)


def lane_blocks(width):
    return [slice(at, at + LANES) for at in range(0, width, LANES)]


def wide(ref, lanes=slice(None)):
    return ref[:, lanes].astype(jnp.float32)


def front_kernel(ks, vs, ql, ct, rate, si_out, state_out):
    si_out[...] = (wide(ks) * wide(vs)).astype(jnp.bfloat16)
    for lanes in lane_blocks(ks.shape[1]):
        back = wide(ct, lanes) * wide(ql, lanes)
        mode_state(rate[:, lanes], back, False, state_out, lanes)


def filters_kernel(ql, ct, taps, rate, res, own_three, back, local_out, long_spec, short_spec, hold):
    block = ql.shape[0]
    for lanes in lane_blocks(ql.shape[1]):
        hold[:, lanes] = mode_sum(rate[:, lanes], res[:, lanes], 0.0, True, block)
    scale = 1.0 / block
    filt = dft_full(own_three[...], hold[...]) * scale
    long_spec[...] = filt
    short_spec[...] = dft_full(own_three[...], taps[...]) * scale
    upstream = dft_full(own_three[...], wide(ct) * wide(ql))
    local_out[...] = dft_back(back[...], *times_conj(upstream, filt))


def long_grad_kernel(local, state, rate, res, kl, qs, grad_out, back_out):
    block = local.shape[0]
    for lanes in lane_blocks(local.shape[1]):
        far = mode_sum(rate[:, lanes], res[:, lanes] * state[:, lanes], 1.0, False, block)
        grad = (local[:, lanes] + far).astype(jnp.bfloat16)
        grad_out[:, lanes] = grad
        hidden_grad = grad.astype(jnp.float32) * wide(kl, lanes)
        back_out[:, lanes] = (hidden_grad * wide(qs, lanes)).astype(jnp.bfloat16)


def short_kernel(si, halo, spec, qs, kl, rate, own_two, nxt_two, back, in_spec, mix_out, hidden_out, long_in, state_out):
    signal = dft_exact(own_two[...], si[...]) - dft_exact(nxt_two[...], halo[...])
    in_spec[...] = signal
    mix = dft_back(back[...], *times(signal, spec[...]))
    mix_out[...] = mix
    hidden = (wide(qs) * mix).astype(jnp.bfloat16)
    hidden_out[...] = hidden
    values = (wide(kl) * hidden.astype(jnp.float32)).astype(jnp.bfloat16)
    long_in[...] = values
    for lanes in lane_blocks(si.shape[1]):
        mode_state(rate[:, lanes], values[:, lanes].astype(jnp.float32), True, state_out, lanes)


def taps_kernel(sb, in_spec, grad, kl, hidden, mix, own_two, back, sb_spec, part_out, key_grad, query_grad):
    spec = dft_exact(own_two[...], sb[...])
    sb_spec[...] = spec
    scale = 1.0 / sb.shape[0]
    part = dft_back(back[...], *times_conj(spec, in_spec[...])) * scale
    part_out[...] = part.astype(jnp.bfloat16)
    slope = wide(grad)
    key_grad[...] = (slope * wide(hidden)).astype(jnp.bfloat16)
    query_grad[...] = (slope * wide(kl) * mix[...]).astype(jnp.bfloat16)


def input_grad_kernel(sb_next, sb_spec, spec, ks, vs, nxt_two, back, key_out, value_out):
    total = sb_spec[...] + dft_exact(nxt_two[...], sb_next[...])
    grad = dft_back(back[...], *times_conj(total, spec[...]))
    key_out[...] = (grad * wide(vs)).astype(jnp.bfloat16)
    value_out[...] = (grad * wide(ks)).astype(jnp.bfloat16)


def long_kernel(values, long_spec, state, rate, res, ql, ct, own_two, back, core_out, gate_out, hold):
    block = values.shape[0]
    for lanes in lane_blocks(values.shape[1]):
        weight = res[:, lanes] * state[:, lanes]
        hold[:, lanes] = mode_sum(rate[:, lanes], weight, 1.0, True, block)
    spec = dft_exact(own_two[...], values[...])
    mix = dft_back(back[...], *times(spec, long_spec[...])) + hold[...]
    core_out[...] = (wide(ql) * mix).astype(jnp.bfloat16)
    gate_out[...] = (wide(ct) * mix).astype(jnp.bfloat16)


def run(body, name, blocked, fixed, outs, width, flops, scratch=()):
    channels = blocked[0].shape[1]
    in_specs = [pl.BlockSpec((a.shape[0], width), lambda i: (0, i)) for a in blocked]
    in_specs += [pl.BlockSpec(a.shape, lambda i: (0, 0)) for a in fixed]
    out_specs = [pl.BlockSpec((rows, width), lambda i: (0, i)) for rows, _ in outs]
    out_shape = [jax.ShapeDtypeStruct((rows, channels), dtype) for rows, dtype in outs]
    moved = sum(a.size * a.dtype.itemsize for a in [*blocked, *fixed])
    moved += sum(s.size * s.dtype.itemsize for s in out_shape)
    return pl.pallas_call(
        body,
        grid=(channels // width,),
        in_specs=in_specs,
        out_specs=out_specs,
        out_shape=out_shape,
        scratch_shapes=[pltpu.VMEM((rows, width), dtype) for rows, dtype in scratch],
        compiler_params=pltpu.CompilerParams(vmem_limit_bytes=VMEM_BYTES),
        cost_estimate=pl.CostEstimate(flops=flops, bytes_accessed=moved, transcendentals=0),
        name=name,
    )(*blocked, *fixed)


def shifted(value, distance):
    size = lax.axis_size("ctx")
    pairs = [(i, i + distance) for i in range(size) if 0 <= i + distance < size]
    return lax.ppermute(value, "ctx", pairs)


def swapped(value, mask):
    size = lax.axis_size("ctx")
    return lax.ppermute(value, "ctx", [(i, i ^ mask) for i in range(size)])


def masks():
    size = lax.axis_size("ctx")
    return [1 << bit for bit in range(size.bit_length() - 1)]


def states_from(state, rate, block, later):
    me = lax.axis_index("ctx")
    got = jnp.zeros_like(state)
    total = state
    for mask in masks():
        other = swapped(total, mask)
        place = me % mask
        mine_low = (me // mask) % 2 == 0
        fade = jnp.exp(-(block * mask) * rate)
        if later:
            takes = mine_low
            steps = mask - 1 - place
        else:
            takes = jnp.logical_not(mine_low)
            steps = place
        near = jnp.exp(-(block * steps).astype(jnp.float32) * rate)
        got = got + jnp.where(takes, near, 0.0) * other
        total = jnp.where(takes, total + fade * other, other + fade * total)
    return got


def taps_total(part):
    me = lax.axis_index("ctx")
    steps = masks()
    channels = part.shape[1]
    half = channels // 2
    first = me % 2 == 0
    keep = jnp.where(first, part[:, :half], part[:, half:])
    send = jnp.where(first, part[:, half:], part[:, :half])
    mine = (keep.astype(jnp.float32) + swapped(send, 1).astype(jnp.float32)).astype(jnp.bfloat16)
    pieces = [mine[:, : half // 2], mine[:, half // 2 :]]
    rest = steps[1:]
    orders = [rest, rest[1:] + rest[:1]]
    for at in range(len(rest)):
        others = [swapped(piece, order[at]) for piece, order in zip(pieces, orders)]
        pieces = [
            (piece.astype(jnp.float32) + other.astype(jnp.float32)).astype(jnp.bfloat16)
            for piece, other in zip(pieces, others)
        ]
    mine = jnp.concatenate(pieces, axis=1)
    other = swapped(mine, 1)
    low = jnp.where(first, mine, other)
    high = jnp.where(first, other, mine)
    return jnp.concatenate([low, high], axis=1)


def local(
    query_short,
    key_short,
    value_short,
    short_taps,
    query_long,
    key_long,
    long_residue,
    long_rate,
    cotangent,
):
    block, channels = query_short.shape
    modes = long_rate.shape[0]
    sequence = block * lax.axis_size("ctx")
    half, full = jnp.bfloat16, jnp.float32
    own_two, own_three, nxt_two, back = [jnp.asarray(t) for t in tables(block)]
    width = 512
    unit = 2 * block * block * channels * 2

    short_in, back_state = run(
        front_kernel,
        "front",
        [key_short, value_short, query_long, cotangent, long_rate],
        [],
        [(block, half), (modes, full)],
        width,
        4 * modes * block * channels,
    )
    halo = shifted(short_in, 1)
    back_far = states_from(back_state, long_rate, block, True)
    grad_local, long_spec, short_spec = run(
        filters_kernel,
        "filters",
        [query_long, cotangent, short_taps, long_rate, long_residue],
        [own_three, back],
        [(block, full), (2 * block, full), (2 * block, full)],
        width,
        12 * unit,
        [(block, full)],
    )
    long_grad, short_back = run(
        long_grad_kernel,
        "long_grad",
        [grad_local, back_far, long_rate, long_residue, key_long, query_short],
        [],
        [(block, half), (block, half)],
        width,
        4 * modes * block * channels,
    )
    in_spec, short_mix, hidden, long_in, fore_state = run(
        short_kernel,
        "short",
        [short_in, halo, short_spec, query_short, key_long, long_rate],
        [own_two, nxt_two, back],
        [(2 * block, full), (block, full), (block, half), (block, half), (modes, full)],
        width,
        7 * unit,
    )
    sb_spec, part, key_long_grad, query_short_grad = run(
        taps_kernel,
        "taps",
        [short_back, in_spec, long_grad, key_long, hidden, short_mix],
        [own_two, back],
        [(2 * block, full), (block, half), (block, half), (block, half)],
        width,
        5 * unit,
    )
    sb_next = shifted(short_back, -1)
    taps_sum = taps_total(part)
    taps_grad = taps_sum.astype(full) * (sequence ** (-0.5))
    fore_far = states_from(fore_state, long_rate, block, False)
    core_output, query_long_grad = run(
        long_kernel,
        "long",
        [long_in, long_spec, fore_far, long_rate, long_residue, query_long, cotangent],
        [own_two, back],
        [(block, half), (block, half)],
        width,
        5 * unit,
        [(block, full)],
    )
    key_short_grad, value_short_grad = run(
        input_grad_kernel,
        "input_grad",
        [sb_next, sb_spec, short_spec, key_short, value_short],
        [nxt_two, back],
        [(block, half), (block, half)],
        width,
        5 * unit,
    )
    return (
        core_output,
        query_short_grad,
        key_short_grad,
        value_short_grad,
        query_long_grad,
        key_long_grad,
        taps_grad,
    )


def solution(mesh):
    tokens, shared = P("ctx", "ch"), P(None, "ch")
    return jax.shard_map(
        local,
        mesh=mesh,
        in_specs=(tokens, tokens, tokens, shared, tokens, tokens, shared, shared, tokens),
        out_specs=(tokens,) * 6 + (shared,),
        check_vma=False,
    )
```

profile of v0, /device:TPU:27, one launch (start us, length us, event | category | flops | bytes accessed | tf_op | source)
XLA Modules:
  0.0 92.2 jit_solution(7096672144922301713)
XLA Ops:
  2.6 1.0 %copy-done.7 = bf16[128,2048]{1,0:T(8,128)(2,1)S(1)} copy-done((bf16[128,2048]{1,0:T(8,128)(2,1)S(1)}, bf16[128,2048]{1,0:T(8,128)(2,1)}, u32[]{:S(2)}) %copy-start.7) | copy-done | bytes 524312
  5.7 2.7 %front.1 = (bf16[128,2048]{1,0:T(8,128)(2,1)}, f32[16,2048]{1,0:T(8,128)}) custom-call(bf16[128,2048]{1,0:T(8,128)(2,1)S(1)} %copy-done.10, bf16[128,2048]{1,0:T(8,128)(2,1)S(1)} %copy-done.12, bf16[128,2048]{1,0:T(8,128)(2,1)S(1)} %copy-done.5, bf16[128,2048]{1,0:T(8,128)(2,1)S(1)} %copy-done.7, f32[16,2048]{1,0:T(8,128)S(1)} %copy-done.1), custom_call_target="tpu_custom_call" | custom-call | flops 16777216 | bytes 2883584 | tf_op jit(solution)/shard_map/front/pallas_call | solution.py:214
  8.5 3.7 %collective-permute-start = (bf16[128,2048]{1,0:T(8,128)(2,1)}, bf16[128,2048]{1,0:T(8,128)(2,1)}, u32[]{:S(2)}, u32[]{:S(2)}) collective-permute-start(bf16[128,2048]{1,0:T(8,128)(2,1)} %get-tuple-element.27.si), channel_id=1, source_target_pairs={{0,4},{4,8},{8,12},{12,16},{16,20},{20,24},{24,28},{1,5},{5,9},{9,... | collective-permute-start | bytes 1572872 | tf_op jit(solution)/shard_map/ppermute | solution.py:230
  12.3 1.3 %copy-done.30 = f32[128,2048]{1,0:T(8,128)S(1)} copy-done((f32[128,2048]{1,0:T(8,128)S(1)}, f32[128,2048]{1,0:T(8,128)}, u32[]{:S(2)}) %copy-start.30) | copy-done | bytes 1048600
  13.6 6.2 %filters.1 = (f32[128,2048]{1,0:T(8,128)S(1)}, f32[256,2048]{1,0:T(8,128)S(1)}, f32[256,2048]{1,0:T(8,128)}) custom-call(bf16[128,2048]{1,0:T(8,128)(2,1)S(1)} %copy-done.6, bf16[128,2048]{1,0:T(8,128)(2,1)S(1)} %copy-done.8, f32[128,2048]{1,0:T(8,128)S(1)} %copy-done.30, f32[16,2048]{1,0:T(8,128)S(1)} %copy-done.2, f32[16,2048]{1,0:T(8,128)S(1)} %copy-done.22, ...), custom_call_target="tpu_custom_call" | custom-call | flops 1610612736 | bytes 7929856 | tf_op jit(solution)/shard_map/filters/pallas_call | solution.py:214
  19.8 1.4 %copy-done.15 = f32[256,2048]{1,0:T(8,128)} copy-done((f32[256,2048]{1,0:T(8,128)}, f32[256,2048]{1,0:T(8,128)S(1)}, u32[]{:S(2)}) %copy-start.15) | copy-done | bytes 2097176
  23.4 5.9 %short.1 = (f32[256,2048]{1,0:T(8,128)}, f32[128,2048]{1,0:T(8,128)S(1)}, bf16[128,2048]{1,0:T(8,128)(2,1)S(1)}, bf16[128,2048]{1,0:T(8,128)(2,1)S(1)}, f32[16,2048]{1,0:T(8,128)S(1)}) custom-call(bf16[128,2048]{1,0:T(8,128)(2,1)} %get-tuple-element.27.si, bf16[128,2048]{1,0:T(8,128)(2,1)} %collective-permute-done.halo, f32[256,2048]{1,0:T(8,128)} %get-tuple-element.28.spec, ...), custom_call_target="tpu_custom_call" | custom-call | flops 939524096 | bytes 9043968 | tf_op jit(solution)/shard_map/short/pallas_call | solution.py:214
  32.5 1.1 %collective-permute-done.1 = f32[16,2048]{1,0:T(8,128)} collective-permute-done((f32[16,2048]{1,0:T(8,128)S(1)}, f32[16,2048]{1,0:T(8,128)}, u32[]{:S(2)}, u32[]{:S(2)}) %collective-permute-start.1) | collective-permute-done | bytes 131104 | tf_op jit(solution)/shard_map/ppermute | solution.py:235
  33.6 1.7 %add_select_fusion = (f32[16,2048]{1,0:T(8,128)}, f32[16,2048]{1,0:T(8,128)}) fusion(f32[16,2048]{1,0:T(8,128)S(1)} %collective-permute-done.5, f32[16,2048]{1,0:T(8,128)S(1)} %add_select_fusion.1, f32[16,2048]{1,0:T(8,128)S(1)} %copy-done.2, pred[]{:T(512)S(6)} %eq.28, f32[16,2048]{1,0:T(8,128)} %collective-permute-done.1, ...), kind=kLoop, calls=%fused_computation.11 | loop fusion | flops 393216 | bytes 917506 | tf_op jit(solution)/shard_map/jit(_where)/select_n | solution.py:260
  35.3 1.2 %collective-permute-start.6 = (f32[16,2048]{1,0:T(8,128)}, f32[16,2048]{1,0:T(8,128)S(1)}, u32[]{:S(2)}, u32[]{:S(2)}) collective-permute-start(f32[16,2048]{1,0:T(8,128)} %get-tuple-element.55), channel_id=1, source_target_pairs={{0,16},{4,20},{8,24},{12,28},{16,0},{20,4},{24,8},{28,12},{1,17},{... | collective-permute-start | bytes 393224 | tf_op jit(solution)/shard_map/ppermute | solution.py:235
  36.5 3.7 %collective-permute-done.6 = f32[16,2048]{1,0:T(8,128)S(1)} collective-permute-done((f32[16,2048]{1,0:T(8,128)}, f32[16,2048]{1,0:T(8,128)S(1)}, u32[]{:S(2)}, u32[]{:S(2)}) %collective-permute-start.6) | collective-permute-done | bytes 131104 | tf_op jit(solution)/shard_map/ppermute | solution.py:235
  41.1 1.8 %multiply_add_fusion = (f32[16,2048]{1,0:T(8,128)S(1)}, f32[16,2048]{1,0:T(8,128)}) fusion(f32[16,2048]{1,0:T(8,128)} %copy-done.33, f32[16,2048]{1,0:T(8,128)S(1)} %copy-done.2, f32[16,2048]{1,0:T(8,128)S(1)} %collective-permute-done.5, f32[16,2048]{1,0:T(8,128)} %collective-permute-done.4, f32[]{:T(128)S(6)} %neg.17, f32[]{:T(128)S(6)} %neg.16, ...), kind=kLoop, calls=%fused_computation.10 | loop fusion | flops 557056 | bytes 1048588 | tf_op jit(solution)/shard_map/add | solution.py:259
  43.0 2.4 %long_grad.1 = (bf16[128,2048]{1,0:T(8,128)(2,1)S(1)}, bf16[128,2048]{1,0:T(8,128)(2,1)S(1)}) custom-call(f32[128,2048]{1,0:T(8,128)S(1)} %get-tuple-element.33.local, f32[16,2048]{1,0:T(8,128)S(1)} %get-tuple-element.53.state, f32[16,2048]{1,0:T(8,128)S(1)} %copy-done.2, f32[16,2048]{1,0:T(8,128)S(1)} %copy-done.23, bf16[128,2048]{1,0:T(8,128)(2,1)S(1)} %copy-done.3, ...), custom_call_target="tpu_custom_call" | custom-call | flops 16777216 | bytes 3538944 | tf_op jit(solution)/shard_map/long_grad/pallas_call | solution.py:214
  45.4 5.2 %taps.3 = (f32[256,2048]{1,0:T(8,128)S(1)}, bf16[128,2048]{1,0:T(8,128)(2,1)S(1)}, bf16[128,2048]{1,0:T(8,128)(2,1)}, bf16[128,2048]{1,0:T(8,128)(2,1)}) custom-call(bf16[128,2048]{1,0:T(8,128)(2,1)S(1)} %get-tuple-element.35.sb, f32[256,2048]{1,0:T(8,128)} %get-tuple-element.36.in_spec, bf16[128,2048]{1,0:T(8,128)(2,1)S(1)} %get-tuple-element.37.grad, ...), custom_call_target="tpu_custom_call" | custom-call | flops 671088640 | bytes 9175040 | tf_op jit(solution)/shard_map/taps/pallas_call | solution.py:214
  50.6 1.6 %collective-permute-start.8 = (bf16[128,1024]{1,0:T(8,128)(2,1)S(1)}, bf16[128,1024]{1,0:T(8,128)(2,1)S(1)}, u32[]{:S(2)}, u32[]{:S(2)}) collective-permute-start(bf16[128,1024]{1,0:T(8,128)(2,1)S(1)} %broadcast_select_fusion.2), channel_id=1, source_target_pairs={{0,4},{4,0},{8,12},{12,8},{16,20},{20,16},{24,28},{28,24},{1,5},{5... | collective-permute-start | bytes 786440 | tf_op jit(solution)/shard_map/ppermute | solution.py:235
  52.2 1.2 %collective-permute-done.8 = bf16[128,1024]{1,0:T(8,128)(2,1)S(1)} collective-permute-done((bf16[128,1024]{1,0:T(8,128)(2,1)S(1)}, bf16[128,1024]{1,0:T(8,128)(2,1)S(1)}, u32[]{:S(2)}, u32[]{:S(2)}) %collective-permute-start.8) | collective-permute-done | bytes 262176 | tf_op jit(solution)/shard_map/ppermute | solution.py:235
  55.0 3.3 %collective-permute-done.9 = bf16[128,512]{1,0:T(8,128)(2,1)S(1)} collective-permute-done((bf16[128,512]{1,0:T(8,128)(2,1)S(1)}, bf16[128,512]{1,0:T(8,128)(2,1)S(1)}, u32[]{:S(2)}, u32[]{:S(2)}) %collective-permute-start.9) | collective-permute-done | bytes 131104 | tf_op jit(solution)/shard_map/ppermute | solution.py:235
  60.2 3.8 %collective-permute-start.7 = (bf16[128,2048]{1,0:T(8,128)(2,1)}, bf16[128,2048]{1,0:T(8,128)(2,1)S(1)}, u32[]{:S(2)}, u32[]{:S(2)}) collective-permute-start(bf16[128,2048]{1,0:T(8,128)(2,1)} %copy-done.29), channel_id=1, source_target_pairs={{4,0},{8,4},{12,8},{16,12},{20,16},{24,20},{28,24},{5,1},{9,5},{13... | collective-permute-start | bytes 1572872 | tf_op jit(solution)/shard_map/ppermute | solution.py:230
  66.6 11.4 %collective-permute-done.10 = bf16[128,512]{1,0:T(8,128)(2,1)S(1)} collective-permute-done((bf16[128,512]{1,0:T(8,128)(2,1)}, bf16[128,512]{1,0:T(8,128)(2,1)S(1)}, u32[]{:S(2)}, u32[]{:S(2)}) %collective-permute-start.10) | collective-permute-done | bytes 131104 | tf_op jit(solution)/shard_map/ppermute | solution.py:235
  79.5 1.0 %multiply_add_fusion.1.state = f32[16,2048]{1,0:T(8,128)S(1)} fusion(f32[16,2048]{1,0:T(8,128)S(1)} %collective-permute-done.3, f32[16,2048]{1,0:T(8,128)S(1)} %copy-done.2, f32[16,2048]{1,0:T(8,128)} %copy-done.32, f32[16,2048]{1,0:T(8,128)} %collective-permute-done.1, f32[]{:T(128)S(6)} %neg.15, f32[]{:T(128)S(6)} %neg.14, pred[]{:T(512)S(6)} %not.11, ...), kind=kLoop, calls=%fused_computation.13 | loop fusion | flops 360448 | bytes 655371 | tf_op jit(solution)/shard_map/add | solution.py:259
  80.6 1.6 %copy-done.16 = f32[256,2048]{1,0:T(8,128)S(1)} copy-done((f32[256,2048]{1,0:T(8,128)S(1)}, f32[256,2048]{1,0:T(8,128)}, u32[]{:S(2)}) %copy-start.16) | copy-done | bytes 2097176
  83.1 4.5 %long.1 = (bf16[128,2048]{1,0:T(8,128)(2,1)}, bf16[128,2048]{1,0:T(8,128)(2,1)}) custom-call(bf16[128,2048]{1,0:T(8,128)(2,1)S(1)} %copy-done.21, f32[256,2048]{1,0:T(8,128)S(1)} %copy-done.16, f32[16,2048]{1,0:T(8,128)S(1)} %multiply_add_fusion.1.state, f32[16,2048]{1,0:T(8,128)S(1)} %copy-done.2, f32[16,2048]{1,0:T(8,128)S(1)} %copy-done.24, ...), custom_call_target="tpu_custom_call" | custom-call | flops 671088640 | bytes 5373952 | tf_op jit(solution)/shard_map/long/pallas_call | solution.py:214
  87.6 3.4 %input_grad.1 = (bf16[128,2048]{1,0:T(8,128)(2,1)}, bf16[128,2048]{1,0:T(8,128)(2,1)}) custom-call(bf16[128,2048]{1,0:T(8,128)(2,1)S(1)} %collective-permute-done.7.sb_next, f32[256,2048]{1,0:T(8,128)S(1)} %get-tuple-element.41.sb_spec, f32[256,2048]{1,0:T(8,128)S(1)} %copy-done, bf16[128,2048]{1,0:T(8,128)(2,1)S(1)} %copy-done.11, ...), custom_call_target="tpu_custom_call" | custom-call | flops 671088640 | bytes 7077888 | tf_op jit(solution)/shard_map/input_grad/pallas_call | solution.py:214
  91.2 1.1 %convert_multiply_fusion = f32[128,2048]{1,0:T(8,128)} fusion(bf16[128,1024]{1,0:T(8,128)(2,1)S(1)} %get-tuple-element.48, bf16[128,1024]{1,0:T(8,128)(2,1)S(1)} %get-tuple-element.47), kind=kLoop, calls=%fused_computation | loop fusion | flops 1310720 | bytes 1572864 | tf_op jit(solution)/shard_map/mul | solution.py:358
  (92 shorter events, 19.2 us)
Async XLA Ops:
  5.7 6.6 %copy-start.22 = (f32[16,2048]{1,0:T(8,128)S(1)}, f32[16,2048]{1,0:T(8,128)}, u32[]{:S(2)}) copy-start(f32[16,2048]{1,0:T(8,128)} %res.5) | copy-start | bytes 393220
  8.5 14.0 %collective-permute-start = (bf16[128,2048]{1,0:T(8,128)(2,1)}, bf16[128,2048]{1,0:T(8,128)(2,1)}, u32[]{:S(2)}, u32[]{:S(2)}) collective-permute-start(bf16[128,2048]{1,0:T(8,128)(2,1)} %get-tuple-element.27.si), channel_id=1, source_target_pairs={{0,4},{4,8},{8,12},{12,16},{16,20},{20,24},{24,28},{1,5},{5,9},{9,... | collective-permute-start | bytes 1572872 | tf_op jit(solution)/shard_map/ppermute | solution.py:230
  12.1 10.3 %copy-start.3 = (bf16[128,2048]{1,0:T(8,128)(2,1)S(1)}, bf16[128,2048]{1,0:T(8,128)(2,1)}, u32[]{:S(2)}) copy-start(bf16[128,2048]{1,0:T(8,128)(2,1)} %kl.5) | copy-start | bytes 1572868
  12.2 10.3 %copy-start.4 = (bf16[128,2048]{1,0:T(8,128)(2,1)S(1)}, bf16[128,2048]{1,0:T(8,128)(2,1)}, u32[]{:S(2)}) copy-start(bf16[128,2048]{1,0:T(8,128)(2,1)} %qs.3) | copy-start | bytes 1572868
  12.2 10.3 %copy-start.17 = (bf16[256,256]{1,0:T(8,128)(2,1)S(1)}, bf16[256,256]{1,0:T(8,128)(2,1)}, u32[]{:S(2)}) copy-start(bf16[256,256]{1,0:T(8,128)(2,1)} %constant.122.clone.own_two) | copy-start | bytes 393220
  12.2 9.0 %collective-permute-start.4 = (f32[16,2048]{1,0:T(8,128)}, f32[16,2048]{1,0:T(8,128)}, u32[]{:S(2)}, u32[]{:S(2)}) collective-permute-start(f32[16,2048]{1,0:T(8,128)} %get-tuple-element.34), channel_id=1, source_target_pairs={{0,4},{4,0},{8,12},{12,8},{16,20},{20,16},{24,28},{28,24},{1,5},{5... | collective-permute-start | bytes 393224 | tf_op jit(solution)/shard_map/ppermute | solution.py:235
  22.2 10.3 %collective-permute-start.5 = (f32[16,2048]{1,0:T(8,128)S(1)}, f32[16,2048]{1,0:T(8,128)S(1)}, u32[]{:S(2)}, u32[]{:S(2)}) collective-permute-start(f32[16,2048]{1,0:T(8,128)S(1)} %add_select_fusion.1), channel_id=1, source_target_pairs={{0,8},{4,12},{8,0},{12,4},{16,24},{20,28},{24,16},{28,20},{1,9},{5... | collective-permute-start | bytes 393224 | tf_op jit(solution)/shard_map/ppermute | solution.py:235
  31.8 11.2 %copy-start.23 = (f32[16,2048]{1,0:T(8,128)S(1)}, f32[16,2048]{1,0:T(8,128)}, u32[]{:S(2)}) copy-start(f32[16,2048]{1,0:T(8,128)} %res.5) | copy-start | bytes 393220
  31.8 1.8 %collective-permute-start.1 = (f32[16,2048]{1,0:T(8,128)S(1)}, f32[16,2048]{1,0:T(8,128)}, u32[]{:S(2)}, u32[]{:S(2)}) collective-permute-start(f32[16,2048]{1,0:T(8,128)S(1)} %get-tuple-element.31), channel_id=1, source_target_pairs={{0,4},{4,0},{8,12},{12,8},{16,20},{20,16},{24,28},{28,24},{1,5},{5... | collective-permute-start | bytes 393224 | tf_op jit(solution)/shard_map/ppermute | solution.py:235
  35.3 4.9 %collective-permute-start.6 = (f32[16,2048]{1,0:T(8,128)}, f32[16,2048]{1,0:T(8,128)S(1)}, u32[]{:S(2)}, u32[]{:S(2)}) collective-permute-start(f32[16,2048]{1,0:T(8,128)} %get-tuple-element.55), channel_id=1, source_target_pairs={{0,16},{4,20},{8,24},{12,28},{16,0},{20,4},{24,8},{28,12},{1,17},{... | collective-permute-start | bytes 393224 | tf_op jit(solution)/shard_map/ppermute | solution.py:235
  36.5 4.6 %collective-permute-start.2 = (f32[16,2048]{1,0:T(8,128)}, f32[16,2048]{1,0:T(8,128)S(1)}, u32[]{:S(2)}, u32[]{:S(2)}) collective-permute-start(f32[16,2048]{1,0:T(8,128)} %get-tuple-element.56), channel_id=1, source_target_pairs={{0,8},{4,12},{8,0},{12,4},{16,24},{20,28},{24,16},{28,20},{1,9},{5... | collective-permute-start | bytes 393224 | tf_op jit(solution)/shard_map/ppermute | solution.py:235
  36.5 8.9 %copy-start.19 = (f32[128,2048]{1,0:T(8,128)S(1)}, f32[128,2048]{1,0:T(8,128)}, u32[]{:S(2)}) copy-start(f32[128,2048]{1,0:T(8,128)} %copy-done.18) | copy-start | bytes 3145732
  36.5 8.9 %copy-start.28 = (bf16[128,2048]{1,0:T(8,128)(2,1)S(1)}, bf16[128,2048]{1,0:T(8,128)(2,1)}, u32[]{:S(2)}) copy-start(bf16[128,2048]{1,0:T(8,128)(2,1)} %copy-done.27) | copy-start | bytes 1572868
  45.4 8.1 %copy-start.29 = (bf16[128,2048]{1,0:T(8,128)(2,1)}, bf16[128,2048]{1,0:T(8,128)(2,1)S(1)}, u32[]{:S(2)}) copy-start(bf16[128,2048]{1,0:T(8,128)(2,1)S(1)} %get-tuple-element.35.sb) | copy-start | bytes 1572868
  50.6 29.9 %copy-start.9 = (bf16[128,2048]{1,0:T(8,128)(2,1)S(1)}, bf16[128,2048]{1,0:T(8,128)(2,1)}, u32[]{:S(2)}) copy-start(bf16[128,2048]{1,0:T(8,128)(2,1)} %ct.5) | copy-start | bytes 1572868
  50.6 2.7 %collective-permute-start.8 = (bf16[128,1024]{1,0:T(8,128)(2,1)S(1)}, bf16[128,1024]{1,0:T(8,128)(2,1)S(1)}, u32[]{:S(2)}, u32[]{:S(2)}) collective-permute-start(bf16[128,1024]{1,0:T(8,128)(2,1)S(1)} %broadcast_select_fusion.2), channel_id=1, source_target_pairs={{0,4},{4,0},{8,12},{12,8},{16,20},{20,16},{24,28},{28,24},{1,5},{5... | collective-permute-start | bytes 786440 | tf_op jit(solution)/shard_map/ppermute | solution.py:235
  53.5 4.8 %collective-permute-start.9 = (bf16[128,512]{1,0:T(8,128)(2,1)S(1)}, bf16[128,512]{1,0:T(8,128)(2,1)S(1)}, u32[]{:S(2)}, u32[]{:S(2)}) collective-permute-start(bf16[128,512]{1,0:T(8,128)(2,1)S(1)} %get-tuple-element.51), channel_id=1, source_target_pairs={{0,8},{4,12},{8,0},{12,4},{16,24},{20,28},{24,16},{28,20},{1,9},{5... | collective-permute-start | bytes 393224 | tf_op jit(solution)/shard_map/ppermute | solution.py:235
  54.2 4.4 %collective-permute-start.11 = (bf16[128,512]{1,0:T(8,128)(2,1)S(1)}, bf16[128,512]{1,0:T(8,128)(2,1)S(1)}, u32[]{:S(2)}, u32[]{:S(2)}) collective-permute-start(bf16[128,512]{1,0:T(8,128)(2,1)S(1)} %get-tuple-element.52), channel_id=1, source_target_pairs={{0,16},{4,20},{8,24},{12,28},{16,0},{20,4},{24,8},{28,12},{1,17},{... | collective-permute-start | bytes 393224 | tf_op jit(solution)/shard_map/ppermute | solution.py:235
  59.4 6.2 %collective-permute-start.12 = (bf16[128,512]{1,0:T(8,128)(2,1)}, bf16[128,512]{1,0:T(8,128)(2,1)}, u32[]{:S(2)}, u32[]{:S(2)}) collective-permute-start(bf16[128,512]{1,0:T(8,128)(2,1)} %get-tuple-element.50), channel_id=1, source_target_pairs={{0,8},{4,12},{8,0},{12,4},{16,24},{20,28},{24,16},{28,20},{1,9},{5... | collective-permute-start | bytes 393224 | tf_op jit(solution)/shard_map/ppermute | solution.py:235
  60.2 20.3 %copy-start.21 = (bf16[128,2048]{1,0:T(8,128)(2,1)S(1)}, bf16[128,2048]{1,0:T(8,128)(2,1)}, u32[]{:S(2)}) copy-start(bf16[128,2048]{1,0:T(8,128)(2,1)} %copy-done.20) | copy-start | bytes 1572868
  60.2 27.4 %collective-permute-start.7 = (bf16[128,2048]{1,0:T(8,128)(2,1)}, bf16[128,2048]{1,0:T(8,128)(2,1)S(1)}, u32[]{:S(2)}, u32[]{:S(2)}) collective-permute-start(bf16[128,2048]{1,0:T(8,128)(2,1)} %copy-done.29), channel_id=1, source_target_pairs={{4,0},{8,4},{12,8},{16,12},{20,16},{24,20},{28,24},{5,1},{9,5},{13... | collective-permute-start | bytes 1572872 | tf_op jit(solution)/shard_map/ppermute | solution.py:230
  64.1 15.4 %collective-permute-start.3 = (f32[16,2048]{1,0:T(8,128)}, f32[16,2048]{1,0:T(8,128)S(1)}, u32[]{:S(2)}, u32[]{:S(2)}) collective-permute-start(f32[16,2048]{1,0:T(8,128)} %get-tuple-element.54), channel_id=1, source_target_pairs={{0,16},{4,20},{8,24},{12,28},{16,0},{20,4},{24,8},{28,12},{1,17},{... | collective-permute-start | bytes 393224 | tf_op jit(solution)/shard_map/ppermute | solution.py:235
  64.8 13.2 %collective-permute-start.10 = (bf16[128,512]{1,0:T(8,128)(2,1)}, bf16[128,512]{1,0:T(8,128)(2,1)S(1)}, u32[]{:S(2)}, u32[]{:S(2)}) collective-permute-start(bf16[128,512]{1,0:T(8,128)(2,1)} %get-tuple-element.49), channel_id=1, source_target_pairs={{0,16},{4,20},{8,24},{12,28},{16,0},{20,4},{24,8},{28,12},{1,17},{... | collective-permute-start | bytes 393224 | tf_op jit(solution)/shard_map/ppermute | solution.py:235
  79.0 12.0 %collective-permute-start.13 = (bf16[128,1024]{1,0:T(8,128)(2,1)S(1)}, bf16[128,1024]{1,0:T(8,128)(2,1)S(1)}, u32[]{:S(2)}, u32[]{:S(2)}) collective-permute-start(bf16[128,1024]{1,0:T(8,128)(2,1)S(1)} %pad_maximum_fusion), channel_id=1, source_target_pairs={{0,4},{4,0},{8,12},{12,8},{16,20},{20,16},{24,28},{28,24},{1,5},{5... | collective-permute-start | bytes 786440 | tf_op jit(solution)/shard_map/ppermute | solution.py:235
  (24 other events, 69.6 us)
where the time goes:
time: 93 us; the launch traced here: 92.2 us
  Pallas kernels  30.2 us (32%)
  waiting for transfers between devices  21.3 us (23%)
  starting transfers between devices  15.7 us (17%)
  local copies, waits for them, and re-layouts  14.4 us (15%)
  other arithmetic  9.64 us (10%)
  between operations  0.96 us (1%)
    pallas_call x7, Pallas kernels, run(): pl.pallas_call(body, grid=(channels // width,), in_specs=in_specs, out_sp...  30.2 us
    ppermute x12, waiting for transfers between devices, swapped(): return lax.ppermute(value, 'ctx', [(i, i ^ mask) for i in range(size)])  21.2 us
    unnamed x68, local copies, waits for them, and re-layouts  14.4 us
    ppermute x12, starting transfers between devices, swapped(): return lax.ppermute(value, 'ctx', [(i, i ^ mask) for i in range(size)])  8.24 us
    ppermute x2, starting transfers between devices, shifted(): return lax.ppermute(value, 'ctx', pairs)  7.5 us
    add x2, other arithmetic, states_from(): got = got + jnp.where(takes, near, 0.0) * other  2.89 us
    convert_element_type x3, other arithmetic, taps_total(): (piece.astype(jnp.float32) + other.astype(jnp.float32)).astype(jnp.bfloat16)  2.7 us
    select_n x2, other arithmetic, states_from(): total = jnp.where(takes, total + fade * other, other + fade * total)  2.69 us
  transfers between devices with their start and end apart: 14, of which 7 were waited for; matrix products, arithmetic and copies ran while one was open for 4% of the time, Pallas kernels for 22%

commit v1 on v0

--- a/solution.py
+++ b/solution.py
@@ -8,7 +8,7 @@
 
 ROWS = 8
 LANES = 128
-VMEM_BYTES = 48 * 1024 * 1024
+VMEM_BYTES = 16 * 1024 * 1024
 
 
 def split_np(matrix):
@@ -132,21 +132,81 @@
     return ref[:, lanes].astype(jnp.float32)
 
 
-def front_kernel(ks, vs, ql, ct, rate, si_out, state_out):
-    si_out[...] = (wide(ks) * wide(vs)).astype(jnp.bfloat16)
-    for lanes in lane_blocks(ks.shape[1]):
-        back = wide(ct, lanes) * wide(ql, lanes)
-        mode_state(rate[:, lanes], back, False, state_out, lanes)
-
-
-def filters_kernel(ql, ct, taps, rate, res, own_three, back, local_out, long_spec, short_spec, hold):
+def in_vmem(value):
+    return pltpu.with_memory_space_constraint(value, pltpu.VMEM)
+
+
+def in_hbm(value):
+    return pltpu.with_memory_space_constraint(value, pltpu.HBM)
+
+
+def front(key_short, value_short, query_long, cotangent, rate, others, width):
+    block, channels = key_short.shape
+    half, full = jnp.bfloat16, jnp.float32
+    parts = range(0, channels, width)
+    brought = [rate, cotangent, query_long, key_short, value_short, *others]
+    pieces = [1] + [len(parts)] * 4 + [1] * len(others)
+    count = len(brought)
+
+    def body(*refs):
+        sources, results, sems = refs[:count], refs[count : 2 * count], refs[-1]
+        si, state = refs[2 * count : 2 * count + 2]
+        copies, at = [], 0
+        for source, result, many in zip(sources, results, pieces):
+            step = source.shape[1] // many
+            row = []
+            for i in range(many):
+                cut = pl.ds(i * step, step)
+                row.append(pltpu.make_async_copy(source.at[:, cut], result.at[:, cut], sems.at[at]))
+                at += 1
+            copies.append(row)
+        order = [copies[0][0]]
+        for i in range(len(parts)):
+            order += [copies[1][i], copies[2][i]]
+        for i in range(len(parts)):
+            order += [copies[3][i], copies[4][i]]
+        for row in copies[5:]:
+            order += row
+        for copy in order:
+            copy.start()
+        copies[0][0].wait()
+        pace, ct, ql, ks, vs = results[:5]
+        for i, start in enumerate(parts):
+            copies[1][i].wait()
+            copies[2][i].wait()
+            for lane in range(start, start + width, LANES):
+                lanes = slice(lane, lane + LANES)
+                back = wide(ct, lanes) * wide(ql, lanes)
+                mode_state(pace[:, lanes], back, False, state, lanes)
+        for i, start in enumerate(parts):
+            copies[3][i].wait()
+            copies[4][i].wait()
+            lanes = slice(start, start + width)
+            si[:, lanes] = (wide(ks, lanes) * wide(vs, lanes)).astype(half)
+        for row in copies[5:]:
+            row[0].wait()
+
+    out_shape = [pltpu.VMEM(a.shape, a.dtype) for a in brought]
+    out_shape += [pltpu.VMEM((block, channels), half), pltpu.VMEM(rate.shape, full)]
+    results = pl.pallas_call(
+        body,
+        in_specs=[pl.BlockSpec(memory_space=pltpu.HBM)] * count,
+        out_specs=[pl.BlockSpec(memory_space=pltpu.VMEM)] * (count + 2),
+        out_shape=out_shape,
+        scratch_shapes=[pltpu.SemaphoreType.DMA((sum(pieces),))],
+        compiler_params=pltpu.CompilerParams(vmem_limit_bytes=VMEM_BYTES),
+        cost_estimate=pl.CostEstimate(flops=0, bytes_accessed=8 * 1024 * 1024, transcendentals=0),
+        name="front",
+    )(*[in_hbm(a) for a in brought])
+    return results[:count], results[count], results[count + 1]
+
+
+def filters_kernel(ql, ct, rate, res, own_three, back, local_out, long_spec, hold):
     block = ql.shape[0]
     for lanes in lane_blocks(ql.shape[1]):
         hold[:, lanes] = mode_sum(rate[:, lanes], res[:, lanes], 0.0, True, block)
-    scale = 1.0 / block
-    filt = dft_full(own_three[...], hold[...]) * scale
+    filt = dft_full(own_three[...], hold[...]) * (1.0 / block)
     long_spec[...] = filt
-    short_spec[...] = dft_full(own_three[...], taps[...]) * scale
     upstream = dft_full(own_three[...], wide(ct) * wide(ql))
     local_out[...] = dft_back(back[...], *times_conj(upstream, filt))
 
@@ -161,28 +221,27 @@
         back_out[:, lanes] = (hidden_grad * wide(qs, lanes)).astype(jnp.bfloat16)
 
 
-def short_kernel(si, halo, spec, qs, kl, rate, own_two, nxt_two, back, in_spec, mix_out, hidden_out, long_in, state_out):
+def taps_kernel(sb, si, halo, own_two, nxt_two, back, sb_spec, in_spec, part_out):
     signal = dft_exact(own_two[...], si[...]) - dft_exact(nxt_two[...], halo[...])
     in_spec[...] = signal
-    mix = dft_back(back[...], *times(signal, spec[...]))
-    mix_out[...] = mix
-    hidden = (wide(qs) * mix).astype(jnp.bfloat16)
-    hidden_out[...] = hidden
-    values = (wide(kl) * hidden.astype(jnp.float32)).astype(jnp.bfloat16)
-    long_in[...] = values
-    for lanes in lane_blocks(si.shape[1]):
-        mode_state(rate[:, lanes], values[:, lanes].astype(jnp.float32), True, state_out, lanes)
-
-
-def taps_kernel(sb, in_spec, grad, kl, hidden, mix, own_two, back, sb_spec, part_out, key_grad, query_grad):
     spec = dft_exact(own_two[...], sb[...])
     sb_spec[...] = spec
-    scale = 1.0 / sb.shape[0]
-    part = dft_back(back[...], *times_conj(spec, in_spec[...])) * scale
+    part = dft_back(back[...], *times_conj(spec, signal)) * (1.0 / sb.shape[0])
     part_out[...] = part.astype(jnp.bfloat16)
+
+
+def short_kernel(in_spec, taps, qs, kl, rate, grad, own_three, back, spec_out, long_in, state_out, key_grad, query_grad):
+    spec = dft_full(own_three[...], taps[...]) * (1.0 / qs.shape[0])
+    spec_out[...] = spec
+    mix = dft_back(back[...], *times(in_spec[...], spec))
+    hidden = (wide(qs) * mix).astype(jnp.bfloat16).astype(jnp.float32)
+    values = (wide(kl) * hidden).astype(jnp.bfloat16)
+    long_in[...] = values
     slope = wide(grad)
-    key_grad[...] = (slope * wide(hidden)).astype(jnp.bfloat16)
-    query_grad[...] = (slope * wide(kl) * mix[...]).astype(jnp.bfloat16)
+    key_grad[...] = (slope * hidden).astype(jnp.bfloat16)
+    query_grad[...] = (slope * wide(kl) * mix).astype(jnp.bfloat16)
+    for lanes in lane_blocks(qs.shape[1]):
+        mode_state(rate[:, lanes], values[:, lanes].astype(jnp.float32), True, state_out, lanes)
 
 
 def input_grad_kernel(sb_next, sb_spec, spec, ks, vs, nxt_two, back, key_out, value_out):
@@ -205,23 +264,56 @@
 
 def run(body, name, blocked, fixed, outs, width, flops, scratch=()):
     channels = blocked[0].shape[1]
-    in_specs = [pl.BlockSpec((a.shape[0], width), lambda i: (0, i)) for a in blocked]
-    in_specs += [pl.BlockSpec(a.shape, lambda i: (0, 0)) for a in fixed]
-    out_specs = [pl.BlockSpec((rows, width), lambda i: (0, i)) for rows, _ in outs]
-    out_shape = [jax.ShapeDtypeStruct((rows, channels), dtype) for rows, dtype in outs]
-    moved = sum(a.size * a.dtype.itemsize for a in [*blocked, *fixed])
-    moved += sum(s.size * s.dtype.itemsize for s in out_shape)
+    n_in, n_fix, n_out = len(blocked), len(fixed), len(outs)
+    leaves = [i for i, (_, _, place) in enumerate(outs) if place == "hbm"]
+    count = channels // width
+
+    def whole(*refs):
+        ins, fix = refs[:n_in], refs[n_in : n_in + n_fix]
+        results, rest = list(refs[n_in + n_fix : n_in + n_fix + n_out]), refs[n_in + n_fix + n_out :]
+        hold, staged = rest[: len(scratch)], rest[len(scratch) : len(scratch) + len(leaves)]
+        copies = []
+        for step in range(count):
+            cut = pl.ds(step * width, width)
+            there = [r.at[:, cut] for r in results]
+            for slot, i in enumerate(leaves):
+                there[i] = staged[slot].at[:, cut]
+            body(*[r.at[:, cut] for r in ins], *fix, *there, *hold)
+            for slot, i in enumerate(leaves):
+                copy = pltpu.make_async_copy(there[i], results[i].at[:, cut], rest[-1].at[slot, step])
+                copy.start()
+                copies.append(copy)
+        for copy in copies:
+            copy.wait()
+
+    places = {"hbm": pltpu.HBM, "vmem": pltpu.VMEM}
+    scratch_shapes = [pltpu.VMEM((rows, width), dtype) for rows, dtype in scratch]
+    scratch_shapes += [pltpu.VMEM((outs[i][0], channels), outs[i][1]) for i in leaves]
+    if leaves:
+        scratch_shapes.append(pltpu.SemaphoreType.DMA((len(leaves), count)))
+    moved = sum(rows * channels * jnp.dtype(dtype).itemsize for rows, dtype, _ in outs)
     return pl.pallas_call(
-        body,
-        grid=(channels // width,),
-        in_specs=in_specs,
-        out_specs=out_specs,
-        out_shape=out_shape,
-        scratch_shapes=[pltpu.VMEM((rows, width), dtype) for rows, dtype in scratch],
+        whole,
+        in_specs=[pl.BlockSpec(memory_space=pltpu.VMEM)] * (n_in + n_fix),
+        out_specs=[pl.BlockSpec(memory_space=places[place]) for _, _, place in outs],
+        out_shape=[places[place]((rows, channels), dtype) for rows, dtype, place in outs],
+        scratch_shapes=scratch_shapes,
         compiler_params=pltpu.CompilerParams(vmem_limit_bytes=VMEM_BYTES),
         cost_estimate=pl.CostEstimate(flops=flops, bytes_accessed=moved, transcendentals=0),
         name=name,
-    )(*blocked, *fixed)
+    )(*[in_vmem(a) for a in [*blocked, *fixed]])
+
+
+def small(body, name, operands, outs, place=pltpu.VMEM):
+    return pl.pallas_call(
+        body,
+        in_specs=[pl.BlockSpec(memory_space=pltpu.VMEM)] * len(operands),
+        out_specs=[pl.BlockSpec(memory_space=pltpu.VMEM)] * len(outs),
+        out_shape=[place(shape, dtype) for shape, dtype in outs],
+        compiler_params=pltpu.CompilerParams(vmem_limit_bytes=VMEM_BYTES),
+        cost_estimate=pl.CostEstimate(flops=0, bytes_accessed=1024, transcendentals=0),
+        name=name,
+    )(*[in_vmem(a) for a in operands])
 
 
 def shifted(value, distance):
@@ -241,49 +333,80 @@
 
 
 def states_from(state, rate, block, later):
-    me = lax.axis_index("ctx")
-    got = jnp.zeros_like(state)
-    total = state
+    got, total = None, state
     for mask in masks():
         other = swapped(total, mask)
-        place = me % mask
-        mine_low = (me // mask) % 2 == 0
-        fade = jnp.exp(-(block * mask) * rate)
-        if later:
-            takes = mine_low
-            steps = mask - 1 - place
-        else:
-            takes = jnp.logical_not(mine_low)
-            steps = place
-        near = jnp.exp(-(block * steps).astype(jnp.float32) * rate)
-        got = got + jnp.where(takes, near, 0.0) * other
-        total = jnp.where(takes, total + fade * other, other + fade * total)
+
+        def body(*refs, mask=mask, start=got is None):
+            total, other, rate = refs[0][...], refs[1][...], refs[2][...]
+            total_out, got_out = refs[-2:]
+            me = lax.axis_index("ctx")
+            place = lax.rem(me, mask)
+            mine_low = lax.rem(lax.div(me, mask), 2) == 0
+            fade = jnp.exp(-(block * mask) * rate)
+            takes = mine_low if later else jnp.logical_not(mine_low)
+            steps = mask - 1 - place if later else place
+            taken = jnp.where(takes, jnp.exp((-block * steps).astype(jnp.float32) * rate) * other, 0.0)
+            got_out[...] = taken if start else refs[3][...] + taken
+            total_out[...] = jnp.where(takes, total + fade * other, other + fade * total)
+
+        operands = [total, other, rate] + ([] if got is None else [got])
+        total, got = small(body, "merge", operands, [(state.shape, jnp.float32)] * 2)
     return got
 
 
-def taps_total(part):
-    me = lax.axis_index("ctx")
+def added(pairs):
+    def body(*refs):
+        for i in range(len(pairs)):
+            total = refs[2 * i][...].astype(jnp.float32) + refs[2 * i + 1][...].astype(jnp.float32)
+            refs[2 * len(pairs) + i][...] = total.astype(jnp.bfloat16)
+
+    flat = [value for pair in pairs for value in pair]
+    return small(body, "added", flat, [(mine.shape, jnp.bfloat16) for mine, _ in pairs])
+
+
+def taps_total(part, scale):
     steps = masks()
-    channels = part.shape[1]
+    block, channels = part.shape
     half = channels // 2
-    first = me % 2 == 0
-    keep = jnp.where(first, part[:, :half], part[:, half:])
-    send = jnp.where(first, part[:, half:], part[:, :half])
-    mine = (keep.astype(jnp.float32) + swapped(send, 1).astype(jnp.float32)).astype(jnp.bfloat16)
-    pieces = [mine[:, : half // 2], mine[:, half // 2 :]]
+    quarter = half // 2
+
+    def apart(part, send, *keep):
+        first = lax.rem(lax.axis_index("ctx"), 2) == 0
+        low, high = part[:, :half], part[:, half:]
+        send[...] = jnp.where(first, high, low)
+        kept = jnp.where(first, low, high)
+        for i, piece in enumerate(keep):
+            piece[...] = kept[:, i * quarter : (i + 1) * quarter]
+
+    def merged(left, right, out):
+        out[:, :quarter] = left[...]
+        out[:, quarter:] = right[...]
+
+    def finish(left, right, other, out):
+        first = lax.rem(lax.axis_index("ctx"), 2) == 0
+        mine = jnp.concatenate([left[...], right[...]], axis=1).astype(jnp.float32) * scale
+        theirs = other[...].astype(jnp.float32) * scale
+        out[:, :half] = jnp.where(first, mine, theirs)
+        out[:, half:] = jnp.where(first, theirs, mine)
+
+    bf = jnp.bfloat16
+    send, *pieces = small(apart, "apart", [part], [((block, half), bf)] + [((block, quarter), bf)] * 2)
+    other = swapped(send, 1)
+
+    def first_sum(left, right, other, *outs):
+        for i, mine in enumerate((left, right)):
+            theirs = other[:, i * quarter : (i + 1) * quarter].astype(jnp.float32)
+            outs[i][...] = (mine[...].astype(jnp.float32) + theirs).astype(bf)
+
+    pieces = small(first_sum, "first_sum", [*pieces, other], [((block, quarter), bf)] * 2)
     rest = steps[1:]
     orders = [rest, rest[1:] + rest[:1]]
     for at in range(len(rest)):
-        others = [swapped(piece, order[at]) for piece, order in zip(pieces, orders)]
-        pieces = [
-            (piece.astype(jnp.float32) + other.astype(jnp.float32)).astype(jnp.bfloat16)
-            for piece, other in zip(pieces, others)
-        ]
-    mine = jnp.concatenate(pieces, axis=1)
+        pieces = added([(piece, swapped(piece, order[at])) for piece, order in zip(pieces, orders)])
+    (mine,) = small(merged, "merged", pieces, [((block, half), bf)])
     other = swapped(mine, 1)
-    low = jnp.where(first, mine, other)
-    high = jnp.where(first, other, mine)
-    return jnp.concatenate([low, high], axis=1)
+    return small(finish, "finish", [*pieces, other], [((block, channels), jnp.float32)], pltpu.HBM)[0]
 
 
 def local(
@@ -301,27 +424,28 @@
     modes = long_rate.shape[0]
     sequence = block * lax.axis_size("ctx")
     half, full = jnp.bfloat16, jnp.float32
-    own_two, own_three, nxt_two, back = [jnp.asarray(t) for t in tables(block)]
+    matrices = [jnp.asarray(t) for t in tables(block)]
     width = 512
     unit = 2 * block * block * channels * 2
 
-    short_in, back_state = run(
-        front_kernel,
-        "front",
-        [key_short, value_short, query_long, cotangent, long_rate],
-        [],
-        [(block, half), (modes, full)],
-        width,
-        4 * modes * block * channels,
-    )
+    brought, short_in, back_state = front(
+        key_short,
+        value_short,
+        query_long,
+        cotangent,
+        long_rate,
+        [long_residue, query_short, key_long, short_taps, *matrices],
+        width,
+    )
+    rate, ct, ql, ks, vs, res, qs, kl, taps, own_two, own_three, nxt_two, back = brought
+    back_far = states_from(back_state, rate, block, True)
     halo = shifted(short_in, 1)
-    back_far = states_from(back_state, long_rate, block, True)
-    grad_local, long_spec, short_spec = run(
+    grad_local, long_spec = run(
         filters_kernel,
         "filters",
-        [query_long, cotangent, short_taps, long_rate, long_residue],
+        [ql, ct, rate, res],
         [own_three, back],
-        [(block, full), (2 * block, full), (2 * block, full)],
+        [(block, full, "vmem"), (2 * block, full, "vmem")],
         width,
         12 * unit,
         [(block, full)],
@@ -329,40 +453,45 @@
     long_grad, short_back = run(
         long_grad_kernel,
         "long_grad",
-        [grad_local, back_far, long_rate, long_residue, key_long, query_short],
+        [grad_local, back_far, rate, res, kl, qs],
         [],
-        [(block, half), (block, half)],
+        [(block, half, "vmem"), (block, half, "vmem")],
         width,
         4 * modes * block * channels,
     )
-    in_spec, short_mix, hidden, long_in, fore_state = run(
+    sb_spec, in_spec, part = run(
+        taps_kernel,
+        "taps",
+        [short_back, short_in, halo],
+        [own_two, nxt_two, back],
+        [(2 * block, full, "vmem"), (2 * block, full, "vmem"), (block, half, "vmem")],
+        width,
+        5 * unit,
+    )
+    taps_grad = taps_total(part, sequence ** (-0.5))
+    sb_next = shifted(short_back, -1)
+    short_spec, long_in, fore_state, key_long_grad, query_short_grad = run(
         short_kernel,
         "short",
-        [short_in, halo, short_spec, query_short, key_long, long_rate],
-        [own_two, nxt_two, back],
-        [(2 * block, full), (block, full), (block, half), (block, half), (modes, full)],
+        [in_spec, taps, qs, kl, rate, long_grad],
+        [own_three, back],
+        [
+            (2 * block, full, "vmem"),
+            (block, half, "vmem"),
+            (modes, full, "vmem"),
+            (block, half, "hbm"),
+            (block, half, "hbm"),
+        ],
         width,
         7 * unit,
     )
-    sb_spec, part, key_long_grad, query_short_grad = run(
-        taps_kernel,
-        "taps",
-        [short_back, in_spec, long_grad, key_long, hidden, short_mix],
-        [own_two, back],
-        [(2 * block, full), (block, half), (block, half), (block, half)],
-        width,
-        5 * unit,
-    )
-    sb_next = shifted(short_back, -1)
-    taps_sum = taps_total(part)
-    taps_grad = taps_sum.astype(full) * (sequence ** (-0.5))
-    fore_far = states_from(fore_state, long_rate, block, False)
+    fore_far = states_from(fore_state, rate, block, False)
     core_output, query_long_grad = run(
         long_kernel,
         "long",
-        [long_in, long_spec, fore_far, long_rate, long_residue, query_long, cotangent],
+        [long_in, long_spec, fore_far, rate, res, ql, ct],
         [own_two, back],
-        [(block, half), (block, half)],
+        [(block, half, "hbm"), (block, half, "hbm")],
         width,
         5 * unit,
         [(block, full)],
@@ -370,9 +499,9 @@
     key_short_grad, value_short_grad = run(
         input_grad_kernel,
         "input_grad",
-        [sb_next, sb_spec, short_spec, key_short, value_short],
+        [sb_next, sb_spec, short_spec, ks, vs],
         [nxt_two, back],
-        [(block, half), (block, half)],
+        [(block, half, "hbm"), (block, half, "hbm")],
         width,
         5 * unit,
     )

time: 93 us -> 63.5 us (0.68)
  the two profiles are of different devices: /device:TPU:27 before, /device:TPU:0 now
where the time goes in v1:
time: 63.5 us; the launch traced here: 63.4 us
  Pallas kernels  24.9 us (39%)
  starting transfers between devices  20.3 us (32%)
  waiting for transfers between devices  17.3 us (27%)
  between operations  0.81 us (1%)
    pallas_call x6, Pallas kernels, run(): pl.pallas_call(whole, in_specs=[pl.BlockSpec(memory_space=pltpu.VMEM)] *...  18.8 us
    ppermute x12, waiting for transfers between devices, swapped(): return lax.ppermute(value, 'ctx', [(i, i ^ mask) for i in range(size)])  17.3 us
    ppermute x12, starting transfers between devices, swapped(): return lax.ppermute(value, 'ctx', [(i, i ^ mask) for i in range(size)])  16.5 us
    ppermute x2, starting transfers between devices, shifted(): return lax.ppermute(value, 'ctx', pairs)  3.85 us
    pallas_call x1, Pallas kernels, front(): pl.pallas_call(body, in_specs=[pl.BlockSpec(memory_space=pltpu.HBM)] * co...  3.1 us
    pallas_call x12, Pallas kernels, small(): pl.pallas_call(body, in_specs=[pl.BlockSpec(memory_space=pltpu.VMEM)] * l...  3.05 us
  transfers between devices with their start and end apart: 14, of which 8 were waited for; matrix products, arithmetic and copies ran while one was open for 0% of the time, Pallas kernels for 29%

profile of v1, /device:TPU:0, one launch (start us, length us, event | category | flops | bytes accessed | tf_op | source)
XLA Modules:
  0.0 63.4 jit_solution(15462824413930488557)
XLA Ops:
  0.6 3.1 %front.1 = (f32[16,2048]{1,0:T(8,128)S(1)}, bf16[128,2048]{1,0:T(8,128)(2,1)S(1)}, bf16[128,2048]{1,0:T(8,128)(2,1)S(1)}, bf16[128,2048]{1,0:T(8,128)(2,1)S(1)},...) custom-call(f32[16,2048]{1,0:T(8,128)} %refs_0_.1, ...), custom_call_target="tpu_custom_call" | custom-call | bytes 8388608 | tf_op jit(solution)/shard_map/front/pallas_call | solution.py:191
  3.7 2.4 %collective-permute-start.3 = (bf16[128,2048]{1,0:T(8,128)(2,1)S(1)}, bf16[128,2048]{1,0:T(8,128)(2,1)S(1)}, u32[]{:S(2)}, u32[]{:S(2)}) collective-permute-start(bf16[128,2048]{1,0:T(8,128)(2,1)S(1)} %get-tuple-element.73.refs_1_), channel_id=1, source_target_pairs={{0,4},{4,8},{8,12},{12,16},{16,20},{20,24},{24,28},{1,5},{5,9},{9,... | collective-permute-start | bytes 1572872 | tf_op jit(solution)/shard_map/ppermute | solution.py:322
  6.1 2.6 %collective-permute-start = (f32[16,2048]{1,0:T(8,128)S(1)}, f32[16,2048]{1,0:T(8,128)S(1)}, u32[]{:S(2)}, u32[]{:S(2)}) collective-permute-start(f32[16,2048]{1,0:T(8,128)S(1)} %get-tuple-element.64.refs_0_), channel_id=1, source_target_pairs={{0,4},{4,0},{8,12},{12,8},{16,20},{20,16},{24,28},{28,24},{1,5},{5... | collective-permute-start | bytes 393224 | tf_op jit(solution)/shard_map/ppermute | solution.py:327
  9.8 1.6 %collective-permute-start.1 = (f32[16,2048]{1,0:T(8,128)S(1)}, f32[16,2048]{1,0:T(8,128)S(1)}, u32[]{:S(2)}, u32[]{:S(2)}) collective-permute-start(f32[16,2048]{1,0:T(8,128)S(1)} %get-tuple-element.65.refs_0_), channel_id=1, source_target_pairs={{0,8},{4,12},{8,0},{12,4},{16,24},{20,28},{24,16},{28,20},{1,9},{5... | collective-permute-start | bytes 393224 | tf_op jit(solution)/shard_map/ppermute | solution.py:327
  11.4 4.9 %collective-permute-done.1.refs_1_ = f32[16,2048]{1,0:T(8,128)S(1)} collective-permute-done((f32[16,2048]{1,0:T(8,128)S(1)}, f32[16,2048]{1,0:T(8,128)S(1)}, u32[]{:S(2)}, u32[]{:S(2)}) %collective-permute-start.1) | collective-permute-done | bytes 131104 | tf_op jit(solution)/shard_map/ppermute | solution.py:327
  17.3 3.8 %filters.1 = (f32[128,2048]{1,0:T(8,128)S(1)}, f32[256,2048]{1,0:T(8,128)S(1)}) custom-call(bf16[128,2048]{1,0:T(8,128)(2,1)S(1)} %get-tuple-element.57.refs_0_.refs_5_, bf16[128,2048]{1,0:T(8,128)(2,1)S(1)} %get-tuple-element.58.refs_1_.refs_6_, f32[16,2048]{1,0:T(8,128)S(1)} %get-tuple-element.59.refs_2_.refs_4_.refs_3_, ...), custom_call_target="tpu_custom_call" | custom-call | flops 1610612736 | bytes 3145728 | tf_op jit(solution)/shard_map/filters/pallas_call | solution.py:295
  22.2 2.2 %long_grad.1 = (bf16[128,2048]{1,0:T(8,128)(2,1)S(1)}, bf16[128,2048]{1,0:T(8,128)(2,1)S(1)}) custom-call(f32[128,2048]{1,0:T(8,128)S(1)} %get-tuple-element.63.refs_0_, f32[16,2048]{1,0:T(8,128)S(1)} %get-tuple-element.69.refs_1_, f32[16,2048]{1,0:T(8,128)S(1)} %get-tuple-element.59.refs_2_.refs_4_.refs_3_, ...), custom_call_target="tpu_custom_call" | custom-call | flops 16777216 | bytes 1048576 | tf_op jit(solution)/shard_map/long_grad/pallas_call | solution.py:295
  24.3 2.2 %taps.1 = (f32[256,2048]{1,0:T(8,128)S(1)}, f32[256,2048]{1,0:T(8,128)S(1)}, bf16[128,2048]{1,0:T(8,128)(2,1)S(1)}) custom-call(bf16[128,2048]{1,0:T(8,128)(2,1)S(1)} %get-tuple-element.72.refs_0_, bf16[128,2048]{1,0:T(8,128)(2,1)S(1)} %get-tuple-element.73.refs_1_, bf16[128,2048]{1,0:T(8,128)(2,1)S(1)} %collective-permute-done.3.refs_2_, ...), custom_call_target="tpu_custom_call" | custom-call | flops 671088640 | bytes 4718592 | tf_op jit(solution)/shard_map/taps/pallas_call | solution.py:295
  26.6 1.9 %collective-permute-start.8 = (bf16[128,1024]{1,0:T(8,128)(2,1)S(1)}, bf16[128,1024]{1,0:T(8,128)(2,1)S(1)}, u32[]{:S(2)}, u32[]{:S(2)}) collective-permute-start(bf16[128,1024]{1,0:T(8,128)(2,1)S(1)} %get-tuple-element.100), channel_id=1, source_target_pairs={{0,4},{4,0},{8,12},{12,8},{16,20},{20,16},{24,28},{28,24},{1,5},{5... | collective-permute-start | bytes 786440 | tf_op jit(solution)/shard_map/ppermute | solution.py:327
  28.5 1.5 %collective-permute-start.7 = (bf16[128,2048]{1,0:T(8,128)(2,1)S(1)}, bf16[128,2048]{1,0:T(8,128)(2,1)S(1)}, u32[]{:S(2)}, u32[]{:S(2)}) collective-permute-start(bf16[128,2048]{1,0:T(8,128)(2,1)S(1)} %get-tuple-element.72.refs_0_), channel_id=1, source_target_pairs={{4,0},{8,4},{12,8},{16,12},{20,16},{24,20},{28,24},{5,1},{9,5},{13... | collective-permute-start | bytes 1572872 | tf_op jit(solution)/shard_map/ppermute | solution.py:322
  30.0 2.5 %collective-permute-start.9 = (bf16[128,512]{1,0:T(8,128)(2,1)S(1)}, bf16[128,512]{1,0:T(8,128)(2,1)S(1)}, u32[]{:S(2)}, u32[]{:S(2)}) collective-permute-start(bf16[128,512]{1,0:T(8,128)(2,1)S(1)} %get-tuple-element.101.refs_0_), channel_id=1, source_target_pairs={{0,8},{4,12},{8,0},{12,4},{16,24},{20,28},{24,16},{28,20},{1,9},{5... | collective-permute-start | bytes 393224 | tf_op jit(solution)/shard_map/ppermute | solution.py:327
  32.5 1.6 %collective-permute-start.10 = (bf16[128,512]{1,0:T(8,128)(2,1)S(1)}, bf16[128,512]{1,0:T(8,128)(2,1)S(1)}, u32[]{:S(2)}, u32[]{:S(2)}) collective-permute-start(bf16[128,512]{1,0:T(8,128)(2,1)S(1)} %get-tuple-element.102.refs_2_), channel_id=1, source_target_pairs={{0,16},{4,20},{8,24},{12,28},{16,0},{20,4},{24,8},{28,12},{1,17},{... | collective-permute-start | bytes 393224 | tf_op jit(solution)/shard_map/ppermute | solution.py:327
  34.1 4.5 %short.1 = (f32[256,2048]{1,0:T(8,128)S(1)}, bf16[128,2048]{1,0:T(8,128)(2,1)S(1)}, f32[16,2048]{1,0:T(8,128)S(1)}, bf16[128,2048]{1,0:T(8,128)(2,1)}, bf16[128,2048]{1,0:T(8,128)(2,1)}) custom-call(f32[256,2048]{1,0:T(8,128)S(1)} %get-tuple-element.76.refs_0_, f32[128,2048]{1,0:T(8,128)S(1)} %get-tuple-element.77.refs_1_, ...), custom_call_target="tpu_custom_call" | custom-call | flops 939524096 | bytes 3801088 | tf_op jit(solution)/shard_map/short/pallas_call | solution.py:295
  38.6 3.5 %collective-permute-done.9.refs_1_ = bf16[128,512]{1,0:T(8,128)(2,1)S(1)} collective-permute-done((bf16[128,512]{1,0:T(8,128)(2,1)S(1)}, bf16[128,512]{1,0:T(8,128)(2,1)S(1)}, u32[]{:S(2)}, u32[]{:S(2)}) %collective-permute-start.9) | collective-permute-done | bytes 131104 | tf_op jit(solution)/shard_map/ppermute | solution.py:327
  42.1 1.7 %collective-permute-start.11 = (bf16[128,512]{1,0:T(8,128)(2,1)S(1)}, bf16[128,512]{1,0:T(8,128)(2,1)S(1)}, u32[]{:S(2)}, u32[]{:S(2)}) collective-permute-start(bf16[128,512]{1,0:T(8,128)(2,1)S(1)} %get-tuple-element.103.refs_0_), channel_id=1, source_target_pairs={{0,16},{4,20},{8,24},{12,28},{16,0},{20,4},{24,8},{28,12},{1,17},{... | collective-permute-start | bytes 393224 | tf_op jit(solution)/shard_map/ppermute | solution.py:327
  44.7 1.3 %collective-permute-start.5 = (f32[16,2048]{1,0:T(8,128)S(1)}, f32[16,2048]{1,0:T(8,128)S(1)}, u32[]{:S(2)}, u32[]{:S(2)}) collective-permute-start(f32[16,2048]{1,0:T(8,128)S(1)} %get-tuple-element.82.refs_0_), channel_id=1, source_target_pairs={{0,8},{4,12},{8,0},{12,4},{16,24},{20,28},{24,16},{28,20},{1,9},{5... | collective-permute-start | bytes 393224 | tf_op jit(solution)/shard_map/ppermute | solution.py:327
  46.0 1.2 %collective-permute-done.11.refs_1_ = bf16[128,512]{1,0:T(8,128)(2,1)S(1)} collective-permute-done((bf16[128,512]{1,0:T(8,128)(2,1)S(1)}, bf16[128,512]{1,0:T(8,128)(2,1)S(1)}, u32[]{:S(2)}, u32[]{:S(2)}) %collective-permute-start.11) | collective-permute-done | bytes 131104 | tf_op jit(solution)/shard_map/ppermute | solution.py:327
  47.2 1.6 %collective-permute-done.12.refs_3_ = bf16[128,512]{1,0:T(8,128)(2,1)S(1)} collective-permute-done((bf16[128,512]{1,0:T(8,128)(2,1)S(1)}, bf16[128,512]{1,0:T(8,128)(2,1)S(1)}, u32[]{:S(2)}, u32[]{:S(2)}) %collective-permute-start.12) | collective-permute-done | bytes 131104 | tf_op jit(solution)/shard_map/ppermute | solution.py:327
  49.0 1.2 %collective-permute-done.5.refs_1_ = f32[16,2048]{1,0:T(8,128)S(1)} collective-permute-done((f32[16,2048]{1,0:T(8,128)S(1)}, f32[16,2048]{1,0:T(8,128)S(1)}, u32[]{:S(2)}, u32[]{:S(2)}) %collective-permute-start.5) | collective-permute-done | bytes 131104 | tf_op jit(solution)/shard_map/ppermute | solution.py:327
  50.3 1.5 %collective-permute-start.6 = (f32[16,2048]{1,0:T(8,128)S(1)}, f32[16,2048]{1,0:T(8,128)S(1)}, u32[]{:S(2)}, u32[]{:S(2)}) collective-permute-start(f32[16,2048]{1,0:T(8,128)S(1)} %get-tuple-element.84.refs_0_), channel_id=1, source_target_pairs={{0,16},{4,20},{8,24},{12,28},{16,0},{20,4},{24,8},{28,12},{1,17},{... | collective-permute-start | bytes 393224 | tf_op jit(solution)/shard_map/ppermute | solution.py:327
  51.8 3.5 %collective-permute-done.6.refs_1_ = f32[16,2048]{1,0:T(8,128)S(1)} collective-permute-done((f32[16,2048]{1,0:T(8,128)S(1)}, f32[16,2048]{1,0:T(8,128)S(1)}, u32[]{:S(2)}, u32[]{:S(2)}) %collective-permute-start.6) | collective-permute-done | bytes 131104 | tf_op jit(solution)/shard_map/ppermute | solution.py:327
  56.0 3.7 %long.1 = (bf16[128,2048]{1,0:T(8,128)(2,1)}, bf16[128,2048]{1,0:T(8,128)(2,1)}) custom-call(bf16[128,2048]{1,0:T(8,128)(2,1)S(1)} %get-tuple-element.79.refs_0_, f32[256,2048]{1,0:T(8,128)S(1)} %get-tuple-element.80.refs_1_, f32[16,2048]{1,0:T(8,128)S(1)} %get-tuple-element.86.refs_2_, f32[16,2048]{1,0:T(8,128)S(1)} %get-tuple-element.59.refs_2_.refs_4_.refs_3_, ...), custom_call_target="tpu_custom_call" | custom-call | flops 671088640 | bytes 1048576 | tf_op jit(solution)/shard_map/long/pallas_call | solution.py:295
  59.7 2.5 %input_grad.1 = (bf16[128,2048]{1,0:T(8,128)(2,1)}, bf16[128,2048]{1,0:T(8,128)(2,1)}) custom-call(bf16[128,2048]{1,0:T(8,128)(2,1)S(1)} %collective-permute-done.7.refs_0_, f32[256,2048]{1,0:T(8,128)S(1)} %get-tuple-element.89.refs_1_, f32[256,2048]{1,0:T(8,128)S(1)} %get-tuple-element.90.refs_2_, bf16[128,2048]{1,0:T(8,128)(2,1)S(1)} %get-tuple-element.91.refs_3_, ...), custom_call_target="tpu_custom_call" | custom-call | flops 671088640 | bytes 1048576 | tf_op jit(solution)/shard_map/input_grad/pallas_call | solution.py:295
  62.2 1.1 %finish.1 = f32[128,2048]{1,0:T(8,128)} custom-call(bf16[128,512]{1,0:T(8,128)(2,1)S(1)} %get-tuple-element.105.left, bf16[128,512]{1,0:T(8,128)(2,1)S(1)} %get-tuple-element.106.right, bf16[128,1024]{1,0:T(8,128)(2,1)S(1)} %collective-permute-done.13.other), custom_call_target="tpu_custom_call" | custom-call | bytes 1024 | tf_op jit(solution)/shard_map/finish/pallas_call | solution.py:308
  (23 shorter events, 5.1 us)
Async XLA Ops:
  3.7 20.6 %collective-permute-start.3 = (bf16[128,2048]{1,0:T(8,128)(2,1)S(1)}, bf16[128,2048]{1,0:T(8,128)(2,1)S(1)}, u32[]{:S(2)}, u32[]{:S(2)}) collective-permute-start(bf16[128,2048]{1,0:T(8,128)(2,1)S(1)} %get-tuple-element.73.refs_1_), channel_id=1, source_target_pairs={{0,4},{4,8},{8,12},{12,16},{16,20},{20,24},{24,28},{1,5},{5,9},{9,... | collective-permute-start | bytes 1572872 | tf_op jit(solution)/shard_map/ppermute | solution.py:322
  6.1 3.6 %collective-permute-start = (f32[16,2048]{1,0:T(8,128)S(1)}, f32[16,2048]{1,0:T(8,128)S(1)}, u32[]{:S(2)}, u32[]{:S(2)}) collective-permute-start(f32[16,2048]{1,0:T(8,128)S(1)} %get-tuple-element.64.refs_0_), channel_id=1, source_target_pairs={{0,4},{4,0},{8,12},{12,8},{16,20},{20,16},{24,28},{28,24},{1,5},{5... | collective-permute-start | bytes 393224 | tf_op jit(solution)/shard_map/ppermute | solution.py:327
  9.8 6.5 %collective-permute-start.1 = (f32[16,2048]{1,0:T(8,128)S(1)}, f32[16,2048]{1,0:T(8,128)S(1)}, u32[]{:S(2)}, u32[]{:S(2)}) collective-permute-start(f32[16,2048]{1,0:T(8,128)S(1)} %get-tuple-element.65.refs_0_), channel_id=1, source_target_pairs={{0,8},{4,12},{8,0},{12,4},{16,24},{20,28},{24,16},{28,20},{1,9},{5... | collective-permute-start | bytes 393224 | tf_op jit(solution)/shard_map/ppermute | solution.py:327
  16.4 5.0 %collective-permute-start.2 = (f32[16,2048]{1,0:T(8,128)S(1)}, f32[16,2048]{1,0:T(8,128)S(1)}, u32[]{:S(2)}, u32[]{:S(2)}) collective-permute-start(f32[16,2048]{1,0:T(8,128)S(1)} %get-tuple-element.67.refs_0_), channel_id=1, source_target_pairs={{0,16},{4,20},{8,24},{12,28},{16,0},{20,4},{24,8},{28,12},{1,17},{... | collective-permute-start | bytes 393224 | tf_op jit(solution)/shard_map/ppermute | solution.py:327
  26.6 3.3 %collective-permute-start.8 = (bf16[128,1024]{1,0:T(8,128)(2,1)S(1)}, bf16[128,1024]{1,0:T(8,128)(2,1)S(1)}, u32[]{:S(2)}, u32[]{:S(2)}) collective-permute-start(bf16[128,1024]{1,0:T(8,128)(2,1)S(1)} %get-tuple-element.100), channel_id=1, source_target_pairs={{0,4},{4,0},{8,12},{12,8},{16,20},{20,16},{24,28},{28,24},{1,5},{5... | collective-permute-start | bytes 786440 | tf_op jit(solution)/shard_map/ppermute | solution.py:327
  28.5 31.3 %collective-permute-start.7 = (bf16[128,2048]{1,0:T(8,128)(2,1)S(1)}, bf16[128,2048]{1,0:T(8,128)(2,1)S(1)}, u32[]{:S(2)}, u32[]{:S(2)}) collective-permute-start(bf16[128,2048]{1,0:T(8,128)(2,1)S(1)} %get-tuple-element.72.refs_0_), channel_id=1, source_target_pairs={{4,0},{8,4},{12,8},{16,12},{20,16},{24,20},{28,24},{5,1},{9,5},{13... | collective-permute-start | bytes 1572872 | tf_op jit(solution)/shard_map/ppermute | solution.py:322
  30.0 12.1 %collective-permute-start.9 = (bf16[128,512]{1,0:T(8,128)(2,1)S(1)}, bf16[128,512]{1,0:T(8,128)(2,1)S(1)}, u32[]{:S(2)}, u32[]{:S(2)}) collective-permute-start(bf16[128,512]{1,0:T(8,128)(2,1)S(1)} %get-tuple-element.101.refs_0_), channel_id=1, source_target_pairs={{0,8},{4,12},{8,0},{12,4},{16,24},{20,28},{24,16},{28,20},{1,9},{5... | collective-permute-start | bytes 393224 | tf_op jit(solution)/shard_map/ppermute | solution.py:327
  32.5 9.6 %collective-permute-start.10 = (bf16[128,512]{1,0:T(8,128)(2,1)S(1)}, bf16[128,512]{1,0:T(8,128)(2,1)S(1)}, u32[]{:S(2)}, u32[]{:S(2)}) collective-permute-start(bf16[128,512]{1,0:T(8,128)(2,1)S(1)} %get-tuple-element.102.refs_2_), channel_id=1, source_target_pairs={{0,16},{4,20},{8,24},{12,28},{16,0},{20,4},{24,8},{28,12},{1,17},{... | collective-permute-start | bytes 393224 | tf_op jit(solution)/shard_map/ppermute | solution.py:327
  38.5 6.1 %collective-permute-start.4 = (f32[16,2048]{1,0:T(8,128)S(1)}, f32[16,2048]{1,0:T(8,128)S(1)}, u32[]{:S(2)}, u32[]{:S(2)}) collective-permute-start(f32[16,2048]{1,0:T(8,128)S(1)} %get-tuple-element.81.refs_0_), channel_id=1, source_target_pairs={{0,4},{4,0},{8,12},{12,8},{16,20},{20,16},{24,28},{28,24},{1,5},{5... | collective-permute-start | bytes 393224 | tf_op jit(solution)/shard_map/ppermute | solution.py:327
  42.1 5.0 %collective-permute-start.11 = (bf16[128,512]{1,0:T(8,128)(2,1)S(1)}, bf16[128,512]{1,0:T(8,128)(2,1)S(1)}, u32[]{:S(2)}, u32[]{:S(2)}) collective-permute-start(bf16[128,512]{1,0:T(8,128)(2,1)S(1)} %get-tuple-element.103.refs_0_), channel_id=1, source_target_pairs={{0,16},{4,20},{8,24},{12,28},{16,0},{20,4},{24,8},{28,12},{1,17},{... | collective-permute-start | bytes 393224 | tf_op jit(solution)/shard_map/ppermute | solution.py:327
  43.8 5.0 %collective-permute-start.12 = (bf16[128,512]{1,0:T(8,128)(2,1)S(1)}, bf16[128,512]{1,0:T(8,128)(2,1)S(1)}, u32[]{:S(2)}, u32[]{:S(2)}) collective-permute-start(bf16[128,512]{1,0:T(8,128)(2,1)S(1)} %get-tuple-element.104.refs_2_), channel_id=1, source_target_pairs={{0,8},{4,12},{8,0},{12,4},{16,24},{20,28},{24,16},{28,20},{1,9},{5... | collective-permute-start | bytes 393224 | tf_op jit(solution)/shard_map/ppermute | solution.py:327
  44.7 5.5 %collective-permute-start.5 = (f32[16,2048]{1,0:T(8,128)S(1)}, f32[16,2048]{1,0:T(8,128)S(1)}, u32[]{:S(2)}, u32[]{:S(2)}) collective-permute-start(f32[16,2048]{1,0:T(8,128)S(1)} %get-tuple-element.82.refs_0_), channel_id=1, source_target_pairs={{0,8},{4,12},{8,0},{12,4},{16,24},{20,28},{24,16},{28,20},{1,9},{5... | collective-permute-start | bytes 393224 | tf_op jit(solution)/shard_map/ppermute | solution.py:327
  48.9 13.3 %collective-permute-start.13 = (bf16[128,1024]{1,0:T(8,128)(2,1)S(1)}, bf16[128,1024]{1,0:T(8,128)(2,1)S(1)}, u32[]{:S(2)}, u32[]{:S(2)}) collective-permute-start(bf16[128,1024]{1,0:T(8,128)(2,1)S(1)} %merged.1), channel_id=1, source_target_pairs={{0,4},{4,0},{8,12},{12,8},{16,20},{20,16},{24,28},{28,24},{1,5},{5... | collective-permute-start | bytes 786440 | tf_op jit(solution)/shard_map/ppermute | solution.py:327
  50.3 5.0 %collective-permute-start.6 = (f32[16,2048]{1,0:T(8,128)S(1)}, f32[16,2048]{1,0:T(8,128)S(1)}, u32[]{:S(2)}, u32[]{:S(2)}) collective-permute-start(f32[16,2048]{1,0:T(8,128)S(1)} %get-tuple-element.84.refs_0_), channel_id=1, source_target_pairs={{0,16},{4,20},{8,24},{12,28},{16,0},{20,4},{24,8},{28,12},{1,17},{... | collective-permute-start | bytes 393224 | tf_op jit(solution)/shard_map/ppermute | solution.py:327

commit v2 on v0

v2 whole, which is shorter than its diff:
```python
import jax
import jax.numpy as jnp
import numpy as np
from jax import lax
from jax.experimental import pallas as pl
from jax.experimental.pallas import tpu as pltpu
from jax.sharding import PartitionSpec as P

ROWS = 8
LANES = 128
VMEM_BYTES = 16 * 1024 * 1024


def split_np(matrix):
    high = matrix.astype(jnp.bfloat16)
    low = (matrix - high.astype(np.float64)).astype(jnp.bfloat16)
    return high, low


def tables(block):
    length = 2 * block
    freq = np.pi * (2 * np.arange(block)[:, None] + 1) / length
    here = freq * np.arange(block)[None, :]
    after = freq * (np.arange(block)[None, :] + block)
    own = np.concatenate([np.cos(here), -np.sin(here)], axis=0)
    nxt = np.concatenate([np.cos(after), -np.sin(after)], axis=0)
    own_hi, own_lo = split_np(own)
    nxt_hi, nxt_lo = split_np(nxt)
    own_two = np.concatenate([own_hi, own_lo], axis=1)
    own_three = np.concatenate([own_hi, own_hi, own_lo], axis=1)
    nxt_two = np.concatenate([nxt_hi, nxt_lo], axis=1)
    back = np.concatenate([own_hi.T, own_lo.T], axis=0)
    return own_two, own_three, nxt_two, back


def mxu(matrix, data):
    return lax.dot_general(
        matrix, data, (((1,), (0,)), ((), ())), preferred_element_type=jnp.float32
    )


def split(value):
    high = value.astype(jnp.bfloat16)
    low = (value - high.astype(jnp.float32)).astype(jnp.bfloat16)
    return high, low


def dft_exact(matrix_two, data):
    return mxu(matrix_two, jnp.concatenate([data, data], axis=0))


def dft_full(matrix_three, data):
    high, low = split(data)
    return mxu(matrix_three, jnp.concatenate([high, low, high], axis=0))


def dft_back(back, spec_re, spec_im):
    block = spec_re.shape[0]
    high, low = split(jnp.concatenate([spec_re, spec_im], axis=0))
    both = mxu(back, high)
    return both[:block] + both[block:] + mxu(back[:block], low)


def halves(spec):
    block = spec.shape[0] // 2
    return spec[:block], spec[block:]


def times(left, right):
    left_re, left_im = halves(left)
    right_re, right_im = halves(right)
    return left_re * right_re - left_im * right_im, left_re * right_im + left_im * right_re


def times_conj(left, right):
    left_re, left_im = halves(left)
    right_re, right_im = halves(right)
    return left_re * right_re + left_im * right_im, left_im * right_re - left_re * right_im


def sublane(shape):
    return lax.broadcasted_iota(jnp.int32, shape, 0).astype(jnp.float32)


def spread(row):
    return jnp.broadcast_to(row, (ROWS, row.shape[1]))


def mode_sum(rate, weight, start, forward, block):
    sub = sublane((ROWS, rate.shape[1]))
    age = start + (sub if forward else ROWS - 1 - sub)
    waves, falls = [], []
    for mode in range(rate.shape[0]):
        pace = spread(rate[mode : mode + 1])
        waves.append(spread(weight[mode : mode + 1]) * jnp.exp(-pace * age))
        falls.append(jnp.exp(-ROWS * pace))
    tiles = []
    count = block // ROWS
    for step in range(count):
        total = waves[0]
        for wave in waves[1:]:
            total = total + wave
        tiles.append(total)
        if step < count - 1:
            waves = [wave * fall for wave, fall in zip(waves, falls)]
    if not forward:
        tiles = tiles[::-1]
    return jnp.concatenate(tiles, axis=0)


def mode_state(rate, data, forward, out_ref, lanes):
    block = data.shape[0]
    sub = sublane((ROWS, rate.shape[1]))
    age = (ROWS - 1 - sub) if forward else sub
    tiles = [data[t : t + ROWS] for t in range(0, block, ROWS)]
    if not forward:
        tiles = tiles[::-1]
    for mode in range(rate.shape[0]):
        pace = spread(rate[mode : mode + 1])
        fall = jnp.exp(-ROWS * pace)
        total = tiles[0]
        for tile in tiles[1:]:
            total = total * fall + tile
        out_ref[mode : mode + 1, lanes] = jnp.sum(total * jnp.exp(-pace * age), axis=0, keepdims=True)


def lane_blocks(width):
    return [slice(at, at + LANES) for at in range(0, width, LANES)]


def wide(ref, lanes=slice(None)):
    return ref[:, lanes].astype(jnp.float32)


def in_vmem(value):
    return pltpu.with_memory_space_constraint(value, pltpu.VMEM)


def in_hbm(value):
    return pltpu.with_memory_space_constraint(value, pltpu.HBM)


def load(brought, outs, body, name, first, width, after=(), scratch=(), blocked=(), fixed=()):
    count, n_after, ready = len(brought), len(after), len(blocked) + len(fixed)
    channels = brought[0].shape[1]
    parts = channels // width
    pieces = [parts] * first + [1] * (count - first)
    offsets = [sum(pieces[:i]) for i in range(count)]

    def whole(*refs):
        sources, refs = refs[:count], refs[count:]
        ins, fix, refs = refs[: len(blocked)], refs[len(blocked) : ready], refs[ready + n_after :]
        results, more, sems = refs[:count], refs[count:-1], refs[-1]
        copies = []
        for i in range(count):
            step = sources[i].shape[1] // pieces[i]
            row = []
            for k in range(pieces[i]):
                cut = pl.ds(k * step, step)
                row.append(
                    pltpu.make_async_copy(sources[i].at[:, cut], results[i].at[:, cut], sems.at[offsets[i] + k])
                )
            copies.append(row)
        for k in range(parts):
            for row in copies[:first]:
                row[k].start()
        for row in copies[first:]:
            row[0].start()
        for k in range(parts):
            for row in copies[:first]:
                row[k].wait()
            cut = pl.ds(k * width, width)
            held = more[len(outs) :]
            there = [r.at[:, cut] for r in more[: len(outs)]]
            body(*[r.at[:, cut] for r in [*results[:first], *ins]], *fix, *there, *held)
        for row in copies[first:]:
            row[0].wait()

    out_shape = [pltpu.VMEM(a.shape, a.dtype) for a in brought]
    out_shape += [pltpu.VMEM(shape, dtype) for shape, dtype in outs]
    results = pl.pallas_call(
        whole,
        in_specs=[pl.BlockSpec(memory_space=pltpu.HBM)] * count
        + [pl.BlockSpec(memory_space=pltpu.VMEM)] * ready
        + [pl.BlockSpec(memory_space=pl.ANY)] * n_after,
        out_specs=[pl.BlockSpec(memory_space=pltpu.VMEM)] * len(out_shape),
        out_shape=out_shape,
        scratch_shapes=[pltpu.VMEM((rows, width), dtype) for rows, dtype in scratch]
        + [pltpu.SemaphoreType.DMA((sum(pieces),))],
        compiler_params=pltpu.CompilerParams(vmem_limit_bytes=VMEM_BYTES),
        cost_estimate=pl.CostEstimate(flops=0, bytes_accessed=1024, transcendentals=0),
        name=name,
    )(*[in_hbm(a) for a in brought], *[in_vmem(a) for a in [*blocked, *fixed]], *after)
    return results[:count], results[count:]


def first_kernel(rate, ct, ql, state):
    for lanes in lane_blocks(ct.shape[1]):
        mode_state(rate[:, lanes], wide(ct, lanes) * wide(ql, lanes), False, state, lanes)


def filter_kernel(rate, res, own_three, long_spec, hold):
    block = hold.shape[0]
    for lanes in lane_blocks(rate.shape[1]):
        hold[:, lanes] = mode_sum(rate[:, lanes], res[:, lanes], 0.0, True, block)
    long_spec[...] = dft_full(own_three[...], hold[...]) * (1.0 / block)


def short_filter_kernel(taps, own_three, short_spec):
    short_spec[...] = dft_full(own_three[...], taps[...]) * (1.0 / taps.shape[0])


def product_kernel(ks, vs, short_in):
    short_in[...] = (wide(ks) * wide(vs)).astype(jnp.bfloat16)


def grad_local_kernel(ql, ct, long_spec, own_three, back, local_out):
    upstream = dft_full(own_three[...], wide(ct) * wide(ql))
    local_out[...] = dft_back(back[...], *times_conj(upstream, long_spec[...]))


def long_grad_kernel(local, state, rate, res, kl, qs, grad_out, back_out):
    block = local.shape[0]
    for lanes in lane_blocks(local.shape[1]):
        far = mode_sum(rate[:, lanes], res[:, lanes] * state[:, lanes], 1.0, False, block)
        grad = (local[:, lanes] + far).astype(jnp.bfloat16)
        grad_out[:, lanes] = grad
        hidden_grad = grad.astype(jnp.float32) * wide(kl, lanes)
        back_out[:, lanes] = (hidden_grad * wide(qs, lanes)).astype(jnp.bfloat16)


def short_kernel(si, halo, spec, qs, kl, rate, own_two, nxt_two, back, in_spec, mix_out, hidden_out, long_in, state_out):
    signal = dft_exact(own_two[...], si[...]) - dft_exact(nxt_two[...], halo[...])
    in_spec[...] = signal
    mix = dft_back(back[...], *times(signal, spec[...]))
    mix_out[...] = mix
    hidden = (wide(qs) * mix).astype(jnp.bfloat16)
    hidden_out[...] = hidden
    values = (wide(kl) * hidden.astype(jnp.float32)).astype(jnp.bfloat16)
    long_in[...] = values
    for lanes in lane_blocks(si.shape[1]):
        mode_state(rate[:, lanes], values[:, lanes].astype(jnp.float32), True, state_out, lanes)


def taps_kernel(sb, in_spec, own_two, back, sb_spec, part_out):
    spec = dft_exact(own_two[...], sb[...])
    sb_spec[...] = spec
    part = dft_back(back[...], *times_conj(spec, in_spec[...])) * (1.0 / sb.shape[0])
    part_out[...] = part.astype(jnp.bfloat16)


def input_grad_kernel(sb_next, sb_spec, spec, ks, vs, grad, kl, hidden, mix, nxt_two, back, key_out, value_out, gate_out, query_out, token):
    token[...] = jnp.zeros(token.shape, jnp.float32)
    slope = wide(grad)
    gate_out[...] = (slope * wide(hidden)).astype(jnp.bfloat16)
    query_out[...] = (slope * wide(kl) * mix[...]).astype(jnp.bfloat16)
    total = sb_spec[...] + dft_exact(nxt_two[...], sb_next[...])
    grad_in = dft_back(back[...], *times_conj(total, spec[...]))
    key_out[...] = (grad_in * wide(vs)).astype(jnp.bfloat16)
    value_out[...] = (grad_in * wide(ks)).astype(jnp.bfloat16)


def long_local_kernel(values, long_spec, own_two, back, mix_out):
    spec = dft_exact(own_two[...], values[...])
    mix_out[...] = dft_back(back[...], *times(spec, long_spec[...]))


def run(body, name, blocked, fixed, outs, width, scratch=(), after=()):
    channels = blocked[0].shape[1]
    n_in, n_fix, n_out = len(blocked), len(fixed), len(outs)
    leaves = [i for i, (_, _, place) in enumerate(outs) if place == "hbm"]
    count = channels // width

    def whole(*refs):
        ins, fix, refs = refs[:n_in], refs[n_in : n_in + n_fix], refs[n_in + n_fix + len(after) :]
        results, rest = list(refs[:n_out]), refs[n_out:]
        hold, staged = rest[: len(scratch)], rest[len(scratch) : len(scratch) + len(leaves)]
        copies = []
        for step in range(count):
            cut = pl.ds(step * width, width)
            there = [r.at[:, cut] for r in results]
            for slot, i in enumerate(leaves):
                there[i] = staged[slot].at[:, cut]
            body(*[r.at[:, cut] for r in ins], *fix, *there, *hold)
            for slot, i in enumerate(leaves):
                copy = pltpu.make_async_copy(there[i], results[i].at[:, cut], rest[-1].at[slot, step])
                copy.start()
                copies.append(copy)
        for copy in copies:
            copy.wait()

    places = {"hbm": pltpu.HBM, "vmem": pltpu.VMEM}
    scratch_shapes = [pltpu.VMEM((rows, width), dtype) for rows, dtype in scratch]
    scratch_shapes += [pltpu.VMEM((outs[i][0], channels), outs[i][1]) for i in leaves]
    if leaves:
        scratch_shapes.append(pltpu.SemaphoreType.DMA((len(leaves), count)))
    return pl.pallas_call(
        whole,
        in_specs=[pl.BlockSpec(memory_space=pltpu.VMEM)] * (n_in + n_fix)
        + [pl.BlockSpec(memory_space=pl.ANY)] * len(after),
        out_specs=[pl.BlockSpec(memory_space=places[place]) for _, _, place in outs],
        out_shape=[places[place]((rows, channels), dtype) for rows, dtype, place in outs],
        scratch_shapes=scratch_shapes,
        compiler_params=pltpu.CompilerParams(vmem_limit_bytes=VMEM_BYTES),
        cost_estimate=pl.CostEstimate(flops=0, bytes_accessed=1024, transcendentals=0),
        name=name,
    )(*[in_vmem(a) for a in [*blocked, *fixed]], *after)


def small(body, name, operands, outs, after=()):
    count, n_after = len(operands), len(after)
    return pl.pallas_call(
        lambda *refs: body(*refs[:count], *refs[count + n_after :]),
        in_specs=[pl.BlockSpec(memory_space=pltpu.VMEM)] * count + [pl.BlockSpec(memory_space=pl.ANY)] * n_after,
        out_specs=[pl.BlockSpec(memory_space=pltpu.VMEM)] * len(outs),
        out_shape=[pltpu.VMEM(shape, dtype) for shape, dtype in outs],
        compiler_params=pltpu.CompilerParams(vmem_limit_bytes=VMEM_BYTES),
        cost_estimate=pl.CostEstimate(flops=0, bytes_accessed=1024, transcendentals=0),
        name=name,
    )(*[in_vmem(a) for a in operands], *after)


def shifted(value, distance):
    size = lax.axis_size("ctx")
    pairs = [(i, i + distance) for i in range(size) if 0 <= i + distance < size]
    return lax.ppermute(value, "ctx", pairs)


def swapped(value, mask):
    size = lax.axis_size("ctx")
    return lax.ppermute(value, "ctx", [(i, i ^ mask) for i in range(size)])


def masks():
    size = lax.axis_size("ctx")
    return [1 << bit for bit in range(size.bit_length() - 1)]


def merge_states(total, other, got, rate, block, mask, last, after):
    def body(*refs):
        other, rate = refs[1][...], refs[2][...]
        me = lax.axis_index("ctx")
        takes = lax.rem(lax.div(me, mask), 2) == 0
        steps = mask - 1 - lax.rem(me, mask)
        taken = jnp.where(takes, jnp.exp((-block * steps).astype(jnp.float32) * rate) * other, 0.0)
        refs[-1][...] = taken if got is None else refs[3][...] + taken
        if not last:
            own = refs[0][...]
            fade = jnp.exp(-(block * mask) * rate)
            refs[-2][...] = jnp.where(takes, own + fade * other, other + fade * own)

    operands = [total, other, rate] + ([] if got is None else [got])
    outs = [(total.shape, jnp.float32)] * (1 if last else 2)
    merged = small(body, "merge", operands, outs, after)
    return (total, merged[0]) if last else merged


def pack(out, row, value):
    high, low = split(value)
    width = out.shape[1]
    rows = value.shape[0]
    for at in range(0, value.shape[1], width):
        out[row : row + rows, :] = high[:, at : at + width]
        out[row + rows : row + 2 * rows, :] = low[:, at : at + width]
        row += 2 * rows


def unpack(ref, row, rows, count):
    pieces = []
    for _ in range(count):
        high = ref[row : row + rows, :].astype(jnp.float32)
        pieces.append(high + ref[row + rows : row + 2 * rows, :].astype(jnp.float32))
        row += 2 * rows
    return jnp.concatenate(pieces, axis=1)


def taps_and_states(part, state, rate, beside, before):
    block, channels = part.shape
    modes = state.shape[0]
    half, quarter = channels // 2, channels // 4
    bf, f32 = jnp.bfloat16, jnp.float32

    def is_first():
        return lax.rem(lax.axis_index("ctx"), 2) == 0

    def mine_of(value):
        return jnp.where(is_first(), value[:, :half], value[:, half:])

    def apart(part, state, send, keep):
        first = is_first()
        low, high = part[:, :half], part[:, half:]
        send[:block, :] = jnp.where(first, high, low)
        keep[...] = jnp.where(first, low, high)
        pack(send, block, state[...])

    tall = (block + 4 * modes, half)
    send, keep = small(apart, "apart", [part, state], [(tall, bf), ((block, half), bf)])
    other = swapped(send, 1)

    def first_sum(keep, other, state, rate, left, right, total, near):
        for i, out in enumerate((left, right)):
            lanes = slice(i * quarter, (i + 1) * quarter)
            both = wide(keep, lanes) + other[:block, lanes].astype(f32)
            out[:block, :] = both.astype(bf)
        own, theirs = state[...], unpack(other, block, modes, 2)
        first = is_first()
        near[...] = jnp.where(first, 0.0, theirs)
        fade = jnp.exp(-block * rate[...])
        chip = mine_of(jnp.where(first, theirs + fade * own, own + fade * theirs))
        total[...] = chip
        pack(left, block, chip)

    wide_piece, piece = ((block + 4 * modes, quarter), bf), ((block, quarter), bf)
    states = ((modes, half), f32)
    left, right, total, near = small(
        first_sum, "first_sum", [keep, other, state, rate], [wide_piece, piece, states, (state.shape, f32)], before
    )
    rest = masks()[1:]
    orders = [rest, rest[1:] + rest[:1]]
    got = None
    for at, mask in enumerate(rest):
        left_other, right_other = swapped(left, orders[0][at]), swapped(right, orders[1][at])
        last = at == len(rest) - 1

        def step(*refs, mask=mask, start=got is None, last=last):
            left, right, left_other, right_other, total, rate = refs[:6]
            sums = [
                (mine[:block, :].astype(f32) + theirs[:block, :].astype(f32)).astype(bf)
                for mine, theirs in ((left, left_other), (right, right_other))
            ]
            me = lax.axis_index("ctx")
            takes = lax.rem(lax.div(me, mask), 2) == 1
            steps = lax.div(lax.rem(me, mask), 2) * 2
            pace = mine_of(rate)
            own, theirs = total[...], unpack(left_other, block, modes, 2)
            taken = jnp.where(takes, jnp.exp((-block * steps).astype(f32) * pace) * theirs, 0.0)
            reached = taken if start else refs[6][...] + taken
            if last:
                mine, got_out = refs[-2:]
                mine[:block, :quarter] = sums[0]
                mine[:block, quarter:] = sums[1]
                pack(mine, block, reached)
                got_out[...] = reached
            else:
                left_out, right_out, total_out, got_out = refs[-4:]
                left_out[:block, :] = sums[0]
                right_out[...] = sums[1]
                fade = jnp.exp(-(block * mask) * pace)
                merged = jnp.where(takes, own + fade * theirs, theirs + fade * own)
                total_out[...] = merged
                pack(left_out, block, merged)
                got_out[...] = reached

        operands = [left, right, left_other, right_other, total, rate] + ([] if got is None else [got])
        after = beside[at] if at < len(beside) else ()
        if last:
            mine, got = small(step, "last_sum", operands, [((block + 2 * modes, half), bf), states], after)
        else:
            left, right, total, got = small(step, "next_sum", operands, [wide_piece, piece, states, states], after)
    other = swapped(mine, 1)
    return mine, other, got, near


def tail(mine, other, got, near, local_mix, rate, res, ql, ct, width, scale):
    block, channels = local_mix.shape
    modes, half = got.shape
    bf, f32 = jnp.bfloat16, jnp.float32
    parts = channels // width

    def body(mine, other, got, near, local_mix, rate, res, ql, ct, core, gate, taps, core_at, gate_at, taps_at, weight, sems):
        first = lax.rem(lax.axis_index("ctx"), 2) == 0
        copies = []

        def leave(source, target, sem):
            copy = pltpu.make_async_copy(source, target, sem)
            copy.start()
            copies.append(copy)

        theirs = unpack(other, block, modes, 1)
        own = got[...]
        fade = jnp.where(first, 1.0, jnp.exp(-block * rate[...]))
        weight[:, :half] = jnp.where(first, own, theirs)
        weight[:, half:] = jnp.where(first, theirs, own)
        weight[...] = res[...] * (near[...] + fade * weight[...])
        taps_at[:, :half] = jnp.where(first, mine[:block, :], other[:block, :]).astype(f32) * scale
        leave(taps_at.at[:, pl.ds(0, half)], taps.at[:, pl.ds(0, half)], sems.at[2 * parts])
        taps_at[:, half:] = jnp.where(first, other[:block, :], mine[:block, :]).astype(f32) * scale
        leave(taps_at.at[:, pl.ds(half, half)], taps.at[:, pl.ds(half, half)], sems.at[2 * parts + 1])
        for k in range(parts):
            for lane in range(k * width, (k + 1) * width, LANES):
                lanes = slice(lane, lane + LANES)
                far = mode_sum(rate[:, lanes], weight[:, lanes], 1.0, True, block)
                mix = local_mix[:, lanes] + far
                core_at[:, lanes] = (wide(ql, lanes) * mix).astype(bf)
                gate_at[:, lanes] = (wide(ct, lanes) * mix).astype(bf)
            cut = pl.ds(k * width, width)
            leave(core_at.at[:, cut], core.at[:, cut], sems.at[k])
            leave(gate_at.at[:, cut], gate.at[:, cut], sems.at[parts + k])
        for copy in copies:
            copy.wait()

    operands = [mine, other, got, near, local_mix, rate, res, ql, ct]
    shape = (block, channels)
    return pl.pallas_call(
        body,
        in_specs=[pl.BlockSpec(memory_space=pltpu.VMEM)] * len(operands),
        out_specs=[pl.BlockSpec(memory_space=pltpu.HBM)] * 3,
        out_shape=[pltpu.HBM(shape, bf), pltpu.HBM(shape, bf), pltpu.HBM(shape, f32)],
        scratch_shapes=[
            pltpu.VMEM(shape, bf),
            pltpu.VMEM(shape, bf),
            pltpu.VMEM(shape, f32),
            pltpu.VMEM((modes, channels), f32),
            pltpu.SemaphoreType.DMA((2 * parts + 2,)),
        ],
        compiler_params=pltpu.CompilerParams(vmem_limit_bytes=VMEM_BYTES),
        cost_estimate=pl.CostEstimate(flops=0, bytes_accessed=1024, transcendentals=0),
        name="tail",
    )(*[in_vmem(a) for a in operands])


def local(
    query_short,
    key_short,
    value_short,
    short_taps,
    query_long,
    key_long,
    long_residue,
    long_rate,
    cotangent,
):
    block, channels = query_short.shape
    modes = long_rate.shape[0]
    sequence = block * lax.axis_size("ctx")
    half, full = jnp.bfloat16, jnp.float32
    matrices = [jnp.asarray(t) for t in tables(block)]
    width = min(512, channels)

    (rate, ct, ql, res, own_three, ks, vs), (total,) = load(
        [long_rate, cotangent, query_long, long_residue, matrices[1], key_short, value_short],
        [((modes, channels), full)],
        first_kernel,
        "first",
        3,
        width,
    )
    far, steps = None, masks()
    for at, mask in enumerate(steps):
        other = swapped(total, mask)
        beside = []
        if at == 1:
            (qs, kl, taps, own_two, nxt_two, back), (long_spec,) = load(
                [query_short, key_long, short_taps, matrices[0], matrices[2], matrices[3]],
                [((2 * block, channels), full)],
                filter_kernel,
                "filter",
                0,
                width,
                [total],
                [(block, full)],
                [rate, res],
                [own_three],
            )
            beside = [long_spec]
        if at == 2:
            (grad_local,) = run(
                grad_local_kernel,
                "grad_local",
                [ql, ct, long_spec],
                [own_three, back],
                [(block, full, "vmem")],
                width,
                (),
                [total],
            )
            beside = [grad_local]
        total, far = merge_states(total, other, far, rate, block, mask, at == len(steps) - 1, beside)
    (short_in,) = run(product_kernel, "product", [ks, vs], [], [(block, half, "vmem")], width, (), [far])
    halo = shifted(short_in, 1)
    (short_spec,) = run(
        short_filter_kernel, "short_filter", [taps], [own_three], [(2 * block, full, "vmem")], width, (), [far]
    )
    in_spec, short_mix, hidden, long_in, fore_state = run(
        short_kernel,
        "short",
        [short_in, halo, short_spec, qs, kl, rate],
        [own_two, nxt_two, back],
        [
            (2 * block, full, "vmem"),
            (block, full, "vmem"),
            (block, half, "vmem"),
            (block, half, "vmem"),
            (modes, full, "vmem"),
        ],
        width,
    )
    long_grad, short_back = run(
        long_grad_kernel,
        "long_grad",
        [grad_local, far, rate, res, kl, qs],
        [],
        [(block, half, "vmem"), (block, half, "vmem")],
        width,
    )
    sb_spec, part = run(
        taps_kernel,
        "taps",
        [short_back, in_spec],
        [own_two, back],
        [(2 * block, full, "vmem"), (block, half, "vmem")],
        width,
    )
    sb_next = shifted(short_back, -1)
    (local_mix,) = run(
        long_local_kernel,
        "long_local",
        [long_in, long_spec],
        [own_two, back],
        [(block, full, "vmem")],
        width,
    )
    key_short_grad, value_short_grad, key_long_grad, query_short_grad, token = run(
        input_grad_kernel,
        "input_grad",
        [sb_next, sb_spec, short_spec, ks, vs, long_grad, kl, hidden, short_mix],
        [nxt_two, back],
        [(block, half, "hbm")] * 4 + [(ROWS, full, "vmem")],
        width,
    )
    mine, other, got, near = taps_and_states(part, fore_state, rate, [[token], [local_mix]], [sb_next])
    core_output, query_long_grad, taps_grad = tail(
        mine, other, got, near, local_mix, rate, res, ql, ct, width, sequence ** (-0.5)
    )
    return (
        core_output,
        query_short_grad,
        key_short_grad,
        value_short_grad,
        query_long_grad,
        key_long_grad,
        taps_grad,
    )


def solution(mesh):
    tokens, shared = P("ctx", "ch"), P(None, "ch")
    return jax.shard_map(
        local,
        mesh=mesh,
        in_specs=(tokens, tokens, tokens, shared, tokens, tokens, shared, shared, tokens),
        out_specs=(tokens,) * 6 + (shared,),
        check_vma=False,
    )
```

time: 93 us -> 55 us (0.59)
  the two profiles are of different devices: /device:TPU:27 before, /device:TPU:0 now
where the time goes in v2:
time: 55 us; the launch traced here: 54.8 us
  Pallas kernels  24.2 us (44%)
  starting transfers between devices  20.2 us (37%)
  waiting for transfers between devices  9.41 us (17%)
  between operations  0.94 us (2%)
    ppermute x9, starting transfers between devices, swapped(): return lax.ppermute(value, 'ctx', [(i, i ^ mask) for i in range(size)])  17.4 us
    pallas_call x8, Pallas kernels, run(): pl.pallas_call(whole, in_specs=[pl.BlockSpec(memory_space=pltpu.VMEM)] *...  14.9 us
    ppermute x9, waiting for transfers between devices, swapped(): return lax.ppermute(value, 'ctx', [(i, i ^ mask) for i in range(size)])  9.4 us
    pallas_call x2, Pallas kernels, load(): pl.pallas_call(whole, in_specs=[pl.BlockSpec(memory_space=pltpu.HBM)] * c...  6.26 us
    ppermute x2, starting transfers between devices, shifted(): return lax.ppermute(value, 'ctx', pairs)  2.8 us
    pallas_call x1, Pallas kernels, tail(): pl.pallas_call(body, in_specs=[pl.BlockSpec(memory_space=pltpu.VMEM)] * l...  2.48 us
  transfers between devices with their start and end apart: 11, of which 7 were waited for; matrix products, arithmetic and copies ran while one was open for 0% of the time, Pallas kernels for 33%

profile of v2, /device:TPU:0, one launch (start us, length us, event | category | flops | bytes accessed | tf_op | source)
XLA Modules:
  0.0 54.8 jit_solution(3610307932188718779)
XLA Ops:
  0.6 2.8 %first.1 = (f32[16,2048]{1,0:T(8,128)S(1)}, bf16[128,2048]{1,0:T(8,128)(2,1)S(1)}, bf16[128,2048]{1,0:T(8,128)(2,1)S(1)}, f32[16,2048]{1,0:T(8,128)S(1)}, bf16[2...) custom-call(f32[16,2048]{1,0:T(8,128)} %refs_0_.2, ...), custom_call_target="tpu_custom_call" | custom-call | bytes 1024 | tf_op jit(solution)/shard_map/first/pallas_call | solution.py:181
  4.0 1.0 %collective-permute-done.refs_1_ = f32[16,2048]{1,0:T(8,128)S(1)} collective-permute-done((f32[16,2048]{1,0:T(8,128)S(1)}, f32[16,2048]{1,0:T(8,128)S(1)}, u32[]{:S(2)}, u32[]{:S(2)}) %collective-permute-start) | collective-permute-done | bytes 131104 | tf_op jit(solution)/shard_map/ppermute | solution.py:331
  5.0 2.9 %collective-permute-start.1 = (f32[16,2048]{1,0:T(8,128)S(1)}, f32[16,2048]{1,0:T(8,128)S(1)}, u32[]{:S(2)}, u32[]{:S(2)}) collective-permute-start(f32[16,2048]{1,0:T(8,128)S(1)} %get-tuple-element.61.refs_9_.refs_0_), channel_id=1, source_target_pairs={{0,8},{4,12},{8,0},{12,4},{16,24},{20,28},{24,16},{28,20},{1,9},{5... | collective-permute-start | bytes 393224 | tf_op jit(solution)/shard_map/ppermute | solution.py:331
  7.9 3.4 %filter.1 = (bf16[128,2048]{1,0:T(8,128)(2,1)S(1)}, bf16[128,2048]{1,0:T(8,128)(2,1)S(1)}, f32[128,2048]{1,0:T(8,128)S(1)}, bf16[256,256]{1,0:T(8,128)(2,1)S(1)}...) custom-call(bf16[128,2048]{1,0:T(8,128)(2,1)} %refs_0_.3, ...), custom_call_target="tpu_custom_call" | custom-call | bytes 1024 | tf_op jit(solution)/shard_map/filter/pallas_call | solution.py:181
  11.8 1.8 %collective-permute-start.2 = (f32[16,2048]{1,0:T(8,128)S(1)}, f32[16,2048]{1,0:T(8,128)S(1)}, u32[]{:S(2)}, u32[]{:S(2)}) collective-permute-start(f32[16,2048]{1,0:T(8,128)S(1)} %get-tuple-element.65.refs_5_.refs_0_), channel_id=1, source_target_pairs={{0,16},{4,20},{8,24},{12,28},{16,0},{20,4},{24,8},{28,12},{1,17},{... | collective-permute-start | bytes 393224 | tf_op jit(solution)/shard_map/ppermute | solution.py:331
  13.7 2.0 %grad_local.1.refs_4_.refs_0_ = f32[128,2048]{1,0:T(8,128)S(1)} custom-call(bf16[128,2048]{1,0:T(8,128)(2,1)S(1)} %get-tuple-element.55.refs_0_.ql, bf16[128,2048]{1,0:T(8,128)(2,1)S(1)} %get-tuple-element.56.refs_1_.ct, f32[256,2048]{1,0:T(8,128)S(1)} %get-tuple-element.62.refs_4_.refs_2_.refs_1_, ...), custom_call_target="tpu_custom_call" | custom-call | bytes 1024 | tf_op jit(solution)/shard_map/grad_local/pallas_call | solution.py:297
  15.7 1.3 %collective-permute-done.2.refs_1_ = f32[16,2048]{1,0:T(8,128)S(1)} collective-permute-done((f32[16,2048]{1,0:T(8,128)S(1)}, f32[16,2048]{1,0:T(8,128)S(1)}, u32[]{:S(2)}, u32[]{:S(2)}) %collective-permute-start.2) | collective-permute-done | bytes 131104 | tf_op jit(solution)/shard_map/ppermute | solution.py:331
  17.1 1.3 %collective-permute-start.3 = (bf16[128,2048]{1,0:T(8,128)(2,1)S(1)}, bf16[128,2048]{1,0:T(8,128)(2,1)S(1)}, u32[]{:S(2)}, u32[]{:S(2)}) collective-permute-start(bf16[128,2048]{1,0:T(8,128)(2,1)S(1)} %product.1.refs_0_), channel_id=1, source_target_pairs={{0,4},{4,8},{8,12},{12,16},{16,20},{20,24},{24,28},{1,5},{5,9},{9,... | collective-permute-start | bytes 1572872 | tf_op jit(solution)/shard_map/ppermute | solution.py:326
  18.4 2.2 %long_grad.1 = (bf16[128,2048]{1,0:T(8,128)(2,1)S(1)}, bf16[128,2048]{1,0:T(8,128)(2,1)S(1)}) custom-call(f32[128,2048]{1,0:T(8,128)S(1)} %grad_local.1.refs_4_.refs_0_, f32[16,2048]{1,0:T(8,128)S(1)} %merge.5.refs_1_.refs_2_, f32[16,2048]{1,0:T(8,128)S(1)} %get-tuple-element.57.refs_2_.refs_6_.refs_5_.refs_3_.rate, ...), custom_call_target="tpu_custom_call" | custom-call | bytes 1024 | tf_op jit(solution)/shard_map/long_grad/pallas_call | solution.py:297
  20.6 1.5 %collective-permute-start.5 = (bf16[128,2048]{1,0:T(8,128)(2,1)S(1)}, bf16[128,2048]{1,0:T(8,128)(2,1)S(1)}, u32[]{:S(2)}, u32[]{:S(2)}) collective-permute-start(bf16[128,2048]{1,0:T(8,128)(2,1)S(1)} %get-tuple-element.69.refs_0_), channel_id=1, source_target_pairs={{4,0},{8,4},{12,8},{16,12},{20,16},{24,20},{28,24},{5,1},{9,5},{13... | collective-permute-start | bytes 1572872 | tf_op jit(solution)/shard_map/ppermute | solution.py:326
  22.1 0.7 %short_filter.1.refs_2_ = f32[256,2048]{1,0:T(8,128)S(1)} custom-call(f32[128,2048]{1,0:T(8,128)S(1)} %get-tuple-element.72.refs_0_, bf16[256,384]{1,0:T(8,128)(2,1)S(1)} %get-tuple-element.59.refs_8_.refs_3_.refs_1_, f32[16,2048]{1,0:T(8,128)S(1)} %merge.5.refs_1_.refs_2_), custom_call_target="tpu_custom_call" | custom-call | bytes 1024 | tf_op jit(solution)/shard_map/short_filter/pallas_call | solution.py:297
  22.8 3.6 %short.1 = (f32[256,2048]{1,0:T(8,128)S(1)}, f32[128,2048]{1,0:T(8,128)S(1)}, bf16[128,2048]{1,0:T(8,128)(2,1)S(1)}, bf16[128,2048]{1,0:T(8,128)(2,1)S(1)}, f32[16,2048]{1,0:T(8,128)S(1)}) custom-call(bf16[128,2048]{1,0:T(8,128)(2,1)S(1)} %product.1.refs_0_, bf16[128,2048]{1,0:T(8,128)(2,1)S(1)} %collective-permute-done.3.refs_1_, ...), custom_call_target="tpu_custom_call" | custom-call | bytes 1024 | tf_op jit(solution)/shard_map/short/pallas_call | solution.py:297
  26.4 1.7 %taps.1 = (f32[256,2048]{1,0:T(8,128)S(1)}, bf16[128,2048]{1,0:T(8,128)(2,1)S(1)}) custom-call(bf16[128,2048]{1,0:T(8,128)(2,1)S(1)} %get-tuple-element.69.refs_0_, f32[256,2048]{1,0:T(8,128)S(1)} %get-tuple-element.75.refs_1_, bf16[256,256]{1,0:T(8,128)(2,1)S(1)} %get-tuple-element.73.refs_6_.refs_2_, ...), custom_call_target="tpu_custom_call" | custom-call | bytes 1024 | tf_op jit(solution)/shard_map/taps/pallas_call | solution.py:297
  28.2 4.1 %collective-permute-start.4 = (bf16[192,1024]{1,0:T(8,128)(2,1)S(1)}, bf16[192,1024]{1,0:T(8,128)(2,1)S(1)}, u32[]{:S(2)}, u32[]{:S(2)}) collective-permute-start(bf16[192,1024]{1,0:T(8,128)(2,1)S(1)} %get-tuple-element.79), channel_id=1, source_target_pairs={{0,4},{4,0},{8,12},{12,8},{16,20},{20,16},{24,28},{28,24},{1,5},{5... | collective-permute-start | bytes 1179656 | tf_op jit(solution)/shard_map/ppermute | solution.py:331
  32.4 1.3 %collective-permute-done.4.refs_1_ = bf16[192,1024]{1,0:T(8,128)(2,1)S(1)} collective-permute-done((bf16[192,1024]{1,0:T(8,128)(2,1)S(1)}, bf16[192,1024]{1,0:T(8,128)(2,1)S(1)}, u32[]{:S(2)}, u32[]{:S(2)}) %collective-permute-start.4) | collective-permute-done | bytes 393248 | tf_op jit(solution)/shard_map/ppermute | solution.py:331
  33.9 2.8 %collective-permute-start.6 = (bf16[192,512]{1,0:T(8,128)(2,1)S(1)}, bf16[192,512]{1,0:T(8,128)(2,1)S(1)}, u32[]{:S(2)}, u32[]{:S(2)}) collective-permute-start(bf16[192,512]{1,0:T(8,128)(2,1)S(1)} %get-tuple-element.80.refs_0_), channel_id=1, source_target_pairs={{0,8},{4,12},{8,0},{12,4},{16,24},{20,28},{24,16},{28,20},{1,9},{5... | collective-permute-start | bytes 589832 | tf_op jit(solution)/shard_map/ppermute | solution.py:331
  36.7 1.6 %collective-permute-start.7 = (bf16[128,512]{1,0:T(8,128)(2,1)S(1)}, bf16[128,512]{1,0:T(8,128)(2,1)S(1)}, u32[]{:S(2)}, u32[]{:S(2)}) collective-permute-start(bf16[128,512]{1,0:T(8,128)(2,1)S(1)} %get-tuple-element.81.refs_1_), channel_id=1, source_target_pairs={{0,16},{4,20},{8,24},{12,28},{16,0},{20,4},{24,8},{28,12},{1,17},{... | collective-permute-start | bytes 393224 | tf_op jit(solution)/shard_map/ppermute | solution.py:331
  38.3 2.9 %input_grad.1 = (bf16[128,2048]{1,0:T(8,128)(2,1)}, bf16[128,2048]{1,0:T(8,128)(2,1)}, bf16[128,2048]{1,0:T(8,128)(2,1)}, bf16[128,2048]{1,0:T(8,128)(2,1)}, f32[8,2048]{1,0:T(8,128)S(1)}) custom-call(bf16[128,2048]{1,0:T(8,128)(2,1)S(1)} %collective-permute-done.5.refs_4_.refs_0_, f32[256,2048]{1,0:T(8,128)S(1)} %get-tuple-element.83.refs_1_, ...), custom_call_target="tpu_custom_call" | custom-call | bytes 1024 | tf_op jit(solution)/shard_map/input_grad/pallas_call | solution.py:297
  41.2 0.9 %collective-permute-done.7.refs_3_ = bf16[128,512]{1,0:T(8,128)(2,1)S(1)} collective-permute-done((bf16[128,512]{1,0:T(8,128)(2,1)S(1)}, bf16[128,512]{1,0:T(8,128)(2,1)S(1)}, u32[]{:S(2)}, u32[]{:S(2)}) %collective-permute-start.7) | collective-permute-done | bytes 131104 | tf_op jit(solution)/shard_map/ppermute | solution.py:331
  42.2 3.1 %collective-permute-start.8 = (bf16[192,512]{1,0:T(8,128)(2,1)S(1)}, bf16[192,512]{1,0:T(8,128)(2,1)S(1)}, u32[]{:S(2)}, u32[]{:S(2)}) collective-permute-start(bf16[192,512]{1,0:T(8,128)(2,1)S(1)} %get-tuple-element.88.refs_0_), channel_id=1, source_target_pairs={{0,16},{4,20},{8,24},{12,28},{16,0},{20,4},{24,8},{28,12},{1,17},{... | collective-permute-start | bytes 589832 | tf_op jit(solution)/shard_map/ppermute | solution.py:331
  45.7 1.7 %long_local.1.refs_7_.local_mix = f32[128,2048]{1,0:T(8,128)S(1)} custom-call(bf16[128,2048]{1,0:T(8,128)(2,1)S(1)} %get-tuple-element.92.refs_0_, f32[256,2048]{1,0:T(8,128)S(1)} %get-tuple-element.62.refs_4_.refs_2_.refs_1_, bf16[256,256]{1,0:T(8,128)(2,1)S(1)} %get-tuple-element.73.refs_6_.refs_2_, ...), custom_call_target="tpu_custom_call" | custom-call | bytes 1024 | tf_op jit(solution)/shard_map/long_local/pallas_call | solution.py:297
  47.4 2.9 %collective-permute-done.9.refs_3_ = bf16[128,512]{1,0:T(8,128)(2,1)S(1)} collective-permute-done((bf16[128,512]{1,0:T(8,128)(2,1)S(1)}, bf16[128,512]{1,0:T(8,128)(2,1)S(1)}, u32[]{:S(2)}, u32[]{:S(2)}) %collective-permute-start.9) | collective-permute-done | bytes 131104 | tf_op jit(solution)/shard_map/ppermute | solution.py:331
  50.5 1.6 %collective-permute-done.10.other = bf16[160,1024]{1,0:T(8,128)(2,1)S(1)} collective-permute-done((bf16[160,1024]{1,0:T(8,128)(2,1)S(1)}, bf16[160,1024]{1,0:T(8,128)(2,1)S(1)}, u32[]{:S(2)}, u32[]{:S(2)}) %collective-permute-start.10) | collective-permute-done | bytes 327712 | tf_op jit(solution)/shard_map/ppermute | solution.py:331
  52.1 2.5 %tail.1 = (bf16[128,2048]{1,0:T(8,128)(2,1)}, bf16[128,2048]{1,0:T(8,128)(2,1)}, f32[128,2048]{1,0:T(8,128)}) custom-call(bf16[160,1024]{1,0:T(8,128)(2,1)S(1)} %get-tuple-element.93.mine, bf16[160,1024]{1,0:T(8,128)(2,1)S(1)} %collective-permute-done.10.other, f32[16,1024]{1,0:T(8,128)S(1)} %get-tuple-element.94.got, ...), custom_call_target="tpu_custom_call" | custom-call | bytes 1024 | tf_op jit(solution)/shard_map/tail/pallas_call | solution.py:504
  (16 shorter events, 2.0 us)
Async XLA Ops:
  3.5 1.5 %collective-permute-start = (f32[16,2048]{1,0:T(8,128)S(1)}, f32[16,2048]{1,0:T(8,128)S(1)}, u32[]{:S(2)}, u32[]{:S(2)}) collective-permute-start(f32[16,2048]{1,0:T(8,128)S(1)} %get-tuple-element.60.refs_0_), channel_id=1, source_target_pairs={{0,4},{4,0},{8,12},{12,8},{16,20},{20,16},{24,28},{28,24},{1,5},{5... | collective-permute-start | bytes 393224 | tf_op jit(solution)/shard_map/ppermute | solution.py:331
  5.0 6.7 %collective-permute-start.1 = (f32[16,2048]{1,0:T(8,128)S(1)}, f32[16,2048]{1,0:T(8,128)S(1)}, u32[]{:S(2)}, u32[]{:S(2)}) collective-permute-start(f32[16,2048]{1,0:T(8,128)S(1)} %get-tuple-element.61.refs_9_.refs_0_), channel_id=1, source_target_pairs={{0,8},{4,12},{8,0},{12,4},{16,24},{20,28},{24,16},{28,20},{1,9},{5... | collective-permute-start | bytes 393224 | tf_op jit(solution)/shard_map/ppermute | solution.py:331
  11.8 5.1 %collective-permute-start.2 = (f32[16,2048]{1,0:T(8,128)S(1)}, f32[16,2048]{1,0:T(8,128)S(1)}, u32[]{:S(2)}, u32[]{:S(2)}) collective-permute-start(f32[16,2048]{1,0:T(8,128)S(1)} %get-tuple-element.65.refs_5_.refs_0_), channel_id=1, source_target_pairs={{0,16},{4,20},{8,24},{12,28},{16,0},{20,4},{24,8},{28,12},{1,17},{... | collective-permute-start | bytes 393224 | tf_op jit(solution)/shard_map/ppermute | solution.py:331
  17.1 5.7 %collective-permute-start.3 = (bf16[128,2048]{1,0:T(8,128)(2,1)S(1)}, bf16[128,2048]{1,0:T(8,128)(2,1)S(1)}, u32[]{:S(2)}, u32[]{:S(2)}) collective-permute-start(bf16[128,2048]{1,0:T(8,128)(2,1)S(1)} %product.1.refs_0_), channel_id=1, source_target_pairs={{0,4},{4,8},{8,12},{12,16},{16,20},{20,24},{24,28},{1,5},{5,9},{9,... | collective-permute-start | bytes 1572872 | tf_op jit(solution)/shard_map/ppermute | solution.py:326
  20.6 11.8 %collective-permute-start.5 = (bf16[128,2048]{1,0:T(8,128)(2,1)S(1)}, bf16[128,2048]{1,0:T(8,128)(2,1)S(1)}, u32[]{:S(2)}, u32[]{:S(2)}) collective-permute-start(bf16[128,2048]{1,0:T(8,128)(2,1)S(1)} %get-tuple-element.69.refs_0_), channel_id=1, source_target_pairs={{4,0},{8,4},{12,8},{16,12},{20,16},{24,20},{28,24},{5,1},{9,5},{13... | collective-permute-start | bytes 1572872 | tf_op jit(solution)/shard_map/ppermute | solution.py:326
  28.2 5.5 %collective-permute-start.4 = (bf16[192,1024]{1,0:T(8,128)(2,1)S(1)}, bf16[192,1024]{1,0:T(8,128)(2,1)S(1)}, u32[]{:S(2)}, u32[]{:S(2)}) collective-permute-start(bf16[192,1024]{1,0:T(8,128)(2,1)S(1)} %get-tuple-element.79), channel_id=1, source_target_pairs={{0,4},{4,0},{8,12},{12,8},{16,20},{20,16},{24,28},{28,24},{1,5},{5... | collective-permute-start | bytes 1179656 | tf_op jit(solution)/shard_map/ppermute | solution.py:331
  33.9 8.2 %collective-permute-start.6 = (bf16[192,512]{1,0:T(8,128)(2,1)S(1)}, bf16[192,512]{1,0:T(8,128)(2,1)S(1)}, u32[]{:S(2)}, u32[]{:S(2)}) collective-permute-start(bf16[192,512]{1,0:T(8,128)(2,1)S(1)} %get-tuple-element.80.refs_0_), channel_id=1, source_target_pairs={{0,8},{4,12},{8,0},{12,4},{16,24},{20,28},{24,16},{28,20},{1,9},{5... | collective-permute-start | bytes 589832 | tf_op jit(solution)/shard_map/ppermute | solution.py:331
  36.7 5.4 %collective-permute-start.7 = (bf16[128,512]{1,0:T(8,128)(2,1)S(1)}, bf16[128,512]{1,0:T(8,128)(2,1)S(1)}, u32[]{:S(2)}, u32[]{:S(2)}) collective-permute-start(bf16[128,512]{1,0:T(8,128)(2,1)S(1)} %get-tuple-element.81.refs_1_), channel_id=1, source_target_pairs={{0,16},{4,20},{8,24},{12,28},{16,0},{20,4},{24,8},{28,12},{1,17},{... | collective-permute-start | bytes 393224 | tf_op jit(solution)/shard_map/ppermute | solution.py:331
  42.2 8.1 %collective-permute-start.8 = (bf16[192,512]{1,0:T(8,128)(2,1)S(1)}, bf16[192,512]{1,0:T(8,128)(2,1)S(1)}, u32[]{:S(2)}, u32[]{:S(2)}) collective-permute-start(bf16[192,512]{1,0:T(8,128)(2,1)S(1)} %get-tuple-element.88.refs_0_), channel_id=1, source_target_pairs={{0,16},{4,20},{8,24},{12,28},{16,0},{20,4},{24,8},{28,12},{1,17},{... | collective-permute-start | bytes 589832 | tf_op jit(solution)/shard_map/ppermute | solution.py:331
  45.3 5.0 %collective-permute-start.9 = (bf16[128,512]{1,0:T(8,128)(2,1)S(1)}, bf16[128,512]{1,0:T(8,128)(2,1)S(1)}, u32[]{:S(2)}, u32[]{:S(2)}) collective-permute-start(bf16[128,512]{1,0:T(8,128)(2,1)S(1)} %get-tuple-element.89.refs_1_), channel_id=1, source_target_pairs={{0,8},{4,12},{8,0},{12,4},{16,24},{20,28},{24,16},{28,20},{1,9},{5... | collective-permute-start | bytes 393224 | tf_op jit(solution)/shard_map/ppermute | solution.py:331
  50.4 1.7 %collective-permute-start.10 = (bf16[160,1024]{1,0:T(8,128)(2,1)S(1)}, bf16[160,1024]{1,0:T(8,128)(2,1)S(1)}, u32[]{:S(2)}, u32[]{:S(2)}) collective-permute-start(bf16[160,1024]{1,0:T(8,128)(2,1)S(1)} %get-tuple-element.93.mine), channel_id=1, source_target_pairs={{0,4},{4,0},{8,12},{12,8},{16,20},{20,16},{24,28},{28,24},{1,5},{5... | collective-permute-start | bytes 983048 | tf_op jit(solution)/shard_map/ppermute | solution.py:331

commit v3 on v2

--- a/solution.py
+++ b/solution.py
@@ -142,9 +142,9 @@
 
 def load(brought, outs, body, name, first, width, after=(), scratch=(), blocked=(), fixed=()):
     count, n_after, ready = len(brought), len(after), len(blocked) + len(fixed)
-    channels = brought[0].shape[1]
+    channels = outs[0][0][1]
     parts = channels // width
-    pieces = [parts] * first + [1] * (count - first)
+    pieces = [parts if i < first or a.shape[1] == channels else 1 for i, a in enumerate(brought)]
     offsets = [sum(pieces[:i]) for i in range(count)]
 
     def whole(*refs):
@@ -165,7 +165,8 @@
             for row in copies[:first]:
                 row[k].start()
         for row in copies[first:]:
-            row[0].start()
+            for copy in row:
+                copy.start()
         for k in range(parts):
             for row in copies[:first]:
                 row[k].wait()
@@ -174,7 +175,8 @@
             there = [r.at[:, cut] for r in more[: len(outs)]]
             body(*[r.at[:, cut] for r in [*results[:first], *ins]], *fix, *there, *held)
         for row in copies[first:]:
-            row[0].wait()
+            for copy in row:
+                copy.wait()
 
     out_shape = [pltpu.VMEM(a.shape, a.dtype) for a in brought]
     out_shape += [pltpu.VMEM(shape, dtype) for shape, dtype in outs]
@@ -206,8 +208,9 @@
     long_spec[...] = dft_full(own_three[...], hold[...]) * (1.0 / block)
 
 
-def short_filter_kernel(taps, own_three, short_spec):
+def short_filter_kernel(taps, si, own_three, own_two, short_spec, own_spec):
     short_spec[...] = dft_full(own_three[...], taps[...]) * (1.0 / taps.shape[0])
+    own_spec[...] = dft_exact(own_two[...], si[...])
 
 
 def product_kernel(ks, vs, short_in):
@@ -229,8 +232,8 @@
         back_out[:, lanes] = (hidden_grad * wide(qs, lanes)).astype(jnp.bfloat16)
 
 
-def short_kernel(si, halo, spec, qs, kl, rate, own_two, nxt_two, back, in_spec, mix_out, hidden_out, long_in, state_out):
-    signal = dft_exact(own_two[...], si[...]) - dft_exact(nxt_two[...], halo[...])
+def short_kernel(own_spec, halo, spec, qs, kl, rate, nxt_two, back, in_spec, mix_out, hidden_out, long_in, state_out):
+    signal = own_spec[...] - dft_exact(nxt_two[...], halo[...])
     in_spec[...] = signal
     mix = dft_back(back[...], *times(signal, spec[...]))
     mix_out[...] = mix
@@ -238,7 +241,7 @@
     hidden_out[...] = hidden
     values = (wide(kl) * hidden.astype(jnp.float32)).astype(jnp.bfloat16)
     long_in[...] = values
-    for lanes in lane_blocks(si.shape[1]):
+    for lanes in lane_blocks(halo.shape[1]):
         mode_state(rate[:, lanes], values[:, lanes].astype(jnp.float32), True, state_out, lanes)
 
 
@@ -357,19 +360,20 @@
 
 def pack(out, row, value):
     high, low = split(value)
-    width = out.shape[1]
-    rows = value.shape[0]
-    for at in range(0, value.shape[1], width):
-        out[row : row + rows, :] = high[:, at : at + width]
-        out[row + rows : row + 2 * rows, :] = low[:, at : at + width]
+    rows, channels = value.shape
+    for at in range(0, channels, out.shape[1]):
+        here = min(out.shape[1], channels - at)
+        out[row : row + rows, :here] = high[:, at : at + here]
+        out[row + rows : row + 2 * rows, :here] = low[:, at : at + here]
         row += 2 * rows
 
 
-def unpack(ref, row, rows, count):
+def unpack(ref, row, rows, channels):
     pieces = []
-    for _ in range(count):
-        high = ref[row : row + rows, :].astype(jnp.float32)
-        pieces.append(high + ref[row + rows : row + 2 * rows, :].astype(jnp.float32))
+    for at in range(0, channels, ref.shape[1]):
+        here = min(ref.shape[1], channels - at)
+        high = ref[row : row + rows, :here].astype(jnp.float32)
+        pieces.append(high + ref[row + rows : row + 2 * rows, :here].astype(jnp.float32))
         row += 2 * rows
     return jnp.concatenate(pieces, axis=1)
 
@@ -377,17 +381,18 @@
 def taps_and_states(part, state, rate, beside, before):
     block, channels = part.shape
     modes = state.shape[0]
-    half, quarter = channels // 2, channels // 4
+    half = channels // 2
+    cut = half * 3 // 8 // LANES * LANES
     bf, f32 = jnp.bfloat16, jnp.float32
 
-    def is_first():
-        return lax.rem(lax.axis_index("ctx"), 2) == 0
-
     def mine_of(value):
-        return jnp.where(is_first(), value[:, :half], value[:, half:])
+        return jnp.where(lax.rem(lax.axis_index("ctx"), 2) == 0, value[:, :half], value[:, half:])
+
+    def sum_of(mine, theirs):
+        return (mine[:block, :].astype(f32) + theirs[:block, :].astype(f32)).astype(bf)
 
     def apart(part, state, send, keep):
-        first = is_first()
+        first = lax.rem(lax.axis_index("ctx"), 2) == 0
         low, high = part[:, :half], part[:, half:]
         send[:block, :] = jnp.where(first, high, low)
         keep[...] = jnp.where(first, low, high)
@@ -398,77 +403,90 @@
     other = swapped(send, 1)
 
     def first_sum(keep, other, state, rate, left, right, total, near):
-        for i, out in enumerate((left, right)):
-            lanes = slice(i * quarter, (i + 1) * quarter)
-            both = wide(keep, lanes) + other[:block, lanes].astype(f32)
-            out[:block, :] = both.astype(bf)
-        own, theirs = state[...], unpack(other, block, modes, 2)
-        first = is_first()
+        both = sum_of(keep, other)
+        left[:block, :] = both[:, :cut]
+        right[...] = both[:, cut:]
+        own, theirs = state[...], unpack(other, block, modes, channels)
+        first = lax.rem(lax.axis_index("ctx"), 2) == 0
         near[...] = jnp.where(first, 0.0, theirs)
         fade = jnp.exp(-block * rate[...])
         chip = mine_of(jnp.where(first, theirs + fade * own, own + fade * theirs))
         total[...] = chip
         pack(left, block, chip)
 
-    wide_piece, piece = ((block + 4 * modes, quarter), bf), ((block, quarter), bf)
-    states = ((modes, half), f32)
+    lefts = ((block + 2 * modes * -(-half // cut), cut), bf)
+    rights, states = ((block, half - cut), bf), ((modes, half), f32)
     left, right, total, near = small(
-        first_sum, "first_sum", [keep, other, state, rate], [wide_piece, piece, states, (state.shape, f32)], before
+        first_sum, "first_sum", [keep, other, state, rate], [lefts, rights, states, (state.shape, f32)], before
     )
     rest = masks()[1:]
-    orders = [rest, rest[1:] + rest[:1]]
     got = None
     for at, mask in enumerate(rest):
-        left_other, right_other = swapped(left, orders[0][at]), swapped(right, orders[1][at])
+        left_other, right_other = swapped(left, mask), swapped(right, rest[(at + 1) % len(rest)])
         last = at == len(rest) - 1
 
-        def step(*refs, mask=mask, start=got is None, last=last):
-            left, right, left_other, right_other, total, rate = refs[:6]
-            sums = [
-                (mine[:block, :].astype(f32) + theirs[:block, :].astype(f32)).astype(bf)
-                for mine, theirs in ((left, left_other), (right, right_other))
-            ]
+        def reach(total, other, rate, got, mask):
             me = lax.axis_index("ctx")
             takes = lax.rem(lax.div(me, mask), 2) == 1
             steps = lax.div(lax.rem(me, mask), 2) * 2
             pace = mine_of(rate)
-            own, theirs = total[...], unpack(left_other, block, modes, 2)
+            theirs = unpack(other, block, modes, half)
             taken = jnp.where(takes, jnp.exp((-block * steps).astype(f32) * pace) * theirs, 0.0)
-            reached = taken if start else refs[6][...] + taken
-            if last:
-                mine, got_out = refs[-2:]
-                mine[:block, :quarter] = sums[0]
-                mine[:block, quarter:] = sums[1]
-                pack(mine, block, reached)
-                got_out[...] = reached
-            else:
-                left_out, right_out, total_out, got_out = refs[-4:]
-                left_out[:block, :] = sums[0]
-                right_out[...] = sums[1]
-                fade = jnp.exp(-(block * mask) * pace)
-                merged = jnp.where(takes, own + fade * theirs, theirs + fade * own)
-                total_out[...] = merged
-                pack(left_out, block, merged)
-                got_out[...] = reached
-
-        operands = [left, right, left_other, right_other, total, rate] + ([] if got is None else [got])
+            reached = taken if got is None else got[...] + taken
+            own, fade = total[...], jnp.exp(-(block * mask) * pace)
+            return reached, jnp.where(takes, own + fade * theirs, theirs + fade * own)
+
+        before_got = () if got is None else (got,)
         after = beside[at] if at < len(beside) else ()
         if last:
-            mine, got = small(step, "last_sum", operands, [((block + 2 * modes, half), bf), states], after)
+
+            def finish(left, left_other, right, right_other, total, rate, *refs, mask=mask):
+                mine, got_out = refs[-2:]
+                mine[:block, :cut] = sum_of(left, left_other)
+                mine[:block, cut:] = sum_of(right, right_other)
+                reached, _ = reach(total, left_other, rate, refs[0] if len(refs) > 2 else None, mask)
+                got_out[...] = reached
+                pack(mine, block, reached)
+
+            operands = [left, left_other, right, right_other, total, rate, *before_got]
+            mine, got = small(finish, "last_sum", operands, [((block + 2 * modes, half), bf), states], after)
         else:
-            left, right, total, got = small(step, "next_sum", operands, [wide_piece, piece, states, states], after)
-    other = swapped(mine, 1)
-    return mine, other, got, near
-
-
-def tail(mine, other, got, near, local_mix, rate, res, ql, ct, width, scale):
+
+            def go_left(left, left_other, total, rate, *refs, mask=mask):
+                out, total_out, got_out = refs[-3:]
+                out[:block, :] = sum_of(left, left_other)
+                reached, merged = reach(total, left_other, rate, refs[0] if len(refs) > 3 else None, mask)
+                got_out[...] = reached
+                total_out[...] = merged
+                pack(out, block, merged)
+
+            def go_right(right, right_other, out):
+                out[...] = sum_of(right, right_other)
+
+            left, total, got = small(
+                go_left, "go_left", [left, left_other, total, rate, *before_got], [lefts, states, states], after
+            )
+            (right,) = small(go_right, "go_right", [right, right_other], [rights])
+    return mine, got, near
+
+
+def gated(own, name, got, near, local_mix, rate, res, ql, ct, width, scale=None, mine=None, outputs=()):
     block, channels = local_mix.shape
-    modes, half = got.shape
+    modes, half = near.shape[0], channels // 2
     bf, f32 = jnp.bfloat16, jnp.float32
-    parts = channels // width
-
-    def body(mine, other, got, near, local_mix, rate, res, ql, ct, core, gate, taps, core_at, gate_at, taps_at, weight, sems):
-        first = lax.rem(lax.axis_index("ctx"), 2) == 0
+    parts = half // width
+
+    def body(*refs):
+        got, near, local_mix, rate, res, ql, ct = refs[:7]
+        refs = refs[7:]
+        if not own:
+            mine, refs = refs[0], refs[3:]
+        outs, refs = refs[: 2 if own else 3], refs[2 if own else 3 :]
+        core_at, gate_at, sems = refs[0], refs[1], refs[-1]
+        side = lax.rem(lax.axis_index("ctx"), 2)
+        first = side == 0
+        start = (side if own else 1 - side) * half
+        states = got[...] if own else unpack(got, block, modes, half)
         copies = []
 
         def leave(source, target, sem):
@@ -476,47 +494,45 @@
             copy.start()
             copies.append(copy)
 
-        theirs = unpack(other, block, modes, 1)
-        own = got[...]
-        fade = jnp.where(first, 1.0, jnp.exp(-block * rate[...]))
-        weight[:, :half] = jnp.where(first, own, theirs)
-        weight[:, half:] = jnp.where(first, theirs, own)
-        weight[...] = res[...] * (near[...] + fade * weight[...])
-        taps_at[:, :half] = jnp.where(first, mine[:block, :], other[:block, :]).astype(f32) * scale
-        leave(taps_at.at[:, pl.ds(0, half)], taps.at[:, pl.ds(0, half)], sems.at[2 * parts])
-        taps_at[:, half:] = jnp.where(first, other[:block, :], mine[:block, :]).astype(f32) * scale
-        leave(taps_at.at[:, pl.ds(half, half)], taps.at[:, pl.ds(half, half)], sems.at[2 * parts + 1])
+        if not own:
+            taps_at = refs[2]
+            low, high = mine[:block, :], got[:block, :]
+            taps_at[:, :half] = jnp.where(first, low, high).astype(f32) * scale
+            leave(taps_at.at[:, pl.ds(0, half)], outs[2].at[:, pl.ds(0, half)], sems.at[2 * parts])
+            taps_at[:, half:] = jnp.where(first, high, low).astype(f32) * scale
+            leave(taps_at.at[:, pl.ds(half, half)], outs[2].at[:, pl.ds(half, half)], sems.at[2 * parts + 1])
         for k in range(parts):
             for lane in range(k * width, (k + 1) * width, LANES):
+                there = pl.ds(pl.multiple_of(start + lane, LANES), LANES)
                 lanes = slice(lane, lane + LANES)
-                far = mode_sum(rate[:, lanes], weight[:, lanes], 1.0, True, block)
-                mix = local_mix[:, lanes] + far
-                core_at[:, lanes] = (wide(ql, lanes) * mix).astype(bf)
-                gate_at[:, lanes] = (wide(ct, lanes) * mix).astype(bf)
-            cut = pl.ds(k * width, width)
-            leave(core_at.at[:, cut], core.at[:, cut], sems.at[k])
-            leave(gate_at.at[:, cut], gate.at[:, cut], sems.at[parts + k])
+                pace = rate[:, there]
+                fade = jnp.where(first, 1.0, jnp.exp(-block * pace))
+                weight = res[:, there] * (near[:, there] + fade * states[:, lanes])
+                mix = local_mix[:, there] + mode_sum(pace, weight, 1.0, True, block)
+                core_at[:, lanes] = (ql[:, there].astype(f32) * mix).astype(bf)
+                gate_at[:, lanes] = (ct[:, there].astype(f32) * mix).astype(bf)
+            here = pl.ds(k * width, width)
+            there = pl.ds(pl.multiple_of(start + k * width, width), width)
+            leave(core_at.at[:, here], outs[0].at[:, there], sems.at[k])
+            leave(gate_at.at[:, here], outs[1].at[:, there], sems.at[parts + k])
         for copy in copies:
             copy.wait()
 
-    operands = [mine, other, got, near, local_mix, rate, res, ql, ct]
+    operands = [got, near, local_mix, rate, res, ql, ct] + ([] if own else [mine])
     shape = (block, channels)
+    scratch_shapes = [pltpu.VMEM((block, half), bf)] * 2 + ([] if own else [pltpu.VMEM(shape, f32)])
     return pl.pallas_call(
         body,
-        in_specs=[pl.BlockSpec(memory_space=pltpu.VMEM)] * len(operands),
-        out_specs=[pl.BlockSpec(memory_space=pltpu.HBM)] * 3,
-        out_shape=[pltpu.HBM(shape, bf), pltpu.HBM(shape, bf), pltpu.HBM(shape, f32)],
-        scratch_shapes=[
-            pltpu.VMEM(shape, bf),
-            pltpu.VMEM(shape, bf),
-            pltpu.VMEM(shape, f32),
-            pltpu.VMEM((modes, channels), f32),
-            pltpu.SemaphoreType.DMA((2 * parts + 2,)),
-        ],
+        in_specs=[pl.BlockSpec(memory_space=pltpu.VMEM)] * len(operands)
+        + [pl.BlockSpec(memory_space=pltpu.HBM)] * len(outputs),
+        out_specs=[pl.BlockSpec(memory_space=pltpu.HBM)] * (2 if own else 3),
+        out_shape=[pltpu.HBM(shape, bf)] * 2 + ([] if own else [pltpu.HBM(shape, f32)]),
+        input_output_aliases={} if own else {len(operands): 0, len(operands) + 1: 1},
+        scratch_shapes=[*scratch_shapes, pltpu.SemaphoreType.DMA((2 * parts + 2,))],
         compiler_params=pltpu.CompilerParams(vmem_limit_bytes=VMEM_BYTES),
         cost_estimate=pl.CostEstimate(flops=0, bytes_accessed=1024, transcendentals=0),
-        name="tail",
-    )(*[in_vmem(a) for a in operands])
+        name=name,
+    )(*[in_vmem(a) for a in operands], *[in_hbm(a) for a in outputs])
 
 
 def local(
@@ -537,33 +553,39 @@
     matrices = [jnp.asarray(t) for t in tables(block)]
     width = min(512, channels)
 
-    (rate, ct, ql, res, own_three, ks, vs), (total,) = load(
-        [long_rate, cotangent, query_long, long_residue, matrices[1], key_short, value_short],
+    (ks, vs, rate, ct, ql), (short_in,) = load(
+        [key_short, value_short, long_rate, cotangent, query_long],
+        [((block, channels), half)],
+        product_kernel,
+        "product",
+        2,
+        width,
+    )
+    halo = shifted(short_in, 1)
+    (res, own_three, qs, kl, taps, own_two, nxt_two, back), (total,) = load(
+        [long_residue, matrices[1], query_short, key_long, short_taps, matrices[0], matrices[2], matrices[3]],
         [((modes, channels), full)],
         first_kernel,
-        "first",
-        3,
+        "states",
+        0,
         width,
+        blocked=[rate, ct, ql],
     )
     far, steps = None, masks()
     for at, mask in enumerate(steps):
         other = swapped(total, mask)
         beside = []
         if at == 1:
-            (qs, kl, taps, own_two, nxt_two, back), (long_spec,) = load(
-                [query_short, key_long, short_taps, matrices[0], matrices[2], matrices[3]],
-                [((2 * block, channels), full)],
+            (long_spec,) = run(
                 filter_kernel,
                 "filter",
-                0,
-                width,
-                [total],
-                [(block, full)],
                 [rate, res],
                 [own_three],
+                [(2 * block, full, "vmem")],
+                width,
+                [(block, full)],
+                [total],
             )
-            beside = [long_spec]
-        if at == 2:
             (grad_local,) = run(
                 grad_local_kernel,
                 "grad_local",
@@ -571,30 +593,35 @@
                 [own_three, back],
                 [(block, full, "vmem")],
                 width,
+            )
+            short_spec, own_spec = run(
+                short_filter_kernel,
+                "short_filter",
+                [taps, short_in],
+                [own_three, own_two],
+                [(2 * block, full, "vmem"), (2 * block, full, "vmem")],
+                width,
+            )
+            beside = [grad_local, short_spec]
+        if at == 2:
+            in_spec, short_mix, hidden, long_in, fore_state = run(
+                short_kernel,
+                "short",
+                [own_spec, halo, short_spec, qs, kl, rate],
+                [nxt_two, back],
+                [
+                    (2 * block, full, "vmem"),
+                    (block, full, "vmem"),
+                    (block, half, "vmem"),
+                    (block, half, "vmem"),
+                    (modes, full, "vmem"),
+                ],
+                width,
                 (),
                 [total],
             )
-            beside = [grad_local]
+            beside = [hidden]
         total, far = merge_states(total, other, far, rate, block, mask, at == len(steps) - 1, beside)
-    (short_in,) = run(product_kernel, "product", [ks, vs], [], [(block, half, "vmem")], width, (), [far])
-    halo = shifted(short_in, 1)
-    (short_spec,) = run(
-        short_filter_kernel, "short_filter", [taps], [own_three], [(2 * block, full, "vmem")], width, (), [far]
-    )
-    in_spec, short_mix, hidden, long_in, fore_state = run(
-        short_kernel,
-        "short",
-        [short_in, halo, short_spec, qs, kl, rate],
-        [own_two, nxt_two, back],
-        [
-            (2 * block, full, "vmem"),
-            (block, full, "vmem"),
-            (block, half, "vmem"),
-            (block, half, "vmem"),
-            (modes, full, "vmem"),
-        ],
-        width,
-    )
     long_grad, short_back = run(
         long_grad_kernel,
         "long_grad",
@@ -628,9 +655,12 @@
         [(block, half, "hbm")] * 4 + [(ROWS, full, "vmem")],
         width,
     )
-    mine, other, got, near = taps_and_states(part, fore_state, rate, [[token], [local_mix]], [sb_next])
-    core_output, query_long_grad, taps_grad = tail(
-        mine, other, got, near, local_mix, rate, res, ql, ct, width, sequence ** (-0.5)
+    mine, got, near = taps_and_states(part, fore_state, rate, [[local_mix], [token]], ())
+    other = swapped(mine, 1)
+    ready = [near, local_mix, rate, res, ql, ct]
+    some = gated(True, "gated_own", got, *ready, min(width, channels // 2))
+    core_output, query_long_grad, taps_grad = gated(
+        False, "gated_other", other, *ready, min(width, channels // 2), sequence ** (-0.5), mine, some
     )
     return (
         core_output,

time: 55 us -> 52.2 us (0.949)
  starting transfers between devices: 20.2 us -> 13.8 us
  waiting for transfers between devices: 9.41 us -> 12.4 us
    ppermute x9, starting transfers between devices: 17.4 us -> 10.1 us  [swapped(): return lax.ppermute(value, 'ctx', [(i, i ^ mask) for i in range(size)])]
    ppermute x9, waiting for transfers between devices: 9.4 us -> 12.4 us  [swapped(): return lax.ppermute(value, 'ctx', [(i, i ^ mask) for i in range(size)])]
    pallas_call x2, Pallas kernels: 6.26 us -> 3.86 us  [load(): pl.pallas_call(whole, in_specs=[pl.BlockSpec(memory_space=pltpu.HBM)] * c...]
    pallas_call x8, Pallas kernels: 14.9 us -> 17 us  [run(): pl.pallas_call(whole, in_specs=[pl.BlockSpec(memory_space=pltpu.VMEM)] *...]
    ppermute x2, starting transfers between devices: 2.8 us -> 3.68 us  [shifted(): return lax.ppermute(value, 'ctx', pairs)]
    pallas_call x1 -> x2, Pallas kernels: 2.48 us -> 3.24 us  [gated(): pl.pallas_call(body, in_specs=[pl.BlockSpec(memory_space=pltpu.VMEM)] * l...]
  transfers between devices with their start and end apart: 11 -> 11, of which waited for: 7 -> 5; matrix products, arithmetic and copies ran while one was open for 0% -> 0% of each run, Pallas kernels for 33% -> 33%
where the time goes in v3:
time: 52.2 us; the launch traced here: 51.9 us
  Pallas kernels  24.7 us (47%)
  starting transfers between devices  13.8 us (26%)
  waiting for transfers between devices  12.4 us (24%)
  between operations  0.95 us (2%)
    pallas_call x8, Pallas kernels, run(): pl.pallas_call(whole, in_specs=[pl.BlockSpec(memory_space=pltpu.VMEM)] *...  17 us
    ppermute x9, waiting for transfers between devices, swapped(): return lax.ppermute(value, 'ctx', [(i, i ^ mask) for i in range(size)])  12.4 us
    ppermute x9, starting transfers between devices, swapped(): return lax.ppermute(value, 'ctx', [(i, i ^ mask) for i in range(size)])  10.1 us
    pallas_call x2, Pallas kernels, load(): pl.pallas_call(whole, in_specs=[pl.BlockSpec(memory_space=pltpu.HBM)] * c...  3.86 us
    ppermute x2, starting transfers between devices, shifted(): return lax.ppermute(value, 'ctx', pairs)  3.68 us
    pallas_call x2, Pallas kernels, gated(): pl.pallas_call(body, in_specs=[pl.BlockSpec(memory_space=pltpu.VMEM)] * l...  3.24 us
  transfers between devices with their start and end apart: 11, of which 5 were waited for; matrix products, arithmetic and copies ran while one was open for 0% of the time, Pallas kernels for 33%

profile of v3, /device:TPU:0, one launch (start us, length us, event | category | flops | bytes accessed | tf_op | source)
XLA Modules:
  0.0 51.9 jit_solution(4191835550354106366)
XLA Ops:
  0.6 1.8 %product.1 = (bf16[128,2048]{1,0:T(8,128)(2,1)S(1)}, bf16[128,2048]{1,0:T(8,128)(2,1)S(1)}, f32[16,2048]{1,0:T(8,128)S(1)}, bf16[128,2048]{1,0:T(8,128)(2,1)S(1)...) custom-call(bf16[128,2048]{1,0:T(8,128)(2,1)} %refs_0_.2, bf16[128,2048]{1,0:T(8,128)(2,1)} %refs_1_.2, ...), custom_call_target="tpu_custom_call" | custom-call | bytes 1024 | tf_op jit(solution)/shard_map/product/pallas_call | solution.py:183
  2.5 2.4 %collective-permute-start.3 = (bf16[128,2048]{1,0:T(8,128)(2,1)S(1)}, bf16[128,2048]{1,0:T(8,128)(2,1)S(1)}, u32[]{:S(2)}, u32[]{:S(2)}) collective-permute-start(bf16[128,2048]{1,0:T(8,128)(2,1)S(1)} %get-tuple-element.68.refs_1_), channel_id=1, source_target_pairs={{0,4},{4,8},{8,12},{12,16},{16,20},{20,24},{24,28},{1,5},{5,9},{9,... | collective-permute-start | bytes 1572872 | tf_op jit(solution)/shard_map/ppermute | solution.py:329
  4.9 2.0 %states.1 = (f32[16,2048]{1,0:T(8,128)S(1)}, bf16[256,384]{1,0:T(8,128)(2,1)S(1)}, bf16[128,2048]{1,0:T(8,128)(2,1)S(1)}, bf16[128,2048]{1,0:T(8,128)(2,1)S(1)},...) custom-call(f32[16,2048]{1,0:T(8,128)} %refs_0_.3, ...), custom_call_target="tpu_custom_call" | custom-call | bytes 1024 | tf_op jit(solution)/shard_map/states/pallas_call | solution.py:183
  6.9 2.6 %collective-permute-start = (f32[16,2048]{1,0:T(8,128)S(1)}, f32[16,2048]{1,0:T(8,128)S(1)}, u32[]{:S(2)}, u32[]{:S(2)}) collective-permute-start(f32[16,2048]{1,0:T(8,128)S(1)} %get-tuple-element.63.refs_0_), channel_id=1, source_target_pairs={{0,4},{4,0},{8,12},{12,8},{16,20},{20,16},{24,28},{28,24},{1,5},{5... | collective-permute-start | bytes 393224 | tf_op jit(solution)/shard_map/ppermute | solution.py:334
  9.5 1.0 %collective-permute-done.refs_1_ = f32[16,2048]{1,0:T(8,128)S(1)} collective-permute-done((f32[16,2048]{1,0:T(8,128)S(1)}, f32[16,2048]{1,0:T(8,128)S(1)}, u32[]{:S(2)}, u32[]{:S(2)}) %collective-permute-start) | collective-permute-done | bytes 131104 | tf_op jit(solution)/shard_map/ppermute | solution.py:334
  10.6 1.6 %collective-permute-start.1 = (f32[16,2048]{1,0:T(8,128)S(1)}, f32[16,2048]{1,0:T(8,128)S(1)}, u32[]{:S(2)}, u32[]{:S(2)}) collective-permute-start(f32[16,2048]{1,0:T(8,128)S(1)} %get-tuple-element.64.refs_3_.refs_0_), channel_id=1, source_target_pairs={{0,8},{4,12},{8,0},{12,4},{16,24},{20,28},{24,16},{28,20},{1,9},{5... | collective-permute-start | bytes 393224 | tf_op jit(solution)/shard_map/ppermute | solution.py:334
  12.2 1.0 %short_filter.1 = (f32[256,2048]{1,0:T(8,128)S(1)}, f32[256,2048]{1,0:T(8,128)S(1)}) custom-call(f32[128,2048]{1,0:T(8,128)S(1)} %get-tuple-element.67.refs_0_, bf16[128,2048]{1,0:T(8,128)(2,1)S(1)} %get-tuple-element.68.refs_1_, bf16[256,384]{1,0:T(8,128)(2,1)S(1)} %get-tuple-element.62.refs_2_.refs_3_, bf16[256,256]{1,0:T(8,128)(2,1)S(1)} %get-tuple-element.69.refs_3_.refs_2_), custom_call_target="tpu_custom_call" | custom-call | bytes 1024 | tf_op jit(solution)/shard_map/short_filter/pallas_call | solution.py:300
  13.2 2.0 %filter.1.refs_2_.refs_1_ = f32[256,2048]{1,0:T(8,128)S(1)} custom-call(f32[16,2048]{1,0:T(8,128)S(1)} %get-tuple-element.60.refs_8_.refs_2_.refs_0_.refs_5_.refs_3_, f32[16,2048]{1,0:T(8,128)S(1)} %get-tuple-element.61.refs_1_.refs_3_.refs_4_, bf16[256,384]{1,0:T(8,128)(2,1)S(1)} %get-tuple-element.62.refs_2_.refs_3_, ...), custom_call_target="tpu_custom_call" | custom-call | bytes 1024 | tf_op jit(solution)/shard_map/filter/pallas_call | solution.py:300
  15.1 2.0 %grad_local.1.refs_4_.refs_0_ = f32[128,2048]{1,0:T(8,128)S(1)} custom-call(bf16[128,2048]{1,0:T(8,128)(2,1)S(1)} %get-tuple-element.58.refs_10_.refs_0_.refs_5_, bf16[128,2048]{1,0:T(8,128)(2,1)S(1)} %get-tuple-element.59.refs_9_.refs_1_.refs_6_, f32[256,2048]{1,0:T(8,128)S(1)} %filter.1.refs_2_.refs_1_, ...), custom_call_target="tpu_custom_call" | custom-call | bytes 1024 | tf_op jit(solution)/shard_map/grad_local/pallas_call | solution.py:300
  17.2 0.9 %collective-permute-start.2 = (f32[16,2048]{1,0:T(8,128)S(1)}, f32[16,2048]{1,0:T(8,128)S(1)}, u32[]{:S(2)}, u32[]{:S(2)}) collective-permute-start(f32[16,2048]{1,0:T(8,128)S(1)} %get-tuple-element.71.refs_8_.refs_0_), channel_id=1, source_target_pairs={{0,16},{4,20},{8,24},{12,28},{16,0},{20,4},{24,8},{28,12},{1,17},{... | collective-permute-start | bytes 393224 | tf_op jit(solution)/shard_map/ppermute | solution.py:334
  18.1 3.5 %short.1 = (f32[256,2048]{1,0:T(8,128)S(1)}, f32[128,2048]{1,0:T(8,128)S(1)}, bf16[128,2048]{1,0:T(8,128)(2,1)S(1)}, bf16[128,2048]{1,0:T(8,128)(2,1)S(1)}, f32[16,2048]{1,0:T(8,128)S(1)}) custom-call(f32[256,2048]{1,0:T(8,128)S(1)} %get-tuple-element.73.refs_0_, bf16[128,2048]{1,0:T(8,128)(2,1)S(1)} %collective-permute-done.3.refs_1_, ...), custom_call_target="tpu_custom_call" | custom-call | bytes 1024 | tf_op jit(solution)/shard_map/short/pallas_call | solution.py:300
  21.6 2.0 %collective-permute-done.2.refs_1_ = f32[16,2048]{1,0:T(8,128)S(1)} collective-permute-done((f32[16,2048]{1,0:T(8,128)S(1)}, f32[16,2048]{1,0:T(8,128)S(1)}, u32[]{:S(2)}, u32[]{:S(2)}) %collective-permute-start.2) | collective-permute-done | bytes 131104 | tf_op jit(solution)/shard_map/ppermute | solution.py:334
  23.6 2.2 %long_grad.1 = (bf16[128,2048]{1,0:T(8,128)(2,1)S(1)}, bf16[128,2048]{1,0:T(8,128)(2,1)S(1)}) custom-call(f32[128,2048]{1,0:T(8,128)S(1)} %grad_local.1.refs_4_.refs_0_, f32[16,2048]{1,0:T(8,128)S(1)} %merge.5.refs_1_, f32[16,2048]{1,0:T(8,128)S(1)} %get-tuple-element.60.refs_8_.refs_2_.refs_0_.refs_5_.refs_3_, ...), custom_call_target="tpu_custom_call" | custom-call | bytes 1024 | tf_op jit(solution)/shard_map/long_grad/pallas_call | solution.py:300
  25.8 1.9 %taps.1 = (f32[256,2048]{1,0:T(8,128)S(1)}, bf16[128,2048]{1,0:T(8,128)(2,1)S(1)}) custom-call(bf16[128,2048]{1,0:T(8,128)(2,1)S(1)} %get-tuple-element.78.refs_0_, f32[256,2048]{1,0:T(8,128)S(1)} %get-tuple-element.79.refs_1_, bf16[256,256]{1,0:T(8,128)(2,1)S(1)} %get-tuple-element.69.refs_3_.refs_2_, ...), custom_call_target="tpu_custom_call" | custom-call | bytes 1024 | tf_op jit(solution)/shard_map/taps/pallas_call | solution.py:300
  27.8 1.3 %collective-permute-start.9 = (bf16[128,2048]{1,0:T(8,128)(2,1)S(1)}, bf16[128,2048]{1,0:T(8,128)(2,1)S(1)}, u32[]{:S(2)}, u32[]{:S(2)}) collective-permute-start(bf16[128,2048]{1,0:T(8,128)(2,1)S(1)} %get-tuple-element.78.refs_0_), channel_id=1, source_target_pairs={{4,0},{8,4},{12,8},{16,12},{20,16},{24,20},{28,24},{5,1},{9,5},{13... | collective-permute-start | bytes 1572872 | tf_op jit(solution)/shard_map/ppermute | solution.py:329
  29.7 2.4 %collective-permute-start.5 = (bf16[224,384]{1,0:T(8,128)(2,1)S(1)}, bf16[224,384]{1,0:T(8,128)(2,1)S(1)}, u32[]{:S(2)}, u32[]{:S(2)}) collective-permute-start(bf16[224,384]{1,0:T(8,128)(2,1)S(1)} %get-tuple-element.84.refs_0_), channel_id=1, source_target_pairs={{0,8},{4,12},{8,0},{12,4},{16,24},{20,28},{24,16},{28,20},{1,9},{5... | collective-permute-start | bytes 516104 | tf_op jit(solution)/shard_map/ppermute | solution.py:334
  32.4 1.7 %long_local.1.refs_4_.refs_2_ = f32[128,2048]{1,0:T(8,128)S(1)} custom-call(bf16[128,2048]{1,0:T(8,128)(2,1)S(1)} %get-tuple-element.86.refs_0_, f32[256,2048]{1,0:T(8,128)S(1)} %filter.1.refs_2_.refs_1_, bf16[256,256]{1,0:T(8,128)(2,1)S(1)} %get-tuple-element.69.refs_3_.refs_2_, bf16[256,256]{1,0:T(8,128)(2,1)S(1)} %get-tuple-element.65.refs_4_.refs_7_.refs_3_.refs_10_), custom_call_target="tpu_custom_call" | custom-call | bytes 1024 | tf_op jit(solution)/shard_map/long_local/pallas_call | solution.py:300
  34.0 8.3 %collective-permute-done.5.refs_1_ = bf16[224,384]{1,0:T(8,128)(2,1)S(1)} collective-permute-done((bf16[224,384]{1,0:T(8,128)(2,1)S(1)}, bf16[224,384]{1,0:T(8,128)(2,1)S(1)}, u32[]{:S(2)}, u32[]{:S(2)}) %collective-permute-start.5) | collective-permute-done | bytes 172064 | tf_op jit(solution)/shard_map/ppermute | solution.py:334
  42.5 0.4 collective-permute-start.6
  42.9 1.8 %collective-permute-start.8 = (bf16[128,640]{1,0:T(8,128)(2,1)S(1)}, bf16[128,640]{1,0:T(8,128)(2,1)S(1)}, u32[]{:S(2)}, u32[]{:S(2)}) collective-permute-start(bf16[128,640]{1,0:T(8,128)(2,1)S(1)} %go_right.1.refs_2_), channel_id=1, source_target_pairs={{0,8},{4,12},{8,0},{12,4},{16,24},{20,28},{24,16},{28,20},{1,9},{5... | collective-permute-start | bytes 491528 | tf_op jit(solution)/shard_map/ppermute | solution.py:334
  44.7 2.9 %input_grad.1 = (bf16[128,2048]{1,0:T(8,128)(2,1)}, bf16[128,2048]{1,0:T(8,128)(2,1)}, bf16[128,2048]{1,0:T(8,128)(2,1)}, bf16[128,2048]{1,0:T(8,128)(2,1)}, f32[8,2048]{1,0:T(8,128)S(1)}) custom-call(bf16[128,2048]{1,0:T(8,128)(2,1)S(1)} %collective-permute-done.9.refs_0_, f32[256,2048]{1,0:T(8,128)S(1)} %get-tuple-element.91.refs_1_, ...), custom_call_target="tpu_custom_call" | custom-call | bytes 1024 | tf_op jit(solution)/shard_map/input_grad/pallas_call | solution.py:300
  47.7 0.6 %collective-permute-done.8.refs_3_ = bf16[128,640]{1,0:T(8,128)(2,1)S(1)} collective-permute-done((bf16[128,640]{1,0:T(8,128)(2,1)S(1)}, bf16[128,640]{1,0:T(8,128)(2,1)S(1)}, u32[]{:S(2)}, u32[]{:S(2)}) %collective-permute-start.8) | collective-permute-done | bytes 163872 | tf_op jit(solution)/shard_map/ppermute | solution.py:334
  48.5 1.6 %gated_own.1 = (bf16[128,2048]{1,0:T(8,128)(2,1)}, bf16[128,2048]{1,0:T(8,128)(2,1)}) custom-call(f32[16,1024]{1,0:T(8,128)S(1)} %get-tuple-element.99.refs_0_, f32[16,2048]{1,0:T(8,128)S(1)} %get-tuple-element.98.refs_1_, f32[128,2048]{1,0:T(8,128)S(1)} %long_local.1.refs_4_.refs_2_, ...), custom_call_target="tpu_custom_call" | custom-call | bytes 1024 | tf_op jit(solution)/shard_map/gated_own/pallas_call | solution.py:524
  50.1 1.7 %gated_other.1 = (bf16[128,2048]{1,0:T(8,128)(2,1)}, bf16[128,2048]{1,0:T(8,128)(2,1)}, f32[128,2048]{1,0:T(8,128)}) custom-call(bf16[160,1024]{1,0:T(8,128)(2,1)S(1)} %collective-permute-done.10.refs_0_, f32[16,2048]{1,0:T(8,128)S(1)} %get-tuple-element.98.refs_1_, ...), custom_call_target="tpu_custom_call", output_to_operand_aliasing={{0}: (8, {}), {1}: (9, {})} | custom-call | bytes 1024 | tf_op jit(solution)/shard_map/gated_other/pallas_call | solution.py:524
  (18 shorter events, 1.5 us)
Async XLA Ops:
  2.5 15.6 %collective-permute-start.3 = (bf16[128,2048]{1,0:T(8,128)(2,1)S(1)}, bf16[128,2048]{1,0:T(8,128)(2,1)S(1)}, u32[]{:S(2)}, u32[]{:S(2)}) collective-permute-start(bf16[128,2048]{1,0:T(8,128)(2,1)S(1)} %get-tuple-element.68.refs_1_), channel_id=1, source_target_pairs={{0,4},{4,8},{8,12},{12,16},{16,20},{20,24},{24,28},{1,5},{5,9},{9,... | collective-permute-start | bytes 1572872 | tf_op jit(solution)/shard_map/ppermute | solution.py:329
  6.9 3.6 %collective-permute-start = (f32[16,2048]{1,0:T(8,128)S(1)}, f32[16,2048]{1,0:T(8,128)S(1)}, u32[]{:S(2)}, u32[]{:S(2)}) collective-permute-start(f32[16,2048]{1,0:T(8,128)S(1)} %get-tuple-element.63.refs_0_), channel_id=1, source_target_pairs={{0,4},{4,0},{8,12},{12,8},{16,20},{20,16},{24,28},{28,24},{1,5},{5... | collective-permute-start | bytes 393224 | tf_op jit(solution)/shard_map/ppermute | solution.py:334
  10.6 6.5 %collective-permute-start.1 = (f32[16,2048]{1,0:T(8,128)S(1)}, f32[16,2048]{1,0:T(8,128)S(1)}, u32[]{:S(2)}, u32[]{:S(2)}) collective-permute-start(f32[16,2048]{1,0:T(8,128)S(1)} %get-tuple-element.64.refs_3_.refs_0_), channel_id=1, source_target_pairs={{0,8},{4,12},{8,0},{12,4},{16,24},{20,28},{24,16},{28,20},{1,9},{5... | collective-permute-start | bytes 393224 | tf_op jit(solution)/shard_map/ppermute | solution.py:334
  17.2 6.3 %collective-permute-start.2 = (f32[16,2048]{1,0:T(8,128)S(1)}, f32[16,2048]{1,0:T(8,128)S(1)}, u32[]{:S(2)}, u32[]{:S(2)}) collective-permute-start(f32[16,2048]{1,0:T(8,128)S(1)} %get-tuple-element.71.refs_8_.refs_0_), channel_id=1, source_target_pairs={{0,16},{4,20},{8,24},{12,28},{16,0},{20,4},{24,8},{28,12},{1,17},{... | collective-permute-start | bytes 393224 | tf_op jit(solution)/shard_map/ppermute | solution.py:334
  27.8 1.8 %collective-permute-start.4 = (bf16[192,1024]{1,0:T(8,128)(2,1)S(1)}, bf16[192,1024]{1,0:T(8,128)(2,1)S(1)}, u32[]{:S(2)}, u32[]{:S(2)}) collective-permute-start(bf16[192,1024]{1,0:T(8,128)(2,1)S(1)} %get-tuple-element.83), channel_id=1, source_target_pairs={{0,4},{4,0},{8,12},{12,8},{16,20},{20,16},{24,28},{28,24},{1,5},{5... | collective-permute-start | bytes 1179656 | tf_op jit(solution)/shard_map/ppermute | solution.py:334
  27.8 16.9 %collective-permute-start.9 = (bf16[128,2048]{1,0:T(8,128)(2,1)S(1)}, bf16[128,2048]{1,0:T(8,128)(2,1)S(1)}, u32[]{:S(2)}, u32[]{:S(2)}) collective-permute-start(bf16[128,2048]{1,0:T(8,128)(2,1)S(1)} %get-tuple-element.78.refs_0_), channel_id=1, source_target_pairs={{4,0},{8,4},{12,8},{16,12},{20,16},{24,20},{28,24},{5,1},{9,5},{13... | collective-permute-start | bytes 1572872 | tf_op jit(solution)/shard_map/ppermute | solution.py:329
  29.7 12.7 %collective-permute-start.5 = (bf16[224,384]{1,0:T(8,128)(2,1)S(1)}, bf16[224,384]{1,0:T(8,128)(2,1)S(1)}, u32[]{:S(2)}, u32[]{:S(2)}) collective-permute-start(bf16[224,384]{1,0:T(8,128)(2,1)S(1)} %get-tuple-element.84.refs_0_), channel_id=1, source_target_pairs={{0,8},{4,12},{8,0},{12,4},{16,24},{20,28},{24,16},{28,20},{1,9},{5... | collective-permute-start | bytes 516104 | tf_op jit(solution)/shard_map/ppermute | solution.py:334
  32.1 10.8 %collective-permute-start.7 = (bf16[128,640]{1,0:T(8,128)(2,1)S(1)}, bf16[128,640]{1,0:T(8,128)(2,1)S(1)}, u32[]{:S(2)}, u32[]{:S(2)}) collective-permute-start(bf16[128,640]{1,0:T(8,128)(2,1)S(1)} %get-tuple-element.88.refs_0_), channel_id=1, source_target_pairs={{0,16},{4,20},{8,24},{12,28},{16,0},{20,4},{24,8},{28,12},{1,17},{... | collective-permute-start | bytes 491528 | tf_op jit(solution)/shard_map/ppermute | solution.py:334
  42.5 5.8 %collective-permute-start.6 = (bf16[224,384]{1,0:T(8,128)(2,1)S(1)}, bf16[224,384]{1,0:T(8,128)(2,1)S(1)}, u32[]{:S(2)}, u32[]{:S(2)}) collective-permute-start(bf16[224,384]{1,0:T(8,128)(2,1)S(1)} %get-tuple-element.87.refs_0_), channel_id=1, source_target_pairs={{0,16},{4,20},{8,24},{12,28},{16,0},{20,4},{24,8},{28,12},{1,17},{... | collective-permute-start | bytes 516104 | tf_op jit(solution)/shard_map/ppermute | solution.py:334
  42.9 5.4 %collective-permute-start.8 = (bf16[128,640]{1,0:T(8,128)(2,1)S(1)}, bf16[128,640]{1,0:T(8,128)(2,1)S(1)}, u32[]{:S(2)}, u32[]{:S(2)}) collective-permute-start(bf16[128,640]{1,0:T(8,128)(2,1)S(1)} %go_right.1.refs_2_), channel_id=1, source_target_pairs={{0,8},{4,12},{8,0},{12,4},{16,24},{20,28},{24,16},{28,20},{1,9},{5... | collective-permute-start | bytes 491528 | tf_op jit(solution)/shard_map/ppermute | solution.py:334
  48.4 1.7 %collective-permute-start.10 = (bf16[160,1024]{1,0:T(8,128)(2,1)S(1)}, bf16[160,1024]{1,0:T(8,128)(2,1)S(1)}, u32[]{:S(2)}, u32[]{:S(2)}) collective-permute-start(bf16[160,1024]{1,0:T(8,128)(2,1)S(1)} %get-tuple-element.97.refs_7_), channel_id=1, source_target_pairs={{0,4},{4,0},{8,12},{12,8},{16,20},{20,16},{24,28},{28,24},{1,5},{5... | collective-permute-start | bytes 983048 | tf_op jit(solution)/shard_map/ppermute | solution.py:334

commit v4 on v3

--- a/solution.py
+++ b/solution.py
@@ -391,22 +391,33 @@
     def sum_of(mine, theirs):
         return (mine[:block, :].astype(f32) + theirs[:block, :].astype(f32)).astype(bf)
 
-    def apart(part, state, send, keep):
+    pieces = 4
+    piece = half // pieces
+
+    def apart(part, state, keep, states, *sends):
         first = lax.rem(lax.axis_index("ctx"), 2) == 0
         low, high = part[:, :half], part[:, half:]
-        send[:block, :] = jnp.where(first, high, low)
+        gone = jnp.where(first, high, low)
+        for i, send in enumerate(sends):
+            send[...] = gone[:, i * piece : (i + 1) * piece]
         keep[...] = jnp.where(first, low, high)
-        pack(send, block, state[...])
-
-    tall = (block + 4 * modes, half)
-    send, keep = small(apart, "apart", [part, state], [(tall, bf), ((block, half), bf)])
-    other = swapped(send, 1)
-
-    def first_sum(keep, other, state, rate, left, right, total, near):
-        both = sum_of(keep, other)
+        pack(states, 0, state[...])
+
+    keep, packed, *sends = small(
+        apart,
+        "apart",
+        [part, state],
+        [((block, half), bf), ((4 * modes, half), bf)] + [((block, piece), bf)] * pieces,
+    )
+    packed = swapped(packed, 1)
+    others = [swapped(send, 1) for send in sends]
+
+    def first_sum(keep, packed, state, rate, *refs):
+        others, (left, right, total, near) = refs[:pieces], refs[pieces:]
+        both = sum_of(keep, jnp.concatenate([other[...] for other in others], axis=1))
         left[:block, :] = both[:, :cut]
         right[...] = both[:, cut:]
-        own, theirs = state[...], unpack(other, block, modes, channels)
+        own, theirs = state[...], unpack(packed, 0, modes, channels)
         first = lax.rem(lax.axis_index("ctx"), 2) == 0
         near[...] = jnp.where(first, 0.0, theirs)
         fade = jnp.exp(-block * rate[...])
@@ -417,7 +428,7 @@
     lefts = ((block + 2 * modes * -(-half // cut), cut), bf)
     rights, states = ((block, half - cut), bf), ((modes, half), f32)
     left, right, total, near = small(
-        first_sum, "first_sum", [keep, other, state, rate], [lefts, rights, states, (state.shape, f32)], before
+        first_sum, "first_sum", [keep, packed, state, rate, *others], [lefts, rights, states, (state.shape, f32)], before
     )
     rest = masks()[1:]
     got = None
@@ -655,7 +666,7 @@
         [(block, half, "hbm")] * 4 + [(ROWS, full, "vmem")],
         width,
     )
-    mine, got, near = taps_and_states(part, fore_state, rate, [[local_mix], [token]], ())
+    mine, got, near = taps_and_states(part, fore_state, rate, [[token], [local_mix]], ())
     other = swapped(mine, 1)
     ready = [near, local_mix, rate, res, ql, ct]
     some = gated(True, "gated_own", got, *ready, min(width, channels // 2))

time: 52.2 us -> 50.3 us (0.964)
  waiting for transfers between devices: 12.4 us -> 9.69 us
  starting transfers between devices: 13.8 us -> 14.9 us
    ppermute x9 -> x13, waiting for transfers between devices: 12.4 us -> 9.69 us  [swapped(): return lax.ppermute(value, 'ctx', [(i, i ^ mask) for i in range(size)])]
    ppermute x9 -> x13, starting transfers between devices: 10.1 us -> 11 us  [swapped(): return lax.ppermute(value, 'ctx', [(i, i ^ mask) for i in range(size)])]
  transfers between devices with their start and end apart: 11 -> 15, of which waited for: 5 -> 8; matrix products, arithmetic and copies ran while one was open for 0% -> 0% of each run, Pallas kernels for 33% -> 37%
where the time goes in v4:
time: 50.3 us; the launch traced here: 50.1 us
  Pallas kernels  24.6 us (49%)
  starting transfers between devices  14.9 us (30%)
  waiting for transfers between devices  9.69 us (19%)
  between operations  0.96 us (2%)
    pallas_call x8, Pallas kernels, run(): pl.pallas_call(whole, in_specs=[pl.BlockSpec(memory_space=pltpu.VMEM)] *...  16.9 us
    ppermute x13, starting transfers between devices, swapped(): return lax.ppermute(value, 'ctx', [(i, i ^ mask) for i in range(size)])  11 us
    ppermute x13, waiting for transfers between devices, swapped(): return lax.ppermute(value, 'ctx', [(i, i ^ mask) for i in range(size)])  9.69 us
    ppermute x2, starting transfers between devices, shifted(): return lax.ppermute(value, 'ctx', pairs)  3.86 us
    pallas_call x2, Pallas kernels, load(): pl.pallas_call(whole, in_specs=[pl.BlockSpec(memory_space=pltpu.HBM)] * c...  3.86 us
    pallas_call x2, Pallas kernels, gated(): pl.pallas_call(body, in_specs=[pl.BlockSpec(memory_space=pltpu.VMEM)] * l...  3.24 us
  transfers between devices with their start and end apart: 15, of which 8 were waited for; matrix products, arithmetic and copies ran while one was open for 0% of the time, Pallas kernels for 37%

profile of v4, /device:TPU:0, one launch (start us, length us, event | category | flops | bytes accessed | tf_op | source)
XLA Modules:
  0.0 50.1 jit_solution(829647329521445376)
XLA Ops:
  0.6 1.8 %product.1 = (bf16[128,2048]{1,0:T(8,128)(2,1)S(1)}, bf16[128,2048]{1,0:T(8,128)(2,1)S(1)}, f32[16,2048]{1,0:T(8,128)S(1)}, bf16[128,2048]{1,0:T(8,128)(2,1)S(1)...) custom-call(bf16[128,2048]{1,0:T(8,128)(2,1)} %refs_0_.2, bf16[128,2048]{1,0:T(8,128)(2,1)} %refs_1_.2, ...), custom_call_target="tpu_custom_call" | custom-call | bytes 1024 | tf_op jit(solution)/shard_map/product/pallas_call | solution.py:183
  2.5 2.4 %collective-permute-start.3 = (bf16[128,2048]{1,0:T(8,128)(2,1)S(1)}, bf16[128,2048]{1,0:T(8,128)(2,1)S(1)}, u32[]{:S(2)}, u32[]{:S(2)}) collective-permute-start(bf16[128,2048]{1,0:T(8,128)(2,1)S(1)} %get-tuple-element.72.refs_1_), channel_id=1, source_target_pairs={{0,4},{4,8},{8,12},{12,16},{16,20},{20,24},{24,28},{1,5},{5,9},{9,... | collective-permute-start | bytes 1572872 | tf_op jit(solution)/shard_map/ppermute | solution.py:329
  4.9 2.0 %states.1 = (f32[16,2048]{1,0:T(8,128)S(1)}, bf16[256,384]{1,0:T(8,128)(2,1)S(1)}, bf16[128,2048]{1,0:T(8,128)(2,1)S(1)}, bf16[128,2048]{1,0:T(8,128)(2,1)S(1)},...) custom-call(f32[16,2048]{1,0:T(8,128)} %refs_0_.3, ...), custom_call_target="tpu_custom_call" | custom-call | bytes 1024 | tf_op jit(solution)/shard_map/states/pallas_call | solution.py:183
  6.9 2.6 %collective-permute-start = (f32[16,2048]{1,0:T(8,128)S(1)}, f32[16,2048]{1,0:T(8,128)S(1)}, u32[]{:S(2)}, u32[]{:S(2)}) collective-permute-start(f32[16,2048]{1,0:T(8,128)S(1)} %get-tuple-element.67.refs_0_), channel_id=1, source_target_pairs={{0,4},{4,0},{8,12},{12,8},{16,20},{20,16},{24,28},{28,24},{1,5},{5... | collective-permute-start | bytes 393224 | tf_op jit(solution)/shard_map/ppermute | solution.py:334
  9.5 1.0 %collective-permute-done.refs_1_ = f32[16,2048]{1,0:T(8,128)S(1)} collective-permute-done((f32[16,2048]{1,0:T(8,128)S(1)}, f32[16,2048]{1,0:T(8,128)S(1)}, u32[]{:S(2)}, u32[]{:S(2)}) %collective-permute-start) | collective-permute-done | bytes 131104 | tf_op jit(solution)/shard_map/ppermute | solution.py:334
  10.6 1.6 %collective-permute-start.1 = (f32[16,2048]{1,0:T(8,128)S(1)}, f32[16,2048]{1,0:T(8,128)S(1)}, u32[]{:S(2)}, u32[]{:S(2)}) collective-permute-start(f32[16,2048]{1,0:T(8,128)S(1)} %get-tuple-element.68.refs_3_.refs_0_), channel_id=1, source_target_pairs={{0,8},{4,12},{8,0},{12,4},{16,24},{20,28},{24,16},{28,20},{1,9},{5... | collective-permute-start | bytes 393224 | tf_op jit(solution)/shard_map/ppermute | solution.py:334
  12.2 1.0 %short_filter.1 = (f32[256,2048]{1,0:T(8,128)S(1)}, f32[256,2048]{1,0:T(8,128)S(1)}) custom-call(f32[128,2048]{1,0:T(8,128)S(1)} %get-tuple-element.71.refs_0_, bf16[128,2048]{1,0:T(8,128)(2,1)S(1)} %get-tuple-element.72.refs_1_, bf16[256,384]{1,0:T(8,128)(2,1)S(1)} %get-tuple-element.66.refs_2_.refs_3_, bf16[256,256]{1,0:T(8,128)(2,1)S(1)} %get-tuple-element.73.refs_3_.refs_2_), custom_call_target="tpu_custom_call" | custom-call | bytes 1024 | tf_op jit(solution)/shard_map/short_filter/pallas_call | solution.py:300
  13.2 2.0 %filter.1.refs_2_.refs_1_ = f32[256,2048]{1,0:T(8,128)S(1)} custom-call(f32[16,2048]{1,0:T(8,128)S(1)} %get-tuple-element.64.refs_8_.refs_2_.refs_0_.refs_5_.refs_3_, f32[16,2048]{1,0:T(8,128)S(1)} %get-tuple-element.65.refs_1_.refs_3_.refs_4_, bf16[256,384]{1,0:T(8,128)(2,1)S(1)} %get-tuple-element.66.refs_2_.refs_3_, ...), custom_call_target="tpu_custom_call" | custom-call | bytes 1024 | tf_op jit(solution)/shard_map/filter/pallas_call | solution.py:300
  15.1 2.0 %grad_local.1.refs_4_.refs_0_ = f32[128,2048]{1,0:T(8,128)S(1)} custom-call(bf16[128,2048]{1,0:T(8,128)(2,1)S(1)} %get-tuple-element.62.refs_10_.refs_0_.refs_5_, bf16[128,2048]{1,0:T(8,128)(2,1)S(1)} %get-tuple-element.63.refs_9_.refs_1_.refs_6_, f32[256,2048]{1,0:T(8,128)S(1)} %filter.1.refs_2_.refs_1_, ...), custom_call_target="tpu_custom_call" | custom-call | bytes 1024 | tf_op jit(solution)/shard_map/grad_local/pallas_call | solution.py:300
  17.2 0.9 %collective-permute-start.2 = (f32[16,2048]{1,0:T(8,128)S(1)}, f32[16,2048]{1,0:T(8,128)S(1)}, u32[]{:S(2)}, u32[]{:S(2)}) collective-permute-start(f32[16,2048]{1,0:T(8,128)S(1)} %get-tuple-element.75.refs_8_.refs_0_), channel_id=1, source_target_pairs={{0,16},{4,20},{8,24},{12,28},{16,0},{20,4},{24,8},{28,12},{1,17},{... | collective-permute-start | bytes 393224 | tf_op jit(solution)/shard_map/ppermute | solution.py:334
  18.1 3.5 %short.1 = (f32[256,2048]{1,0:T(8,128)S(1)}, f32[128,2048]{1,0:T(8,128)S(1)}, bf16[128,2048]{1,0:T(8,128)(2,1)S(1)}, bf16[128,2048]{1,0:T(8,128)(2,1)S(1)}, f32[16,2048]{1,0:T(8,128)S(1)}) custom-call(f32[256,2048]{1,0:T(8,128)S(1)} %get-tuple-element.77.refs_0_, bf16[128,2048]{1,0:T(8,128)(2,1)S(1)} %collective-permute-done.3.refs_1_, ...), custom_call_target="tpu_custom_call" | custom-call | bytes 1024 | tf_op jit(solution)/shard_map/short/pallas_call | solution.py:300
  21.6 2.0 %collective-permute-done.2.refs_1_ = f32[16,2048]{1,0:T(8,128)S(1)} collective-permute-done((f32[16,2048]{1,0:T(8,128)S(1)}, f32[16,2048]{1,0:T(8,128)S(1)}, u32[]{:S(2)}, u32[]{:S(2)}) %collective-permute-start.2) | collective-permute-done | bytes 131104 | tf_op jit(solution)/shard_map/ppermute | solution.py:334
  23.6 2.2 %long_grad.1 = (bf16[128,2048]{1,0:T(8,128)(2,1)S(1)}, bf16[128,2048]{1,0:T(8,128)(2,1)S(1)}) custom-call(f32[128,2048]{1,0:T(8,128)S(1)} %grad_local.1.refs_4_.refs_0_, f32[16,2048]{1,0:T(8,128)S(1)} %merge.5.refs_1_, f32[16,2048]{1,0:T(8,128)S(1)} %get-tuple-element.64.refs_8_.refs_2_.refs_0_.refs_5_.refs_3_, ...), custom_call_target="tpu_custom_call" | custom-call | bytes 1024 | tf_op jit(solution)/shard_map/long_grad/pallas_call | solution.py:300
  25.8 1.5 %collective-permute-start.10 = (bf16[128,2048]{1,0:T(8,128)(2,1)S(1)}, bf16[128,2048]{1,0:T(8,128)(2,1)S(1)}, u32[]{:S(2)}, u32[]{:S(2)}) collective-permute-start(bf16[128,2048]{1,0:T(8,128)(2,1)S(1)} %get-tuple-element.82.refs_0_), channel_id=1, source_target_pairs={{4,0},{8,4},{12,8},{16,12},{20,16},{24,20},{28,24},{5,1},{9,5},{13... | collective-permute-start | bytes 1572872 | tf_op jit(solution)/shard_map/ppermute | solution.py:329
  27.2 1.7 %taps.1 = (f32[256,2048]{1,0:T(8,128)S(1)}, bf16[128,2048]{1,0:T(8,128)(2,1)S(1)}) custom-call(bf16[128,2048]{1,0:T(8,128)(2,1)S(1)} %get-tuple-element.82.refs_0_, f32[256,2048]{1,0:T(8,128)S(1)} %get-tuple-element.83.refs_1_, bf16[256,256]{1,0:T(8,128)(2,1)S(1)} %get-tuple-element.73.refs_3_.refs_2_, ...), custom_call_target="tpu_custom_call" | custom-call | bytes 1024 | tf_op jit(solution)/shard_map/taps/pallas_call | solution.py:300
  29.1 1.2 %collective-permute-start.5 = (bf16[128,256]{1,0:T(8,128)(2,1)S(1)}, bf16[128,256]{1,0:T(8,128)(2,1)S(1)}, u32[]{:S(2)}, u32[]{:S(2)}) collective-permute-start(bf16[128,256]{1,0:T(8,128)(2,1)S(1)} %get-tuple-element.88), channel_id=1, source_target_pairs={{0,4},{4,0},{8,12},{12,8},{16,20},{20,16},{24,28},{28,24},{1,5},{5... | collective-permute-start | bytes 196616 | tf_op jit(solution)/shard_map/ppermute | solution.py:334
  32.6 1.6 %collective-permute-start.9 = (bf16[224,384]{1,0:T(8,128)(2,1)S(1)}, bf16[224,384]{1,0:T(8,128)(2,1)S(1)}, u32[]{:S(2)}, u32[]{:S(2)}) collective-permute-start(bf16[224,384]{1,0:T(8,128)(2,1)S(1)} %get-tuple-element.92.refs_0_), channel_id=1, source_target_pairs={{0,8},{4,12},{8,0},{12,4},{16,24},{20,28},{24,16},{28,20},{1,9},{5... | collective-permute-start | bytes 516104 | tf_op jit(solution)/shard_map/ppermute | solution.py:334
  34.7 2.9 %input_grad.1 = (bf16[128,2048]{1,0:T(8,128)(2,1)}, bf16[128,2048]{1,0:T(8,128)(2,1)}, bf16[128,2048]{1,0:T(8,128)(2,1)}, bf16[128,2048]{1,0:T(8,128)(2,1)}, f32[8,2048]{1,0:T(8,128)S(1)}) custom-call(bf16[128,2048]{1,0:T(8,128)(2,1)S(1)} %collective-permute-done.10.refs_0_, f32[256,2048]{1,0:T(8,128)S(1)} %get-tuple-element.94.refs_1_, ...), custom_call_target="tpu_custom_call" | custom-call | bytes 1024 | tf_op jit(solution)/shard_map/input_grad/pallas_call | solution.py:300
  37.7 2.5 %collective-permute-done.9.refs_1_ = bf16[224,384]{1,0:T(8,128)(2,1)S(1)} collective-permute-done((bf16[224,384]{1,0:T(8,128)(2,1)S(1)}, bf16[224,384]{1,0:T(8,128)(2,1)S(1)}, u32[]{:S(2)}, u32[]{:S(2)}) %collective-permute-start.9) | collective-permute-done | bytes 172064 | tf_op jit(solution)/shard_map/ppermute | solution.py:334
  40.8 1.1 %collective-permute-start.13 = (bf16[128,640]{1,0:T(8,128)(2,1)S(1)}, bf16[128,640]{1,0:T(8,128)(2,1)S(1)}, u32[]{:S(2)}, u32[]{:S(2)}) collective-permute-start(bf16[128,640]{1,0:T(8,128)(2,1)S(1)} %go_right.1.refs_2_), channel_id=1, source_target_pairs={{0,8},{4,12},{8,0},{12,4},{16,24},{20,28},{24,16},{28,20},{1,9},{5... | collective-permute-start | bytes 491528 | tf_op jit(solution)/shard_map/ppermute | solution.py:334
  41.8 1.7 %long_local.1.refs_7_.refs_2_ = f32[128,2048]{1,0:T(8,128)S(1)} custom-call(bf16[128,2048]{1,0:T(8,128)(2,1)S(1)} %get-tuple-element.104.refs_0_, f32[256,2048]{1,0:T(8,128)S(1)} %filter.1.refs_2_.refs_1_, bf16[256,256]{1,0:T(8,128)(2,1)S(1)} %get-tuple-element.73.refs_3_.refs_2_, bf16[256,256]{1,0:T(8,128)(2,1)S(1)} %get-tuple-element.69.refs_4_.refs_7_.refs_3_.refs_10_), custom_call_target="tpu_custom_call" | custom-call | bytes 1024 | tf_op jit(solution)/shard_map/long_local/pallas_call | solution.py:300
  43.5 2.9 %collective-permute-done.13.refs_3_ = bf16[128,640]{1,0:T(8,128)(2,1)S(1)} collective-permute-done((bf16[128,640]{1,0:T(8,128)(2,1)S(1)}, bf16[128,640]{1,0:T(8,128)(2,1)S(1)}, u32[]{:S(2)}, u32[]{:S(2)}) %collective-permute-start.13) | collective-permute-done | bytes 163872 | tf_op jit(solution)/shard_map/ppermute | solution.py:334
  46.6 1.6 %gated_own.1 = (bf16[128,2048]{1,0:T(8,128)(2,1)}, bf16[128,2048]{1,0:T(8,128)(2,1)}) custom-call(f32[16,1024]{1,0:T(8,128)S(1)} %get-tuple-element.107.refs_0_, f32[16,2048]{1,0:T(8,128)S(1)} %get-tuple-element.106.refs_1_, f32[128,2048]{1,0:T(8,128)S(1)} %long_local.1.refs_7_.refs_2_, ...), custom_call_target="tpu_custom_call" | custom-call | bytes 1024 | tf_op jit(solution)/shard_map/gated_own/pallas_call | solution.py:535
  48.3 1.7 %gated_other.1 = (bf16[128,2048]{1,0:T(8,128)(2,1)}, bf16[128,2048]{1,0:T(8,128)(2,1)}, f32[128,2048]{1,0:T(8,128)}) custom-call(bf16[160,1024]{1,0:T(8,128)(2,1)S(1)} %collective-permute-done.14.refs_0_, f32[16,2048]{1,0:T(8,128)S(1)} %get-tuple-element.106.refs_1_, ...), custom_call_target="tpu_custom_call", output_to_operand_aliasing={{0}: (8, {}), {1}: (9, {})} | custom-call | bytes 1024 | tf_op jit(solution)/shard_map/gated_other/pallas_call | solution.py:535
  (26 shorter events, 4.0 us)
Async XLA Ops:
  2.5 15.6 %collective-permute-start.3 = (bf16[128,2048]{1,0:T(8,128)(2,1)S(1)}, bf16[128,2048]{1,0:T(8,128)(2,1)S(1)}, u32[]{:S(2)}, u32[]{:S(2)}) collective-permute-start(bf16[128,2048]{1,0:T(8,128)(2,1)S(1)} %get-tuple-element.72.refs_1_), channel_id=1, source_target_pairs={{0,4},{4,8},{8,12},{12,16},{16,20},{20,24},{24,28},{1,5},{5,9},{9,... | collective-permute-start | bytes 1572872 | tf_op jit(solution)/shard_map/ppermute | solution.py:329
  6.9 3.6 %collective-permute-start = (f32[16,2048]{1,0:T(8,128)S(1)}, f32[16,2048]{1,0:T(8,128)S(1)}, u32[]{:S(2)}, u32[]{:S(2)}) collective-permute-start(f32[16,2048]{1,0:T(8,128)S(1)} %get-tuple-element.67.refs_0_), channel_id=1, source_target_pairs={{0,4},{4,0},{8,12},{12,8},{16,20},{20,16},{24,28},{28,24},{1,5},{5... | collective-permute-start | bytes 393224 | tf_op jit(solution)/shard_map/ppermute | solution.py:334
  10.6 6.5 %collective-permute-start.1 = (f32[16,2048]{1,0:T(8,128)S(1)}, f32[16,2048]{1,0:T(8,128)S(1)}, u32[]{:S(2)}, u32[]{:S(2)}) collective-permute-start(f32[16,2048]{1,0:T(8,128)S(1)} %get-tuple-element.68.refs_3_.refs_0_), channel_id=1, source_target_pairs={{0,8},{4,12},{8,0},{12,4},{16,24},{20,28},{24,16},{28,20},{1,9},{5... | collective-permute-start | bytes 393224 | tf_op jit(solution)/shard_map/ppermute | solution.py:334
  17.2 6.3 %collective-permute-start.2 = (f32[16,2048]{1,0:T(8,128)S(1)}, f32[16,2048]{1,0:T(8,128)S(1)}, u32[]{:S(2)}, u32[]{:S(2)}) collective-permute-start(f32[16,2048]{1,0:T(8,128)S(1)} %get-tuple-element.75.refs_8_.refs_0_), channel_id=1, source_target_pairs={{0,16},{4,20},{8,24},{12,28},{16,0},{20,4},{24,8},{28,12},{1,17},{... | collective-permute-start | bytes 393224 | tf_op jit(solution)/shard_map/ppermute | solution.py:334
  25.8 8.9 %collective-permute-start.10 = (bf16[128,2048]{1,0:T(8,128)(2,1)S(1)}, bf16[128,2048]{1,0:T(8,128)(2,1)S(1)}, u32[]{:S(2)}, u32[]{:S(2)}) collective-permute-start(bf16[128,2048]{1,0:T(8,128)(2,1)S(1)} %get-tuple-element.82.refs_0_), channel_id=1, source_target_pairs={{4,0},{8,4},{12,8},{16,12},{20,16},{24,20},{28,24},{5,1},{9,5},{13... | collective-permute-start | bytes 1572872 | tf_op jit(solution)/shard_map/ppermute | solution.py:329
  29.1 2.1 %collective-permute-start.5 = (bf16[128,256]{1,0:T(8,128)(2,1)S(1)}, bf16[128,256]{1,0:T(8,128)(2,1)S(1)}, u32[]{:S(2)}, u32[]{:S(2)}) collective-permute-start(bf16[128,256]{1,0:T(8,128)(2,1)S(1)} %get-tuple-element.88), channel_id=1, source_target_pairs={{0,4},{4,0},{8,12},{12,8},{16,20},{20,16},{24,28},{28,24},{1,5},{5... | collective-permute-start | bytes 196616 | tf_op jit(solution)/shard_map/ppermute | solution.py:334
  30.3 2.2 %collective-permute-start.4 = (bf16[64,1024]{1,0:T(8,128)(2,1)S(1)}, bf16[64,1024]{1,0:T(8,128)(2,1)S(1)}, u32[]{:S(2)}, u32[]{:S(2)}) collective-permute-start(bf16[64,1024]{1,0:T(8,128)(2,1)S(1)} %get-tuple-element.87), channel_id=1, source_target_pairs={{0,4},{4,0},{8,12},{12,8},{16,20},{20,16},{24,28},{28,24},{1,5},{5... | collective-permute-start | bytes 393224 | tf_op jit(solution)/shard_map/ppermute | solution.py:334
  30.3 1.4 %collective-permute-start.6 = (bf16[128,256]{1,0:T(8,128)(2,1)S(1)}, bf16[128,256]{1,0:T(8,128)(2,1)S(1)}, u32[]{:S(2)}, u32[]{:S(2)}) collective-permute-start(bf16[128,256]{1,0:T(8,128)(2,1)S(1)} %get-tuple-element.89), channel_id=1, source_target_pairs={{0,4},{4,0},{8,12},{12,8},{16,20},{20,16},{24,28},{28,24},{1,5},{5... | collective-permute-start | bytes 196616 | tf_op jit(solution)/shard_map/ppermute | solution.py:334
  30.8 1.3 %collective-permute-start.7 = (bf16[128,256]{1,0:T(8,128)(2,1)S(1)}, bf16[128,256]{1,0:T(8,128)(2,1)S(1)}, u32[]{:S(2)}, u32[]{:S(2)}) collective-permute-start(bf16[128,256]{1,0:T(8,128)(2,1)S(1)} %get-tuple-element.90), channel_id=1, source_target_pairs={{0,4},{4,0},{8,12},{12,8},{16,20},{20,16},{24,28},{28,24},{1,5},{5... | collective-permute-start | bytes 196616 | tf_op jit(solution)/shard_map/ppermute | solution.py:334
  31.2 1.3 %collective-permute-start.8 = (bf16[128,256]{1,0:T(8,128)(2,1)S(1)}, bf16[128,256]{1,0:T(8,128)(2,1)S(1)}, u32[]{:S(2)}, u32[]{:S(2)}) collective-permute-start(bf16[128,256]{1,0:T(8,128)(2,1)S(1)} %get-tuple-element.91), channel_id=1, source_target_pairs={{0,4},{4,0},{8,12},{12,8},{16,20},{20,16},{24,28},{28,24},{1,5},{5... | collective-permute-start | bytes 196616 | tf_op jit(solution)/shard_map/ppermute | solution.py:334
  32.6 7.6 %collective-permute-start.9 = (bf16[224,384]{1,0:T(8,128)(2,1)S(1)}, bf16[224,384]{1,0:T(8,128)(2,1)S(1)}, u32[]{:S(2)}, u32[]{:S(2)}) collective-permute-start(bf16[224,384]{1,0:T(8,128)(2,1)S(1)} %get-tuple-element.92.refs_0_), channel_id=1, source_target_pairs={{0,8},{4,12},{8,0},{12,4},{16,24},{20,28},{24,16},{28,20},{1,9},{5... | collective-permute-start | bytes 516104 | tf_op jit(solution)/shard_map/ppermute | solution.py:334
  34.1 6.6 %collective-permute-start.12 = (bf16[128,640]{1,0:T(8,128)(2,1)S(1)}, bf16[128,640]{1,0:T(8,128)(2,1)S(1)}, u32[]{:S(2)}, u32[]{:S(2)}) collective-permute-start(bf16[128,640]{1,0:T(8,128)(2,1)S(1)} %get-tuple-element.101.refs_0_), channel_id=1, source_target_pairs={{0,16},{4,20},{8,24},{12,28},{16,0},{20,4},{24,8},{28,12},{1,17},{... | collective-permute-start | bytes 491528 | tf_op jit(solution)/shard_map/ppermute | solution.py:334
  40.2 6.2 %collective-permute-start.11 = (bf16[224,384]{1,0:T(8,128)(2,1)S(1)}, bf16[224,384]{1,0:T(8,128)(2,1)S(1)}, u32[]{:S(2)}, u32[]{:S(2)}) collective-permute-start(bf16[224,384]{1,0:T(8,128)(2,1)S(1)} %get-tuple-element.100.refs_0_), channel_id=1, source_target_pairs={{0,16},{4,20},{8,24},{12,28},{16,0},{20,4},{24,8},{28,12},{1,17},{... | collective-permute-start | bytes 516104 | tf_op jit(solution)/shard_map/ppermute | solution.py:334
  40.8 5.7 %collective-permute-start.13 = (bf16[128,640]{1,0:T(8,128)(2,1)S(1)}, bf16[128,640]{1,0:T(8,128)(2,1)S(1)}, u32[]{:S(2)}, u32[]{:S(2)}) collective-permute-start(bf16[128,640]{1,0:T(8,128)(2,1)S(1)} %go_right.1.refs_2_), channel_id=1, source_target_pairs={{0,8},{4,12},{8,0},{12,4},{16,24},{20,28},{24,16},{28,20},{1,9},{5... | collective-permute-start | bytes 491528 | tf_op jit(solution)/shard_map/ppermute | solution.py:334
  46.6 1.7 %collective-permute-start.14 = (bf16[160,1024]{1,0:T(8,128)(2,1)S(1)}, bf16[160,1024]{1,0:T(8,128)(2,1)S(1)}, u32[]{:S(2)}, u32[]{:S(2)}) collective-permute-start(bf16[160,1024]{1,0:T(8,128)(2,1)S(1)} %get-tuple-element.105.refs_7_), channel_id=1, source_target_pairs={{0,4},{4,0},{8,12},{12,8},{16,20},{20,16},{24,28},{28,24},{1,5},{5... | collective-permute-start | bytes 983048 | tf_op jit(solution)/shard_map/ppermute | solution.py:334

commit v5 on v4

--- a/solution.py
+++ b/solution.py
@@ -339,23 +339,46 @@
     return [1 << bit for bit in range(size.bit_length() - 1)]
 
 
-def merge_states(total, other, got, rate, block, mask, last, after):
+def chip_states(state, other, rate, block):
+    def body(state, other, rate, chip):
+        first = lax.rem(lax.axis_index("ctx"), 2) == 0
+        own, theirs, fade = state[...], other[...], jnp.exp(-block * rate[...])
+        chip[...] = jnp.where(first, own + fade * theirs, theirs + fade * own)
+
+    return small(body, "chip_states", [state, other, rate], [(state.shape, jnp.float32)])[0]
+
+
+def column_states(total, other, got, chip, rate, block, mask, last, after):
     def body(*refs):
-        other, rate = refs[1][...], refs[2][...]
+        total, other, rate = refs[0][...], refs[1][...], refs[2][...]
+        refs = refs[3:]
         me = lax.axis_index("ctx")
         takes = lax.rem(lax.div(me, mask), 2) == 0
-        steps = mask - 1 - lax.rem(me, mask)
-        taken = jnp.where(takes, jnp.exp((-block * steps).astype(jnp.float32) * rate) * other, 0.0)
-        refs[-1][...] = taken if got is None else refs[3][...] + taken
-        if not last:
-            own = refs[0][...]
+        steps = mask - 4 - lax.div(lax.rem(me, mask), 4) * 4
+        reached = jnp.where(takes, jnp.exp((-block * steps).astype(jnp.float32) * rate) * other, 0.0)
+        if got is not None:
+            reached = reached + refs[0][...]
+        refs[-1][...] = reached
+        if last:
+            chip = refs[-3][...]
+            later = lax.rem(lax.div(me, 2), 2) == 1
+            refs[-2][...] = jnp.where(later, chip + jnp.exp(-4 * block * rate) * reached, reached)
+        else:
             fade = jnp.exp(-(block * mask) * rate)
-            refs[-2][...] = jnp.where(takes, own + fade * other, other + fade * own)
-
-    operands = [total, other, rate] + ([] if got is None else [got])
-    outs = [(total.shape, jnp.float32)] * (1 if last else 2)
-    merged = small(body, "merge", operands, outs, after)
-    return (total, merged[0]) if last else merged
+            refs[-2][...] = jnp.where(takes, total + fade * other, other + fade * total)
+
+    operands = [total, other, rate] + ([] if got is None else [got]) + ([chip] if last else [])
+    return small(body, "column_states", operands, [(total.shape, jnp.float32)] * 2, after)
+
+
+def far_states(column, other, near, rate, block, after):
+    def body(column, other, near, rate, out):
+        pace = rate[...]
+        far = jnp.exp(-2 * block * pace) * column[...] + other[...]
+        first = lax.rem(lax.axis_index("ctx"), 2) == 0
+        out[...] = jnp.where(first, near[...] + jnp.exp(-block * pace) * far, far)
+
+    return small(body, "far_states", [column, other, near, rate], [(column.shape, jnp.float32)], after)[0]
 
 
 def pack(out, row, value):
@@ -564,75 +587,85 @@
     matrices = [jnp.asarray(t) for t in tables(block)]
     width = min(512, channels)
 
-    (ks, vs, rate, ct, ql), (short_in,) = load(
-        [key_short, value_short, long_rate, cotangent, query_long],
-        [((block, channels), half)],
-        product_kernel,
-        "product",
-        2,
-        width,
+    (ks, vs), (short_in,) = load(
+        [key_short, value_short], [((block, channels), half)], product_kernel, "product", 2, width
     )
     halo = shifted(short_in, 1)
-    (res, own_three, qs, kl, taps, own_two, nxt_two, back), (total,) = load(
-        [long_residue, matrices[1], query_short, key_long, short_taps, matrices[0], matrices[2], matrices[3]],
+    (rate, ct, ql, res, own_three, qs, kl, taps, own_two, nxt_two, back), (total,) = load(
+        [
+            long_rate,
+            cotangent,
+            query_long,
+            long_residue,
+            matrices[1],
+            query_short,
+            key_long,
+            short_taps,
+            matrices[0],
+            matrices[2],
+            matrices[3],
+        ],
         [((modes, channels), full)],
         first_kernel,
         "states",
-        0,
-        width,
-        blocked=[rate, ct, ql],
-    )
-    far, steps = None, masks()
-    for at, mask in enumerate(steps):
-        other = swapped(total, mask)
-        beside = []
-        if at == 1:
-            (long_spec,) = run(
-                filter_kernel,
-                "filter",
-                [rate, res],
-                [own_three],
-                [(2 * block, full, "vmem")],
-                width,
-                [(block, full)],
-                [total],
-            )
-            (grad_local,) = run(
-                grad_local_kernel,
-                "grad_local",
-                [ql, ct, long_spec],
-                [own_three, back],
-                [(block, full, "vmem")],
-                width,
-            )
-            short_spec, own_spec = run(
-                short_filter_kernel,
-                "short_filter",
-                [taps, short_in],
-                [own_three, own_two],
-                [(2 * block, full, "vmem"), (2 * block, full, "vmem")],
-                width,
-            )
-            beside = [grad_local, short_spec]
-        if at == 2:
-            in_spec, short_mix, hidden, long_in, fore_state = run(
-                short_kernel,
-                "short",
-                [own_spec, halo, short_spec, qs, kl, rate],
-                [nxt_two, back],
-                [
-                    (2 * block, full, "vmem"),
-                    (block, full, "vmem"),
-                    (block, half, "vmem"),
-                    (block, half, "vmem"),
-                    (modes, full, "vmem"),
-                ],
-                width,
-                (),
-                [total],
-            )
-            beside = [hidden]
-        total, far = merge_states(total, other, far, rate, block, mask, at == len(steps) - 1, beside)
+        3,
+        width,
+        [short_in],
+    )
+    near = swapped(total, 1)
+    chip = chip_states(total, near, rate, block)
+    total, column, rest = chip, None, masks()[2:]
+    other = swapped(total, rest[0])
+    (long_spec,) = run(
+        filter_kernel,
+        "filter",
+        [rate, res],
+        [own_three],
+        [(2 * block, full, "vmem")],
+        width,
+        [(block, full)],
+        [chip],
+    )
+    (grad_local,) = run(
+        grad_local_kernel,
+        "grad_local",
+        [ql, ct, long_spec],
+        [own_three, back],
+        [(block, full, "vmem")],
+        width,
+    )
+    short_spec, own_spec = run(
+        short_filter_kernel,
+        "short_filter",
+        [taps, short_in],
+        [own_three, own_two],
+        [(2 * block, full, "vmem"), (2 * block, full, "vmem")],
+        width,
+    )
+    for at, mask in enumerate(rest):
+        if at > 0:
+            other = swapped(total, mask)
+        last = at == len(rest) - 1
+        beside = [grad_local, short_spec] if at == 0 else []
+        total, column = column_states(total, other, column, chip, rate, block, mask, last, beside)
+    other = swapped(total, 2)
+    in_spec, short_mix, hidden, long_in, fore_state = run(
+        short_kernel,
+        "short",
+        [own_spec, halo, short_spec, qs, kl, rate],
+        [nxt_two, back],
+        [
+            (2 * block, full, "vmem"),
+            (block, full, "vmem"),
+            (block, half, "vmem"),
+            (block, half, "vmem"),
+            (modes, full, "vmem"),
+        ],
+        width,
+        (),
+        [total],
+    )
+    far = far_states(column, other, near, rate, block, [hidden])
     long_grad, short_back = run(
         long_grad_kernel,
         "long_grad",

time: 50.3 us -> 50.2 us (level)
  waiting for transfers between devices: 9.69 us -> 7.76 us
  starting transfers between devices: 14.9 us -> 16.2 us
    ppermute x13, waiting for transfers between devices: 9.69 us -> 7.75 us  [swapped(): return lax.ppermute(value, 'ctx', [(i, i ^ mask) for i in range(size)])]
    ppermute x13, starting transfers between devices: 11 us -> 12.3 us  [swapped(): return lax.ppermute(value, 'ctx', [(i, i ^ mask) for i in range(size)])]
    pallas_call x2, Pallas kernels: 3.86 us -> 4.39 us  [load(): pl.pallas_call(whole, in_specs=[pl.BlockSpec(memory_space=pltpu.HBM)] * c...]
  transfers between devices with their start and end apart: 15 -> 15, of which waited for: 8 -> 8; matrix products, arithmetic and copies ran while one was open for 0% -> 0% of each run, Pallas kernels for 37% -> 39%
where the time goes in v5:
time: 50.2 us; the launch traced here: 50 us
  Pallas kernels  25 us (50%)
  starting transfers between devices  16.2 us (32%)
  waiting for transfers between devices  7.76 us (15%)
  between operations  0.96 us (2%)
    pallas_call x8, Pallas kernels, run(): pl.pallas_call(whole, in_specs=[pl.BlockSpec(memory_space=pltpu.VMEM)] *...  16.8 us
    ppermute x13, starting transfers between devices, swapped(): return lax.ppermute(value, 'ctx', [(i, i ^ mask) for i in range(size)])  12.3 us
    ppermute x13, waiting for transfers between devices, swapped(): return lax.ppermute(value, 'ctx', [(i, i ^ mask) for i in range(size)])  7.75 us
    pallas_call x2, Pallas kernels, load(): pl.pallas_call(whole, in_specs=[pl.BlockSpec(memory_space=pltpu.HBM)] * c...  4.39 us
    ppermute x2, starting transfers between devices, shifted(): return lax.ppermute(value, 'ctx', pairs)  3.86 us
    pallas_call x2, Pallas kernels, gated(): pl.pallas_call(body, in_specs=[pl.BlockSpec(memory_space=pltpu.VMEM)] * l...  3.24 us
  transfers between devices with their start and end apart: 15, of which 8 were waited for; matrix products, arithmetic and copies ran while one was open for 0% of the time, Pallas kernels for 39%

profile of v5, /device:TPU:0, one launch (start us, length us, event | category | flops | bytes accessed | tf_op | source)
XLA Modules:
  0.0 50.0 jit_solution(4637779328690611195)
XLA Ops:
  0.6 1.4 %product.1 = (bf16[128,2048]{1,0:T(8,128)(2,1)S(1)}, bf16[128,2048]{1,0:T(8,128)(2,1)S(1)}, bf16[128,2048]{1,0:T(8,128)(2,1)S(1)}) custom-call(bf16[128,2048]{1,0:T(8,128)(2,1)} %refs_0_.2, bf16[128,2048]{1,0:T(8,128)(2,1)} %refs_1_.2), custom_call_target="tpu_custom_call" | custom-call | bytes 1024 | tf_op jit(solution)/shard_map/product/pallas_call | solution.py:183
  2.0 2.4 %collective-permute-start.3 = (bf16[128,2048]{1,0:T(8,128)(2,1)S(1)}, bf16[128,2048]{1,0:T(8,128)(2,1)S(1)}, u32[]{:S(2)}, u32[]{:S(2)}) collective-permute-start(bf16[128,2048]{1,0:T(8,128)(2,1)S(1)} %get-tuple-element.60.refs_11_.refs_1_), channel_id=1, source_target_pairs={{0,4},{4,8},{8,12},{12,16},{16,20},{20,24},{24,28},{1,5},{5,9},{9,... | collective-permute-start | bytes 1572872 | tf_op jit(solution)/shard_map/ppermute | solution.py:329
  4.4 3.0 %states.1 = (f32[16,2048]{1,0:T(8,128)S(1)}, bf16[128,2048]{1,0:T(8,128)(2,1)S(1)}, bf16[128,2048]{1,0:T(8,128)(2,1)S(1)}, f32[16,2048]{1,0:T(8,128)S(1)}, bf16[...) custom-call(f32[16,2048]{1,0:T(8,128)} %refs_0_.3, ...), custom_call_target="tpu_custom_call" | custom-call | bytes 1024 | tf_op jit(solution)/shard_map/states/pallas_call | solution.py:183
  7.4 2.6 %collective-permute-start = (f32[16,2048]{1,0:T(8,128)S(1)}, f32[16,2048]{1,0:T(8,128)S(1)}, u32[]{:S(2)}, u32[]{:S(2)}) collective-permute-start(f32[16,2048]{1,0:T(8,128)S(1)} %get-tuple-element.66.refs_0_), channel_id=1, source_target_pairs={{0,4},{4,0},{8,12},{12,8},{16,20},{20,16},{24,28},{28,24},{1,5},{5... | collective-permute-start | bytes 393224 | tf_op jit(solution)/shard_map/ppermute | solution.py:334
  10.1 1.0 %collective-permute-done.refs_1_.refs_2_ = f32[16,2048]{1,0:T(8,128)S(1)} collective-permute-done((f32[16,2048]{1,0:T(8,128)S(1)}, f32[16,2048]{1,0:T(8,128)S(1)}, u32[]{:S(2)}, u32[]{:S(2)}) %collective-permute-start) | collective-permute-done | bytes 131104 | tf_op jit(solution)/shard_map/ppermute | solution.py:334
  11.1 1.6 %collective-permute-start.1 = (f32[16,2048]{1,0:T(8,128)S(1)}, f32[16,2048]{1,0:T(8,128)S(1)}, u32[]{:S(2)}, u32[]{:S(2)}) collective-permute-start(f32[16,2048]{1,0:T(8,128)S(1)} %chip_states.1.refs_3_.refs_0_), channel_id=1, source_target_pairs={{0,16},{4,20},{8,24},{12,28},{16,0},{20,4},{24,8},{28,12},{1,17},{... | collective-permute-start | bytes 393224 | tf_op jit(solution)/shard_map/ppermute | solution.py:334
  12.7 1.0 %short_filter.1 = (f32[256,2048]{1,0:T(8,128)S(1)}, f32[256,2048]{1,0:T(8,128)S(1)}) custom-call(f32[128,2048]{1,0:T(8,128)S(1)} %get-tuple-element.68.refs_0_, bf16[128,2048]{1,0:T(8,128)(2,1)S(1)} %get-tuple-element.60.refs_11_.refs_1_, bf16[256,384]{1,0:T(8,128)(2,1)S(1)} %get-tuple-element.65.refs_2_.refs_3_, ...), custom_call_target="tpu_custom_call" | custom-call | bytes 1024 | tf_op jit(solution)/shard_map/short_filter/pallas_call | solution.py:300
  13.7 2.0 %filter.1.refs_2_.refs_1_ = f32[256,2048]{1,0:T(8,128)S(1)} custom-call(f32[16,2048]{1,0:T(8,128)S(1)} %get-tuple-element.63.refs_2_.refs_0_.refs_5_.refs_3_, f32[16,2048]{1,0:T(8,128)S(1)} %get-tuple-element.64.refs_1_.refs_3_.refs_4_, bf16[256,384]{1,0:T(8,128)(2,1)S(1)} %get-tuple-element.65.refs_2_.refs_3_, f32[16,2048]{1,0:T(8,128)S(1)} %chip_states.1.refs_3_.refs_0_), custom_call_target="tpu_custom_call" | custom-call | bytes 1024 | tf_op jit(solution)/shard_map/filter/pallas_call | solution.py:300
  15.7 2.0 %grad_local.1.refs_4_.refs_0_ = f32[128,2048]{1,0:T(8,128)S(1)} custom-call(bf16[128,2048]{1,0:T(8,128)(2,1)S(1)} %get-tuple-element.61.refs_0_.refs_5_, bf16[128,2048]{1,0:T(8,128)(2,1)S(1)} %get-tuple-element.62.refs_1_.refs_6_, f32[256,2048]{1,0:T(8,128)S(1)} %filter.1.refs_2_.refs_1_, bf16[256,384]{1,0:T(8,128)(2,1)S(1)} %get-tuple-element.65.refs_2_.refs_3_, ...), custom_call_target="tpu_custom_call" | custom-call | bytes 1024 | tf_op jit(solution)/shard_map/grad_local/pallas_call | solution.py:300
  18.6 3.4 %short.1 = (f32[256,2048]{1,0:T(8,128)S(1)}, f32[128,2048]{1,0:T(8,128)S(1)}, bf16[128,2048]{1,0:T(8,128)(2,1)S(1)}, bf16[128,2048]{1,0:T(8,128)(2,1)S(1)}, f32[16,2048]{1,0:T(8,128)S(1)}) custom-call(f32[256,2048]{1,0:T(8,128)S(1)} %get-tuple-element.73.refs_0_, bf16[128,2048]{1,0:T(8,128)(2,1)S(1)} %collective-permute-done.3.refs_1_, ...), custom_call_target="tpu_custom_call" | custom-call | bytes 1024 | tf_op jit(solution)/shard_map/short/pallas_call | solution.py:300
  22.0 1.3 %collective-permute-done.2.refs_1_ = f32[16,2048]{1,0:T(8,128)S(1)} collective-permute-done((f32[16,2048]{1,0:T(8,128)S(1)}, f32[16,2048]{1,0:T(8,128)S(1)}, u32[]{:S(2)}, u32[]{:S(2)}) %collective-permute-start.2) | collective-permute-done | bytes 131104 | tf_op jit(solution)/shard_map/ppermute | solution.py:334
  23.3 2.2 %long_grad.1 = (bf16[128,2048]{1,0:T(8,128)(2,1)S(1)}, bf16[128,2048]{1,0:T(8,128)(2,1)S(1)}) custom-call(f32[128,2048]{1,0:T(8,128)S(1)} %grad_local.1.refs_4_.refs_0_, f32[16,2048]{1,0:T(8,128)S(1)} %far_states.1.refs_1_, f32[16,2048]{1,0:T(8,128)S(1)} %get-tuple-element.63.refs_2_.refs_0_.refs_5_.refs_3_, ...), custom_call_target="tpu_custom_call" | custom-call | bytes 1024 | tf_op jit(solution)/shard_map/long_grad/pallas_call | solution.py:300
  25.5 1.5 %collective-permute-start.10 = (bf16[128,2048]{1,0:T(8,128)(2,1)S(1)}, bf16[128,2048]{1,0:T(8,128)(2,1)S(1)}, u32[]{:S(2)}, u32[]{:S(2)}) collective-permute-start(bf16[128,2048]{1,0:T(8,128)(2,1)S(1)} %get-tuple-element.78.refs_0_), channel_id=1, source_target_pairs={{4,0},{8,4},{12,8},{16,12},{20,16},{24,20},{28,24},{5,1},{9,5},{13... | collective-permute-start | bytes 1572872 | tf_op jit(solution)/shard_map/ppermute | solution.py:329
  27.0 1.7 %taps.1 = (f32[256,2048]{1,0:T(8,128)S(1)}, bf16[128,2048]{1,0:T(8,128)(2,1)S(1)}) custom-call(bf16[128,2048]{1,0:T(8,128)(2,1)S(1)} %get-tuple-element.78.refs_0_, f32[256,2048]{1,0:T(8,128)S(1)} %get-tuple-element.79.refs_1_, bf16[256,256]{1,0:T(8,128)(2,1)S(1)} %get-tuple-element.69.refs_3_.refs_2_, ...), custom_call_target="tpu_custom_call" | custom-call | bytes 1024 | tf_op jit(solution)/shard_map/taps/pallas_call | solution.py:300
  28.8 1.2 %collective-permute-start.5 = (bf16[128,256]{1,0:T(8,128)(2,1)S(1)}, bf16[128,256]{1,0:T(8,128)(2,1)S(1)}, u32[]{:S(2)}, u32[]{:S(2)}) collective-permute-start(bf16[128,256]{1,0:T(8,128)(2,1)S(1)} %get-tuple-element.84), channel_id=1, source_target_pairs={{0,4},{4,0},{8,12},{12,8},{16,20},{20,16},{24,28},{28,24},{1,5},{5... | collective-permute-start | bytes 196616 | tf_op jit(solution)/shard_map/ppermute | solution.py:334
  33.1 1.5 %collective-permute-start.12 = (bf16[128,640]{1,0:T(8,128)(2,1)S(1)}, bf16[128,640]{1,0:T(8,128)(2,1)S(1)}, u32[]{:S(2)}, u32[]{:S(2)}) collective-permute-start(bf16[128,640]{1,0:T(8,128)(2,1)S(1)} %get-tuple-element.97.refs_0_), channel_id=1, source_target_pairs={{0,16},{4,20},{8,24},{12,28},{16,0},{20,4},{24,8},{28,12},{1,17},{... | collective-permute-start | bytes 491528 | tf_op jit(solution)/shard_map/ppermute | solution.py:334
  34.6 2.9 %input_grad.1 = (bf16[128,2048]{1,0:T(8,128)(2,1)}, bf16[128,2048]{1,0:T(8,128)(2,1)}, bf16[128,2048]{1,0:T(8,128)(2,1)}, bf16[128,2048]{1,0:T(8,128)(2,1)}, f32[8,2048]{1,0:T(8,128)S(1)}) custom-call(bf16[128,2048]{1,0:T(8,128)(2,1)S(1)} %collective-permute-done.10.refs_0_, f32[256,2048]{1,0:T(8,128)S(1)} %get-tuple-element.90.refs_1_, ...), custom_call_target="tpu_custom_call" | custom-call | bytes 1024 | tf_op jit(solution)/shard_map/input_grad/pallas_call | solution.py:300
  37.5 1.6 %collective-permute-done.9.refs_1_ = bf16[224,384]{1,0:T(8,128)(2,1)S(1)} collective-permute-done((bf16[224,384]{1,0:T(8,128)(2,1)S(1)}, bf16[224,384]{1,0:T(8,128)(2,1)S(1)}, u32[]{:S(2)}, u32[]{:S(2)}) %collective-permute-start.9) | collective-permute-done | bytes 172064 | tf_op jit(solution)/shard_map/ppermute | solution.py:334
  39.2 1.5 %collective-permute-start.11 = (bf16[224,384]{1,0:T(8,128)(2,1)S(1)}, bf16[224,384]{1,0:T(8,128)(2,1)S(1)}, u32[]{:S(2)}, u32[]{:S(2)}) collective-permute-start(bf16[224,384]{1,0:T(8,128)(2,1)S(1)} %get-tuple-element.96.refs_0_), channel_id=1, source_target_pairs={{0,16},{4,20},{8,24},{12,28},{16,0},{20,4},{24,8},{28,12},{1,17},{... | collective-permute-start | bytes 516104 | tf_op jit(solution)/shard_map/ppermute | solution.py:334
  40.8 1.3 %collective-permute-start.13 = (bf16[128,640]{1,0:T(8,128)(2,1)S(1)}, bf16[128,640]{1,0:T(8,128)(2,1)S(1)}, u32[]{:S(2)}, u32[]{:S(2)}) collective-permute-start(bf16[128,640]{1,0:T(8,128)(2,1)S(1)} %go_right.1.refs_2_), channel_id=1, source_target_pairs={{0,8},{4,12},{8,0},{12,4},{16,24},{20,28},{24,16},{28,20},{1,9},{5... | collective-permute-start | bytes 491528 | tf_op jit(solution)/shard_map/ppermute | solution.py:334
  42.1 1.7 %long_local.1.refs_7_.refs_2_ = f32[128,2048]{1,0:T(8,128)S(1)} custom-call(bf16[128,2048]{1,0:T(8,128)(2,1)S(1)} %get-tuple-element.100.refs_0_, f32[256,2048]{1,0:T(8,128)S(1)} %filter.1.refs_2_.refs_1_, bf16[256,256]{1,0:T(8,128)(2,1)S(1)} %get-tuple-element.69.refs_3_.refs_2_, bf16[256,256]{1,0:T(8,128)(2,1)S(1)} %get-tuple-element.67.refs_4_.refs_7_.refs_3_.refs_10_), custom_call_target="tpu_custom_call" | custom-call | bytes 1024 | tf_op jit(solution)/shard_map/long_local/pallas_call | solution.py:300
  43.7 2.6 %collective-permute-done.13.refs_3_ = bf16[128,640]{1,0:T(8,128)(2,1)S(1)} collective-permute-done((bf16[128,640]{1,0:T(8,128)(2,1)S(1)}, bf16[128,640]{1,0:T(8,128)(2,1)S(1)}, u32[]{:S(2)}, u32[]{:S(2)}) %collective-permute-start.13) | collective-permute-done | bytes 163872 | tf_op jit(solution)/shard_map/ppermute | solution.py:334
  46.5 1.6 %gated_own.1 = (bf16[128,2048]{1,0:T(8,128)(2,1)}, bf16[128,2048]{1,0:T(8,128)(2,1)}) custom-call(f32[16,1024]{1,0:T(8,128)S(1)} %get-tuple-element.103.refs_0_, f32[16,2048]{1,0:T(8,128)S(1)} %get-tuple-element.102.refs_1_, f32[128,2048]{1,0:T(8,128)S(1)} %long_local.1.refs_7_.refs_2_, f32[16,2048]{1,0:T(8,128)S(1)} %get-tuple-element.63.refs_2_.refs_0_.refs_5_.refs_3_, ...), custom_call_target="tpu_custom_call" | custom-call | bytes 1024 | tf_op jit(solution)/shard_map/gated_own/pallas_call | solution.py:558
  48.1 1.7 %gated_other.1 = (bf16[128,2048]{1,0:T(8,128)(2,1)}, bf16[128,2048]{1,0:T(8,128)(2,1)}, f32[128,2048]{1,0:T(8,128)}) custom-call(bf16[160,1024]{1,0:T(8,128)(2,1)S(1)} %collective-permute-done.14.refs_0_, f32[16,2048]{1,0:T(8,128)S(1)} %get-tuple-element.102.refs_1_, ...), custom_call_target="tpu_custom_call", output_to_operand_aliasing={{0}: (8, {}), {1}: (9, {})} | custom-call | bytes 1024 | tf_op jit(solution)/shard_map/gated_other/pallas_call | solution.py:558
  (26 shorter events, 4.5 us)
Async XLA Ops:
  2.0 16.5 %collective-permute-start.3 = (bf16[128,2048]{1,0:T(8,128)(2,1)S(1)}, bf16[128,2048]{1,0:T(8,128)(2,1)S(1)}, u32[]{:S(2)}, u32[]{:S(2)}) collective-permute-start(bf16[128,2048]{1,0:T(8,128)(2,1)S(1)} %get-tuple-element.60.refs_11_.refs_1_), channel_id=1, source_target_pairs={{0,4},{4,8},{8,12},{12,16},{16,20},{20,24},{24,28},{1,5},{5,9},{9,... | collective-permute-start | bytes 1572872 | tf_op jit(solution)/shard_map/ppermute | solution.py:329
  7.4 3.6 %collective-permute-start = (f32[16,2048]{1,0:T(8,128)S(1)}, f32[16,2048]{1,0:T(8,128)S(1)}, u32[]{:S(2)}, u32[]{:S(2)}) collective-permute-start(f32[16,2048]{1,0:T(8,128)S(1)} %get-tuple-element.66.refs_0_), channel_id=1, source_target_pairs={{0,4},{4,0},{8,12},{12,8},{16,20},{20,16},{24,28},{28,24},{1,5},{5... | collective-permute-start | bytes 393224 | tf_op jit(solution)/shard_map/ppermute | solution.py:334
  11.1 6.5 %collective-permute-start.1 = (f32[16,2048]{1,0:T(8,128)S(1)}, f32[16,2048]{1,0:T(8,128)S(1)}, u32[]{:S(2)}, u32[]{:S(2)}) collective-permute-start(f32[16,2048]{1,0:T(8,128)S(1)} %chip_states.1.refs_3_.refs_0_), channel_id=1, source_target_pairs={{0,16},{4,20},{8,24},{12,28},{16,0},{20,4},{24,8},{28,12},{1,17},{... | collective-permute-start | bytes 393224 | tf_op jit(solution)/shard_map/ppermute | solution.py:334
  17.7 5.6 %collective-permute-start.2 = (f32[16,2048]{1,0:T(8,128)S(1)}, f32[16,2048]{1,0:T(8,128)S(1)}, u32[]{:S(2)}, u32[]{:S(2)}) collective-permute-start(f32[16,2048]{1,0:T(8,128)S(1)} %get-tuple-element.72.refs_8_), channel_id=1, source_target_pairs={{0,8},{4,12},{8,0},{12,4},{16,24},{20,28},{24,16},{28,20},{1,9},{5... | collective-permute-start | bytes 393224 | tf_op jit(solution)/shard_map/ppermute | solution.py:334
  25.5 9.1 %collective-permute-start.10 = (bf16[128,2048]{1,0:T(8,128)(2,1)S(1)}, bf16[128,2048]{1,0:T(8,128)(2,1)S(1)}, u32[]{:S(2)}, u32[]{:S(2)}) collective-permute-start(bf16[128,2048]{1,0:T(8,128)(2,1)S(1)} %get-tuple-element.78.refs_0_), channel_id=1, source_target_pairs={{4,0},{8,4},{12,8},{16,12},{20,16},{24,20},{28,24},{5,1},{9,5},{13... | collective-permute-start | bytes 1572872 | tf_op jit(solution)/shard_map/ppermute | solution.py:329
  28.8 2.1 %collective-permute-start.5 = (bf16[128,256]{1,0:T(8,128)(2,1)S(1)}, bf16[128,256]{1,0:T(8,128)(2,1)S(1)}, u32[]{:S(2)}, u32[]{:S(2)}) collective-permute-start(bf16[128,256]{1,0:T(8,128)(2,1)S(1)} %get-tuple-element.84), channel_id=1, source_target_pairs={{0,4},{4,0},{8,12},{12,8},{16,20},{20,16},{24,28},{28,24},{1,5},{5... | collective-permute-start | bytes 196616 | tf_op jit(solution)/shard_map/ppermute | solution.py:334
  30.0 2.2 %collective-permute-start.4 = (bf16[64,1024]{1,0:T(8,128)(2,1)S(1)}, bf16[64,1024]{1,0:T(8,128)(2,1)S(1)}, u32[]{:S(2)}, u32[]{:S(2)}) collective-permute-start(bf16[64,1024]{1,0:T(8,128)(2,1)S(1)} %get-tuple-element.83), channel_id=1, source_target_pairs={{0,4},{4,0},{8,12},{12,8},{16,20},{20,16},{24,28},{28,24},{1,5},{5... | collective-permute-start | bytes 393224 | tf_op jit(solution)/shard_map/ppermute | solution.py:334
  30.1 1.4 %collective-permute-start.6 = (bf16[128,256]{1,0:T(8,128)(2,1)S(1)}, bf16[128,256]{1,0:T(8,128)(2,1)S(1)}, u32[]{:S(2)}, u32[]{:S(2)}) collective-permute-start(bf16[128,256]{1,0:T(8,128)(2,1)S(1)} %get-tuple-element.85), channel_id=1, source_target_pairs={{0,4},{4,0},{8,12},{12,8},{16,20},{20,16},{24,28},{28,24},{1,5},{5... | collective-permute-start | bytes 196616 | tf_op jit(solution)/shard_map/ppermute | solution.py:334
  30.5 1.3 %collective-permute-start.7 = (bf16[128,256]{1,0:T(8,128)(2,1)S(1)}, bf16[128,256]{1,0:T(8,128)(2,1)S(1)}, u32[]{:S(2)}, u32[]{:S(2)}) collective-permute-start(bf16[128,256]{1,0:T(8,128)(2,1)S(1)} %get-tuple-element.86), channel_id=1, source_target_pairs={{0,4},{4,0},{8,12},{12,8},{16,20},{20,16},{24,28},{28,24},{1,5},{5... | collective-permute-start | bytes 196616 | tf_op jit(solution)/shard_map/ppermute | solution.py:334
  30.9 1.3 %collective-permute-start.8 = (bf16[128,256]{1,0:T(8,128)(2,1)S(1)}, bf16[128,256]{1,0:T(8,128)(2,1)S(1)}, u32[]{:S(2)}, u32[]{:S(2)}) collective-permute-start(bf16[128,256]{1,0:T(8,128)(2,1)S(1)} %get-tuple-element.87), channel_id=1, source_target_pairs={{0,4},{4,0},{8,12},{12,8},{16,20},{20,16},{24,28},{28,24},{1,5},{5... | collective-permute-start | bytes 196616 | tf_op jit(solution)/shard_map/ppermute | solution.py:334
  32.3 6.8 %collective-permute-start.9 = (bf16[224,384]{1,0:T(8,128)(2,1)S(1)}, bf16[224,384]{1,0:T(8,128)(2,1)S(1)}, u32[]{:S(2)}, u32[]{:S(2)}) collective-permute-start(bf16[224,384]{1,0:T(8,128)(2,1)S(1)} %get-tuple-element.88.refs_0_), channel_id=1, source_target_pairs={{0,8},{4,12},{8,0},{12,4},{16,24},{20,28},{24,16},{28,20},{1,9},{5... | collective-permute-start | bytes 516104 | tf_op jit(solution)/shard_map/ppermute | solution.py:334
  33.1 7.7 %collective-permute-start.12 = (bf16[128,640]{1,0:T(8,128)(2,1)S(1)}, bf16[128,640]{1,0:T(8,128)(2,1)S(1)}, u32[]{:S(2)}, u32[]{:S(2)}) collective-permute-start(bf16[128,640]{1,0:T(8,128)(2,1)S(1)} %get-tuple-element.97.refs_0_), channel_id=1, source_target_pairs={{0,16},{4,20},{8,24},{12,28},{16,0},{20,4},{24,8},{28,12},{1,17},{... | collective-permute-start | bytes 491528 | tf_op jit(solution)/shard_map/ppermute | solution.py:334
  39.2 7.1 %collective-permute-start.11 = (bf16[224,384]{1,0:T(8,128)(2,1)S(1)}, bf16[224,384]{1,0:T(8,128)(2,1)S(1)}, u32[]{:S(2)}, u32[]{:S(2)}) collective-permute-start(bf16[224,384]{1,0:T(8,128)(2,1)S(1)} %get-tuple-element.96.refs_0_), channel_id=1, source_target_pairs={{0,16},{4,20},{8,24},{12,28},{16,0},{20,4},{24,8},{28,12},{1,17},{... | collective-permute-start | bytes 516104 | tf_op jit(solution)/shard_map/ppermute | solution.py:334
  40.8 5.5 %collective-permute-start.13 = (bf16[128,640]{1,0:T(8,128)(2,1)S(1)}, bf16[128,640]{1,0:T(8,128)(2,1)S(1)}, u32[]{:S(2)}, u32[]{:S(2)}) collective-permute-start(bf16[128,640]{1,0:T(8,128)(2,1)S(1)} %go_right.1.refs_2_), channel_id=1, source_target_pairs={{0,8},{4,12},{8,0},{12,4},{16,24},{20,28},{24,16},{28,20},{1,9},{5... | collective-permute-start | bytes 491528 | tf_op jit(solution)/shard_map/ppermute | solution.py:334
  46.4 1.7 %collective-permute-start.14 = (bf16[160,1024]{1,0:T(8,128)(2,1)S(1)}, bf16[160,1024]{1,0:T(8,128)(2,1)S(1)}, u32[]{:S(2)}, u32[]{:S(2)}) collective-permute-start(bf16[160,1024]{1,0:T(8,128)(2,1)S(1)} %get-tuple-element.101.refs_7_), channel_id=1, source_target_pairs={{0,4},{4,0},{8,12},{12,8},{16,20},{20,16},{24,28},{28,24},{1,5},{5... | collective-permute-start | bytes 983048 | tf_op jit(solution)/shard_map/ppermute | solution.py:334

commit v6 on v5

--- a/solution.py
+++ b/solution.py
@@ -252,11 +252,15 @@
     part_out[...] = part.astype(jnp.bfloat16)
 
 
-def input_grad_kernel(sb_next, sb_spec, spec, ks, vs, grad, kl, hidden, mix, nxt_two, back, key_out, value_out, gate_out, query_out, token):
+def gates_kernel(grad, kl, hidden, mix, gate_out, query_out, token):
     token[...] = jnp.zeros(token.shape, jnp.float32)
     slope = wide(grad)
     gate_out[...] = (slope * wide(hidden)).astype(jnp.bfloat16)
     query_out[...] = (slope * wide(kl) * mix[...]).astype(jnp.bfloat16)
+
+
+def input_grad_kernel(sb_next, sb_spec, spec, ks, vs, nxt_two, back, key_out, value_out, token):
+    token[...] = jnp.zeros(token.shape, jnp.float32)
     total = sb_spec[...] + dft_exact(nxt_two[...], sb_next[...])
     grad_in = dft_back(back[...], *times_conj(total, spec[...]))
     key_out[...] = (grad_in * wide(vs)).astype(jnp.bfloat16)
@@ -691,15 +695,25 @@
         [(block, full, "vmem")],
         width,
     )
-    key_short_grad, value_short_grad, key_long_grad, query_short_grad, token = run(
+    key_short_grad, value_short_grad, token = run(
         input_grad_kernel,
         "input_grad",
-        [sb_next, sb_spec, short_spec, ks, vs, long_grad, kl, hidden, short_mix],
+        [sb_next, sb_spec, short_spec, ks, vs],
         [nxt_two, back],
-        [(block, half, "hbm")] * 4 + [(ROWS, full, "vmem")],
-        width,
-    )
-    mine, got, near = taps_and_states(part, fore_state, rate, [[token], [local_mix]], ())
+        [(block, half, "hbm")] * 2 + [(ROWS, full, "vmem")],
+        width,
+    )
+    key_long_grad, query_short_grad, gates_token = run(
+        gates_kernel,
+        "gates",
+        [long_grad, kl, hidden, short_mix],
+        [],
+        [(block, half, "hbm")] * 2 + [(ROWS, full, "vmem")],
+        width,
+        (),
+        [token],
+    )
+    mine, got, near = taps_and_states(part, fore_state, rate, [[token], [local_mix, gates_token]], ())
     other = swapped(mine, 1)
     ready = [near, local_mix, rate, res, ql, ct]
     some = gated(True, "gated_own", got, *ready, min(width, channels // 2))

time: 50.2 us -> 50.2 us (level)
  Pallas kernels: 25 us -> 25.7 us
  waiting for transfers between devices: 7.76 us -> 7.12 us
    ppermute x13, waiting for transfers between devices: 7.75 us -> 7.11 us  [swapped(): return lax.ppermute(value, 'ctx', [(i, i ^ mask) for i in range(size)])]
    pallas_call x8 -> x9, Pallas kernels: 16.8 us -> 17.5 us  [run(): pl.pallas_call(whole, in_specs=[pl.BlockSpec(memory_space=pltpu.VMEM)] *...]
  transfers between devices with their start and end apart: 15 -> 15, of which waited for: 8 -> 8; matrix products, arithmetic and copies ran while one was open for 0% -> 0% of each run, Pallas kernels for 39% -> 41%
where the time goes in v6:
time: 50.2 us; the launch traced here: 50 us
  Pallas kernels  25.7 us (51%)
  starting transfers between devices  16.2 us (32%)
  waiting for transfers between devices  7.12 us (14%)
  between operations  0.97 us (2%)
    pallas_call x9, Pallas kernels, run(): pl.pallas_call(whole, in_specs=[pl.BlockSpec(memory_space=pltpu.VMEM)] *...  17.5 us
    ppermute x13, starting transfers between devices, swapped(): return lax.ppermute(value, 'ctx', [(i, i ^ mask) for i in range(size)])  12.3 us
    ppermute x13, waiting for transfers between devices, swapped(): return lax.ppermute(value, 'ctx', [(i, i ^ mask) for i in range(size)])  7.11 us
    pallas_call x2, Pallas kernels, load(): pl.pallas_call(whole, in_specs=[pl.BlockSpec(memory_space=pltpu.HBM)] * c...  4.39 us
    ppermute x2, starting transfers between devices, shifted(): return lax.ppermute(value, 'ctx', pairs)  3.86 us
    pallas_call x2, Pallas kernels, gated(): pl.pallas_call(body, in_specs=[pl.BlockSpec(memory_space=pltpu.VMEM)] * l...  3.24 us
  transfers between devices with their start and end apart: 15, of which 8 were waited for; matrix products, arithmetic and copies ran while one was open for 0% of the time, Pallas kernels for 41%

profile of v6, /device:TPU:0, one launch (start us, length us, event | category | flops | bytes accessed | tf_op | source)
XLA Modules:
  0.0 50.0 jit_solution(16137732986391950810)
XLA Ops:
  0.6 1.4 %product.1 = (bf16[128,2048]{1,0:T(8,128)(2,1)S(1)}, bf16[128,2048]{1,0:T(8,128)(2,1)S(1)}, bf16[128,2048]{1,0:T(8,128)(2,1)S(1)}) custom-call(bf16[128,2048]{1,0:T(8,128)(2,1)} %refs_0_.2, bf16[128,2048]{1,0:T(8,128)(2,1)} %refs_1_.2), custom_call_target="tpu_custom_call" | custom-call | bytes 1024 | tf_op jit(solution)/shard_map/product/pallas_call | solution.py:183
  2.0 2.4 %collective-permute-start.3 = (bf16[128,2048]{1,0:T(8,128)(2,1)S(1)}, bf16[128,2048]{1,0:T(8,128)(2,1)S(1)}, u32[]{:S(2)}, u32[]{:S(2)}) collective-permute-start(bf16[128,2048]{1,0:T(8,128)(2,1)S(1)} %get-tuple-element.61.refs_11_.refs_1_), channel_id=1, source_target_pairs={{0,4},{4,8},{8,12},{12,16},{16,20},{20,24},{24,28},{1,5},{5,9},{9,... | collective-permute-start | bytes 1572872 | tf_op jit(solution)/shard_map/ppermute | solution.py:333
  4.4 3.0 %states.1 = (f32[16,2048]{1,0:T(8,128)S(1)}, bf16[128,2048]{1,0:T(8,128)(2,1)S(1)}, bf16[128,2048]{1,0:T(8,128)(2,1)S(1)}, f32[16,2048]{1,0:T(8,128)S(1)}, bf16[...) custom-call(f32[16,2048]{1,0:T(8,128)} %refs_0_.3, ...), custom_call_target="tpu_custom_call" | custom-call | bytes 1024 | tf_op jit(solution)/shard_map/states/pallas_call | solution.py:183
  7.4 2.6 %collective-permute-start = (f32[16,2048]{1,0:T(8,128)S(1)}, f32[16,2048]{1,0:T(8,128)S(1)}, u32[]{:S(2)}, u32[]{:S(2)}) collective-permute-start(f32[16,2048]{1,0:T(8,128)S(1)} %get-tuple-element.67.refs_0_), channel_id=1, source_target_pairs={{0,4},{4,0},{8,12},{12,8},{16,20},{20,16},{24,28},{28,24},{1,5},{5... | collective-permute-start | bytes 393224 | tf_op jit(solution)/shard_map/ppermute | solution.py:338
  10.1 1.0 %collective-permute-done.refs_1_.refs_2_ = f32[16,2048]{1,0:T(8,128)S(1)} collective-permute-done((f32[16,2048]{1,0:T(8,128)S(1)}, f32[16,2048]{1,0:T(8,128)S(1)}, u32[]{:S(2)}, u32[]{:S(2)}) %collective-permute-start) | collective-permute-done | bytes 131104 | tf_op jit(solution)/shard_map/ppermute | solution.py:338
  11.1 1.6 %collective-permute-start.1 = (f32[16,2048]{1,0:T(8,128)S(1)}, f32[16,2048]{1,0:T(8,128)S(1)}, u32[]{:S(2)}, u32[]{:S(2)}) collective-permute-start(f32[16,2048]{1,0:T(8,128)S(1)} %chip_states.1.refs_3_.refs_0_), channel_id=1, source_target_pairs={{0,16},{4,20},{8,24},{12,28},{16,0},{20,4},{24,8},{28,12},{1,17},{... | collective-permute-start | bytes 393224 | tf_op jit(solution)/shard_map/ppermute | solution.py:338
  13.7 2.0 %filter.1.refs_2_.refs_1_ = f32[256,2048]{1,0:T(8,128)S(1)} custom-call(f32[16,2048]{1,0:T(8,128)S(1)} %get-tuple-element.64.refs_2_.refs_0_.refs_5_.refs_3_, f32[16,2048]{1,0:T(8,128)S(1)} %get-tuple-element.65.refs_1_.refs_3_.refs_4_, bf16[256,384]{1,0:T(8,128)(2,1)S(1)} %get-tuple-element.66.refs_2_.refs_3_, f32[16,2048]{1,0:T(8,128)S(1)} %chip_states.1.refs_3_.refs_0_), custom_call_target="tpu_custom_call" | custom-call | bytes 1024 | tf_op jit(solution)/shard_map/filter/pallas_call | solution.py:304
  15.7 2.0 %grad_local.1.refs_4_.refs_0_ = f32[128,2048]{1,0:T(8,128)S(1)} custom-call(bf16[128,2048]{1,0:T(8,128)(2,1)S(1)} %get-tuple-element.62.refs_0_.refs_5_, bf16[128,2048]{1,0:T(8,128)(2,1)S(1)} %get-tuple-element.63.refs_1_.refs_6_, f32[256,2048]{1,0:T(8,128)S(1)} %filter.1.refs_2_.refs_1_, bf16[256,384]{1,0:T(8,128)(2,1)S(1)} %get-tuple-element.66.refs_2_.refs_3_, ...), custom_call_target="tpu_custom_call" | custom-call | bytes 1024 | tf_op jit(solution)/shard_map/grad_local/pallas_call | solution.py:304
  18.6 3.4 %short.1 = (f32[256,2048]{1,0:T(8,128)S(1)}, f32[128,2048]{1,0:T(8,128)S(1)}, bf16[128,2048]{1,0:T(8,128)(2,1)S(1)}, bf16[128,2048]{1,0:T(8,128)(2,1)S(1)}, f32[16,2048]{1,0:T(8,128)S(1)}) custom-call(f32[256,2048]{1,0:T(8,128)S(1)} %get-tuple-element.74.refs_0_, bf16[128,2048]{1,0:T(8,128)(2,1)S(1)} %collective-permute-done.3.refs_1_, ...), custom_call_target="tpu_custom_call" | custom-call | bytes 1024 | tf_op jit(solution)/shard_map/short/pallas_call | solution.py:304
  22.0 1.3 %collective-permute-done.2.refs_1_ = f32[16,2048]{1,0:T(8,128)S(1)} collective-permute-done((f32[16,2048]{1,0:T(8,128)S(1)}, f32[16,2048]{1,0:T(8,128)S(1)}, u32[]{:S(2)}, u32[]{:S(2)}) %collective-permute-start.2) | collective-permute-done | bytes 131104 | tf_op jit(solution)/shard_map/ppermute | solution.py:338
  23.3 2.2 %long_grad.1 = (bf16[128,2048]{1,0:T(8,128)(2,1)S(1)}, bf16[128,2048]{1,0:T(8,128)(2,1)S(1)}) custom-call(f32[128,2048]{1,0:T(8,128)S(1)} %grad_local.1.refs_4_.refs_0_, f32[16,2048]{1,0:T(8,128)S(1)} %far_states.1.refs_1_, f32[16,2048]{1,0:T(8,128)S(1)} %get-tuple-element.64.refs_2_.refs_0_.refs_5_.refs_3_, ...), custom_call_target="tpu_custom_call" | custom-call | bytes 1024 | tf_op jit(solution)/shard_map/long_grad/pallas_call | solution.py:304
  25.5 1.5 %collective-permute-start.10 = (bf16[128,2048]{1,0:T(8,128)(2,1)S(1)}, bf16[128,2048]{1,0:T(8,128)(2,1)S(1)}, u32[]{:S(2)}, u32[]{:S(2)}) collective-permute-start(bf16[128,2048]{1,0:T(8,128)(2,1)S(1)} %get-tuple-element.79.refs_0_), channel_id=1, source_target_pairs={{4,0},{8,4},{12,8},{16,12},{20,16},{24,20},{28,24},{5,1},{9,5},{13... | collective-permute-start | bytes 1572872 | tf_op jit(solution)/shard_map/ppermute | solution.py:333
  27.0 1.7 %taps.1 = (f32[256,2048]{1,0:T(8,128)S(1)}, bf16[128,2048]{1,0:T(8,128)(2,1)S(1)}) custom-call(bf16[128,2048]{1,0:T(8,128)(2,1)S(1)} %get-tuple-element.79.refs_0_, f32[256,2048]{1,0:T(8,128)S(1)} %get-tuple-element.80.refs_1_, bf16[256,256]{1,0:T(8,128)(2,1)S(1)} %get-tuple-element.70.refs_3_.refs_2_, ...), custom_call_target="tpu_custom_call" | custom-call | bytes 1024 | tf_op jit(solution)/shard_map/taps/pallas_call | solution.py:304
  28.8 1.2 %collective-permute-start.5 = (bf16[128,256]{1,0:T(8,128)(2,1)S(1)}, bf16[128,256]{1,0:T(8,128)(2,1)S(1)}, u32[]{:S(2)}, u32[]{:S(2)}) collective-permute-start(bf16[128,256]{1,0:T(8,128)(2,1)S(1)} %get-tuple-element.85), channel_id=1, source_target_pairs={{0,4},{4,0},{8,12},{12,8},{16,20},{20,16},{24,28},{28,24},{1,5},{5... | collective-permute-start | bytes 196616 | tf_op jit(solution)/shard_map/ppermute | solution.py:338
  33.1 1.5 %collective-permute-start.12 = (bf16[128,640]{1,0:T(8,128)(2,1)S(1)}, bf16[128,640]{1,0:T(8,128)(2,1)S(1)}, u32[]{:S(2)}, u32[]{:S(2)}) collective-permute-start(bf16[128,640]{1,0:T(8,128)(2,1)S(1)} %get-tuple-element.96.refs_0_), channel_id=1, source_target_pairs={{0,16},{4,20},{8,24},{12,28},{16,0},{20,4},{24,8},{28,12},{1,17},{... | collective-permute-start | bytes 491528 | tf_op jit(solution)/shard_map/ppermute | solution.py:338
  34.6 2.5 %input_grad.1 = (bf16[128,2048]{1,0:T(8,128)(2,1)}, bf16[128,2048]{1,0:T(8,128)(2,1)}, f32[8,2048]{1,0:T(8,128)S(1)}) custom-call(bf16[128,2048]{1,0:T(8,128)(2,1)S(1)} %collective-permute-done.10.refs_0_, f32[256,2048]{1,0:T(8,128)S(1)} %get-tuple-element.91.refs_1_, f32[256,2048]{1,0:T(8,128)S(1)} %get-tuple-element.71.refs_5_.refs_2_, ...), custom_call_target="tpu_custom_call" | custom-call | bytes 1024 | tf_op jit(solution)/shard_map/input_grad/pallas_call | solution.py:304
  37.1 2.1 %collective-permute-done.9.refs_1_ = bf16[224,384]{1,0:T(8,128)(2,1)S(1)} collective-permute-done((bf16[224,384]{1,0:T(8,128)(2,1)S(1)}, bf16[224,384]{1,0:T(8,128)(2,1)S(1)}, u32[]{:S(2)}, u32[]{:S(2)}) %collective-permute-start.9) | collective-permute-done | bytes 172064 | tf_op jit(solution)/shard_map/ppermute | solution.py:338
  39.2 1.5 %collective-permute-start.11 = (bf16[224,384]{1,0:T(8,128)(2,1)S(1)}, bf16[224,384]{1,0:T(8,128)(2,1)S(1)}, u32[]{:S(2)}, u32[]{:S(2)}) collective-permute-start(bf16[224,384]{1,0:T(8,128)(2,1)S(1)} %get-tuple-element.95.refs_0_), channel_id=1, source_target_pairs={{0,16},{4,20},{8,24},{12,28},{16,0},{20,4},{24,8},{28,12},{1,17},{... | collective-permute-start | bytes 516104 | tf_op jit(solution)/shard_map/ppermute | solution.py:338
  40.8 1.3 %collective-permute-start.13 = (bf16[128,640]{1,0:T(8,128)(2,1)S(1)}, bf16[128,640]{1,0:T(8,128)(2,1)S(1)}, u32[]{:S(2)}, u32[]{:S(2)}) collective-permute-start(bf16[128,640]{1,0:T(8,128)(2,1)S(1)} %go_right.1.refs_2_), channel_id=1, source_target_pairs={{0,8},{4,12},{8,0},{12,4},{16,24},{20,28},{24,16},{28,20},{1,9},{5... | collective-permute-start | bytes 491528 | tf_op jit(solution)/shard_map/ppermute | solution.py:338
  42.1 1.7 %long_local.1.refs_7_.refs_2_ = f32[128,2048]{1,0:T(8,128)S(1)} custom-call(bf16[128,2048]{1,0:T(8,128)(2,1)S(1)} %get-tuple-element.99.refs_0_, f32[256,2048]{1,0:T(8,128)S(1)} %filter.1.refs_2_.refs_1_, bf16[256,256]{1,0:T(8,128)(2,1)S(1)} %get-tuple-element.70.refs_3_.refs_2_, bf16[256,256]{1,0:T(8,128)(2,1)S(1)} %get-tuple-element.68.refs_4_.refs_7_.refs_3_.refs_6_), custom_call_target="tpu_custom_call" | custom-call | bytes 1024 | tf_op jit(solution)/shard_map/long_local/pallas_call | solution.py:304
  43.7 1.1 %gates.1 = (bf16[128,2048]{1,0:T(8,128)(2,1)}, bf16[128,2048]{1,0:T(8,128)(2,1)}, f32[8,2048]{1,0:T(8,128)S(1)}) custom-call(bf16[128,2048]{1,0:T(8,128)(2,1)S(1)} %get-tuple-element.100.refs_0_, bf16[128,2048]{1,0:T(8,128)(2,1)S(1)} %get-tuple-element.76.refs_4_.refs_1_, bf16[128,2048]{1,0:T(8,128)(2,1)S(1)} %get-tuple-element.78.refs_4_.refs_2_, ...), custom_call_target="tpu_custom_call" | custom-call | bytes 1024 | tf_op jit(solution)/shard_map/gates/pallas_call | solution.py:304
  44.8 1.5 %collective-permute-done.13.refs_3_ = bf16[128,640]{1,0:T(8,128)(2,1)S(1)} collective-permute-done((bf16[128,640]{1,0:T(8,128)(2,1)S(1)}, bf16[128,640]{1,0:T(8,128)(2,1)S(1)}, u32[]{:S(2)}, u32[]{:S(2)}) %collective-permute-start.13) | collective-permute-done | bytes 163872 | tf_op jit(solution)/shard_map/ppermute | solution.py:338
  46.5 1.6 %gated_own.1 = (bf16[128,2048]{1,0:T(8,128)(2,1)}, bf16[128,2048]{1,0:T(8,128)(2,1)}) custom-call(f32[16,1024]{1,0:T(8,128)S(1)} %get-tuple-element.105.refs_0_, f32[16,2048]{1,0:T(8,128)S(1)} %get-tuple-element.104.refs_1_, f32[128,2048]{1,0:T(8,128)S(1)} %long_local.1.refs_7_.refs_2_, f32[16,2048]{1,0:T(8,128)S(1)} %get-tuple-element.64.refs_2_.refs_0_.refs_5_.refs_3_, ...), custom_call_target="tpu_custom_call" | custom-call | bytes 1024 | tf_op jit(solution)/shard_map/gated_own/pallas_call | solution.py:562
  48.1 1.7 %gated_other.1 = (bf16[128,2048]{1,0:T(8,128)(2,1)}, bf16[128,2048]{1,0:T(8,128)(2,1)}, f32[128,2048]{1,0:T(8,128)}) custom-call(bf16[160,1024]{1,0:T(8,128)(2,1)S(1)} %collective-permute-done.14.refs_0_, f32[16,2048]{1,0:T(8,128)S(1)} %get-tuple-element.104.refs_1_, ...), custom_call_target="tpu_custom_call", output_to_operand_aliasing={{0}: (8, {}), {1}: (9, {})} | custom-call | bytes 1024 | tf_op jit(solution)/shard_map/gated_other/pallas_call | solution.py:562
  (27 shorter events, 5.5 us)
Async XLA Ops:
  2.0 16.5 %collective-permute-start.3 = (bf16[128,2048]{1,0:T(8,128)(2,1)S(1)}, bf16[128,2048]{1,0:T(8,128)(2,1)S(1)}, u32[]{:S(2)}, u32[]{:S(2)}) collective-permute-start(bf16[128,2048]{1,0:T(8,128)(2,1)S(1)} %get-tuple-element.61.refs_11_.refs_1_), channel_id=1, source_target_pairs={{0,4},{4,8},{8,12},{12,16},{16,20},{20,24},{24,28},{1,5},{5,9},{9,... | collective-permute-start | bytes 1572872 | tf_op jit(solution)/shard_map/ppermute | solution.py:333
  7.4 3.6 %collective-permute-start = (f32[16,2048]{1,0:T(8,128)S(1)}, f32[16,2048]{1,0:T(8,128)S(1)}, u32[]{:S(2)}, u32[]{:S(2)}) collective-permute-start(f32[16,2048]{1,0:T(8,128)S(1)} %get-tuple-element.67.refs_0_), channel_id=1, source_target_pairs={{0,4},{4,0},{8,12},{12,8},{16,20},{20,16},{24,28},{28,24},{1,5},{5... | collective-permute-start | bytes 393224 | tf_op jit(solution)/shard_map/ppermute | solution.py:338
  11.1 6.5 %collective-permute-start.1 = (f32[16,2048]{1,0:T(8,128)S(1)}, f32[16,2048]{1,0:T(8,128)S(1)}, u32[]{:S(2)}, u32[]{:S(2)}) collective-permute-start(f32[16,2048]{1,0:T(8,128)S(1)} %chip_states.1.refs_3_.refs_0_), channel_id=1, source_target_pairs={{0,16},{4,20},{8,24},{12,28},{16,0},{20,4},{24,8},{28,12},{1,17},{... | collective-permute-start | bytes 393224 | tf_op jit(solution)/shard_map/ppermute | solution.py:338
  17.7 5.6 %collective-permute-start.2 = (f32[16,2048]{1,0:T(8,128)S(1)}, f32[16,2048]{1,0:T(8,128)S(1)}, u32[]{:S(2)}, u32[]{:S(2)}) collective-permute-start(f32[16,2048]{1,0:T(8,128)S(1)} %get-tuple-element.73.refs_8_), channel_id=1, source_target_pairs={{0,8},{4,12},{8,0},{12,4},{16,24},{20,28},{24,16},{28,20},{1,9},{5... | collective-permute-start | bytes 393224 | tf_op jit(solution)/shard_map/ppermute | solution.py:338
  25.5 9.1 %collective-permute-start.10 = (bf16[128,2048]{1,0:T(8,128)(2,1)S(1)}, bf16[128,2048]{1,0:T(8,128)(2,1)S(1)}, u32[]{:S(2)}, u32[]{:S(2)}) collective-permute-start(bf16[128,2048]{1,0:T(8,128)(2,1)S(1)} %get-tuple-element.79.refs_0_), channel_id=1, source_target_pairs={{4,0},{8,4},{12,8},{16,12},{20,16},{24,20},{28,24},{5,1},{9,5},{13... | collective-permute-start | bytes 1572872 | tf_op jit(solution)/shard_map/ppermute | solution.py:333
  28.8 2.1 %collective-permute-start.5 = (bf16[128,256]{1,0:T(8,128)(2,1)S(1)}, bf16[128,256]{1,0:T(8,128)(2,1)S(1)}, u32[]{:S(2)}, u32[]{:S(2)}) collective-permute-start(bf16[128,256]{1,0:T(8,128)(2,1)S(1)} %get-tuple-element.85), channel_id=1, source_target_pairs={{0,4},{4,0},{8,12},{12,8},{16,20},{20,16},{24,28},{28,24},{1,5},{5... | collective-permute-start | bytes 196616 | tf_op jit(solution)/shard_map/ppermute | solution.py:338
  30.0 2.2 %collective-permute-start.4 = (bf16[64,1024]{1,0:T(8,128)(2,1)S(1)}, bf16[64,1024]{1,0:T(8,128)(2,1)S(1)}, u32[]{:S(2)}, u32[]{:S(2)}) collective-permute-start(bf16[64,1024]{1,0:T(8,128)(2,1)S(1)} %get-tuple-element.84), channel_id=1, source_target_pairs={{0,4},{4,0},{8,12},{12,8},{16,20},{20,16},{24,28},{28,24},{1,5},{5... | collective-permute-start | bytes 393224 | tf_op jit(solution)/shard_map/ppermute | solution.py:338
  30.1 1.4 %collective-permute-start.6 = (bf16[128,256]{1,0:T(8,128)(2,1)S(1)}, bf16[128,256]{1,0:T(8,128)(2,1)S(1)}, u32[]{:S(2)}, u32[]{:S(2)}) collective-permute-start(bf16[128,256]{1,0:T(8,128)(2,1)S(1)} %get-tuple-element.86), channel_id=1, source_target_pairs={{0,4},{4,0},{8,12},{12,8},{16,20},{20,16},{24,28},{28,24},{1,5},{5... | collective-permute-start | bytes 196616 | tf_op jit(solution)/shard_map/ppermute | solution.py:338
  30.5 1.3 %collective-permute-start.7 = (bf16[128,256]{1,0:T(8,128)(2,1)S(1)}, bf16[128,256]{1,0:T(8,128)(2,1)S(1)}, u32[]{:S(2)}, u32[]{:S(2)}) collective-permute-start(bf16[128,256]{1,0:T(8,128)(2,1)S(1)} %get-tuple-element.87), channel_id=1, source_target_pairs={{0,4},{4,0},{8,12},{12,8},{16,20},{20,16},{24,28},{28,24},{1,5},{5... | collective-permute-start | bytes 196616 | tf_op jit(solution)/shard_map/ppermute | solution.py:338
  30.9 1.3 %collective-permute-start.8 = (bf16[128,256]{1,0:T(8,128)(2,1)S(1)}, bf16[128,256]{1,0:T(8,128)(2,1)S(1)}, u32[]{:S(2)}, u32[]{:S(2)}) collective-permute-start(bf16[128,256]{1,0:T(8,128)(2,1)S(1)} %get-tuple-element.88), channel_id=1, source_target_pairs={{0,4},{4,0},{8,12},{12,8},{16,20},{20,16},{24,28},{28,24},{1,5},{5... | collective-permute-start | bytes 196616 | tf_op jit(solution)/shard_map/ppermute | solution.py:338
  32.3 6.8 %collective-permute-start.9 = (bf16[224,384]{1,0:T(8,128)(2,1)S(1)}, bf16[224,384]{1,0:T(8,128)(2,1)S(1)}, u32[]{:S(2)}, u32[]{:S(2)}) collective-permute-start(bf16[224,384]{1,0:T(8,128)(2,1)S(1)} %get-tuple-element.89.refs_0_), channel_id=1, source_target_pairs={{0,8},{4,12},{8,0},{12,4},{16,24},{20,28},{24,16},{28,20},{1,9},{5... | collective-permute-start | bytes 516104 | tf_op jit(solution)/shard_map/ppermute | solution.py:338
  33.1 7.7 %collective-permute-start.12 = (bf16[128,640]{1,0:T(8,128)(2,1)S(1)}, bf16[128,640]{1,0:T(8,128)(2,1)S(1)}, u32[]{:S(2)}, u32[]{:S(2)}) collective-permute-start(bf16[128,640]{1,0:T(8,128)(2,1)S(1)} %get-tuple-element.96.refs_0_), channel_id=1, source_target_pairs={{0,16},{4,20},{8,24},{12,28},{16,0},{20,4},{24,8},{28,12},{1,17},{... | collective-permute-start | bytes 491528 | tf_op jit(solution)/shard_map/ppermute | solution.py:338
  39.2 7.1 %collective-permute-start.11 = (bf16[224,384]{1,0:T(8,128)(2,1)S(1)}, bf16[224,384]{1,0:T(8,128)(2,1)S(1)}, u32[]{:S(2)}, u32[]{:S(2)}) collective-permute-start(bf16[224,384]{1,0:T(8,128)(2,1)S(1)} %get-tuple-element.95.refs_0_), channel_id=1, source_target_pairs={{0,16},{4,20},{8,24},{12,28},{16,0},{20,4},{24,8},{28,12},{1,17},{... | collective-permute-start | bytes 516104 | tf_op jit(solution)/shard_map/ppermute | solution.py:338
  40.8 5.5 %collective-permute-start.13 = (bf16[128,640]{1,0:T(8,128)(2,1)S(1)}, bf16[128,640]{1,0:T(8,128)(2,1)S(1)}, u32[]{:S(2)}, u32[]{:S(2)}) collective-permute-start(bf16[128,640]{1,0:T(8,128)(2,1)S(1)} %go_right.1.refs_2_), channel_id=1, source_target_pairs={{0,8},{4,12},{8,0},{12,4},{16,24},{20,28},{24,16},{28,20},{1,9},{5... | collective-permute-start | bytes 491528 | tf_op jit(solution)/shard_map/ppermute | solution.py:338
  46.4 1.7 %collective-permute-start.14 = (bf16[160,1024]{1,0:T(8,128)(2,1)S(1)}, bf16[160,1024]{1,0:T(8,128)(2,1)S(1)}, u32[]{:S(2)}, u32[]{:S(2)}) collective-permute-start(bf16[160,1024]{1,0:T(8,128)(2,1)S(1)} %get-tuple-element.103.refs_7_), channel_id=1, source_target_pairs={{0,4},{4,0},{8,12},{12,8},{16,20},{20,16},{24,28},{28,24},{1,5},{5... | collective-permute-start | bytes 983048 | tf_op jit(solution)/shard_map/ppermute | solution.py:338

commit v7 on v6

--- a/solution.py
+++ b/solution.py
@@ -90,17 +90,18 @@
     sub = sublane((ROWS, rate.shape[1]))
     age = start + (sub if forward else ROWS - 1 - sub)
     waves, falls = [], []
+    slow = jnp.exp(-ROWS * rate)
     for mode in range(rate.shape[0]):
         pace = spread(rate[mode : mode + 1])
         waves.append(spread(weight[mode : mode + 1]) * jnp.exp(-pace * age))
-        falls.append(jnp.exp(-ROWS * pace))
+        falls.append(spread(slow[mode : mode + 1]))
     tiles = []
     count = block // ROWS
     for step in range(count):
-        total = waves[0]
-        for wave in waves[1:]:
-            total = total + wave
-        tiles.append(total)
+        level = waves
+        while len(level) > 1:
+            level = [sum(level[i : i + 2][1:], level[i]) for i in range(0, len(level), 2)]
+        tiles.append(level[0])
         if step < count - 1:
             waves = [wave * fall for wave, fall in zip(waves, falls)]
     if not forward:
@@ -115,9 +116,10 @@
     tiles = [data[t : t + ROWS] for t in range(0, block, ROWS)]
     if not forward:
         tiles = tiles[::-1]
+    slow = jnp.exp(-ROWS * rate)
     for mode in range(rate.shape[0]):
         pace = spread(rate[mode : mode + 1])
-        fall = jnp.exp(-ROWS * pace)
+        fall = spread(slow[mode : mode + 1])
         total = tiles[0]
         for tile in tiles[1:]:
             total = total * fall + tile

time: 50.2 us -> 50.1 us (level)
  transfers between devices with their start and end apart: 15 -> 15, of which waited for: 8 -> 9; matrix products, arithmetic and copies ran while one was open for 0% -> 0% of each run, Pallas kernels for 41% -> 41%
where the time goes in v7:
time: 50.1 us; the launch traced here: 49.9 us
  Pallas kernels  25.6 us (51%)
  starting transfers between devices  16.4 us (33%)
  waiting for transfers between devices  6.98 us (14%)
  between operations  0.96 us (2%)
    pallas_call x9, Pallas kernels, run(): pl.pallas_call(whole, in_specs=[pl.BlockSpec(memory_space=pltpu.VMEM)] *...  17.5 us
    ppermute x13, starting transfers between devices, swapped(): return lax.ppermute(value, 'ctx', [(i, i ^ mask) for i in range(size)])  12.5 us
    ppermute x13, waiting for transfers between devices, swapped(): return lax.ppermute(value, 'ctx', [(i, i ^ mask) for i in range(size)])  6.98 us
    pallas_call x2, Pallas kernels, load(): pl.pallas_call(whole, in_specs=[pl.BlockSpec(memory_space=pltpu.HBM)] * c...  4.37 us
    ppermute x2, starting transfers between devices, shifted(): return lax.ppermute(value, 'ctx', pairs)  3.86 us
    pallas_call x2, Pallas kernels, gated(): pl.pallas_call(body, in_specs=[pl.BlockSpec(memory_space=pltpu.VMEM)] * l...  3.15 us
  transfers between devices with their start and end apart: 15, of which 9 were waited for; matrix products, arithmetic and copies ran while one was open for 0% of the time, Pallas kernels for 41%

profile of v7, /device:TPU:0, one launch (start us, length us, event | category | flops | bytes accessed | tf_op | source)
XLA Modules:
  0.0 49.9 jit_solution(621080242127333092)
XLA Ops:
  0.6 1.4 %product.1 = (bf16[128,2048]{1,0:T(8,128)(2,1)S(1)}, bf16[128,2048]{1,0:T(8,128)(2,1)S(1)}, bf16[128,2048]{1,0:T(8,128)(2,1)S(1)}) custom-call(bf16[128,2048]{1,0:T(8,128)(2,1)} %refs_0_.2, bf16[128,2048]{1,0:T(8,128)(2,1)} %refs_1_.2), custom_call_target="tpu_custom_call" | custom-call | bytes 1024 | tf_op jit(solution)/shard_map/product/pallas_call | solution.py:185
  2.0 2.4 %collective-permute-start.3 = (bf16[128,2048]{1,0:T(8,128)(2,1)S(1)}, bf16[128,2048]{1,0:T(8,128)(2,1)S(1)}, u32[]{:S(2)}, u32[]{:S(2)}) collective-permute-start(bf16[128,2048]{1,0:T(8,128)(2,1)S(1)} %get-tuple-element.61.refs_11_.refs_1_), channel_id=1, source_target_pairs={{0,4},{4,8},{8,12},{12,16},{16,20},{20,24},{24,28},{1,5},{5,9},{9,... | collective-permute-start | bytes 1572872 | tf_op jit(solution)/shard_map/ppermute | solution.py:335
  4.4 3.0 %states.1 = (f32[16,2048]{1,0:T(8,128)S(1)}, bf16[128,2048]{1,0:T(8,128)(2,1)S(1)}, bf16[128,2048]{1,0:T(8,128)(2,1)S(1)}, f32[16,2048]{1,0:T(8,128)S(1)}, bf16[...) custom-call(f32[16,2048]{1,0:T(8,128)} %refs_0_.3, ...), custom_call_target="tpu_custom_call" | custom-call | bytes 1024 | tf_op jit(solution)/shard_map/states/pallas_call | solution.py:185
  7.4 2.6 %collective-permute-start = (f32[16,2048]{1,0:T(8,128)S(1)}, f32[16,2048]{1,0:T(8,128)S(1)}, u32[]{:S(2)}, u32[]{:S(2)}) collective-permute-start(f32[16,2048]{1,0:T(8,128)S(1)} %get-tuple-element.67.refs_0_), channel_id=1, source_target_pairs={{0,4},{4,0},{8,12},{12,8},{16,20},{20,16},{24,28},{28,24},{1,5},{5... | collective-permute-start | bytes 393224 | tf_op jit(solution)/shard_map/ppermute | solution.py:340
  10.1 1.0 %collective-permute-done.refs_1_.refs_2_ = f32[16,2048]{1,0:T(8,128)S(1)} collective-permute-done((f32[16,2048]{1,0:T(8,128)S(1)}, f32[16,2048]{1,0:T(8,128)S(1)}, u32[]{:S(2)}, u32[]{:S(2)}) %collective-permute-start) | collective-permute-done | bytes 131104 | tf_op jit(solution)/shard_map/ppermute | solution.py:340
  11.1 1.6 %collective-permute-start.1 = (f32[16,2048]{1,0:T(8,128)S(1)}, f32[16,2048]{1,0:T(8,128)S(1)}, u32[]{:S(2)}, u32[]{:S(2)}) collective-permute-start(f32[16,2048]{1,0:T(8,128)S(1)} %chip_states.1.refs_3_.refs_0_), channel_id=1, source_target_pairs={{0,16},{4,20},{8,24},{12,28},{16,0},{20,4},{24,8},{28,12},{1,17},{... | collective-permute-start | bytes 393224 | tf_op jit(solution)/shard_map/ppermute | solution.py:340
  13.7 1.9 %filter.1.refs_2_.refs_1_ = f32[256,2048]{1,0:T(8,128)S(1)} custom-call(f32[16,2048]{1,0:T(8,128)S(1)} %get-tuple-element.64.refs_2_.refs_0_.refs_5_.refs_3_, f32[16,2048]{1,0:T(8,128)S(1)} %get-tuple-element.65.refs_1_.refs_3_.refs_4_, bf16[256,384]{1,0:T(8,128)(2,1)S(1)} %get-tuple-element.66.refs_2_.refs_3_, f32[16,2048]{1,0:T(8,128)S(1)} %chip_states.1.refs_3_.refs_0_), custom_call_target="tpu_custom_call" | custom-call | bytes 1024 | tf_op jit(solution)/shard_map/filter/pallas_call | solution.py:306
  15.6 2.0 %grad_local.1.refs_4_.refs_0_ = f32[128,2048]{1,0:T(8,128)S(1)} custom-call(bf16[128,2048]{1,0:T(8,128)(2,1)S(1)} %get-tuple-element.62.refs_0_.refs_5_, bf16[128,2048]{1,0:T(8,128)(2,1)S(1)} %get-tuple-element.63.refs_1_.refs_6_, f32[256,2048]{1,0:T(8,128)S(1)} %filter.1.refs_2_.refs_1_, bf16[256,384]{1,0:T(8,128)(2,1)S(1)} %get-tuple-element.66.refs_2_.refs_3_, ...), custom_call_target="tpu_custom_call" | custom-call | bytes 1024 | tf_op jit(solution)/shard_map/grad_local/pallas_call | solution.py:306
  18.5 3.4 %short.1 = (f32[256,2048]{1,0:T(8,128)S(1)}, f32[128,2048]{1,0:T(8,128)S(1)}, bf16[128,2048]{1,0:T(8,128)(2,1)S(1)}, bf16[128,2048]{1,0:T(8,128)(2,1)S(1)}, f32[16,2048]{1,0:T(8,128)S(1)}) custom-call(f32[256,2048]{1,0:T(8,128)S(1)} %get-tuple-element.74.refs_0_, bf16[128,2048]{1,0:T(8,128)(2,1)S(1)} %collective-permute-done.3.refs_1_, ...), custom_call_target="tpu_custom_call" | custom-call | bytes 1024 | tf_op jit(solution)/shard_map/short/pallas_call | solution.py:306
  22.0 1.2 %collective-permute-done.2.refs_1_ = f32[16,2048]{1,0:T(8,128)S(1)} collective-permute-done((f32[16,2048]{1,0:T(8,128)S(1)}, f32[16,2048]{1,0:T(8,128)S(1)}, u32[]{:S(2)}, u32[]{:S(2)}) %collective-permute-start.2) | collective-permute-done | bytes 131104 | tf_op jit(solution)/shard_map/ppermute | solution.py:340
  23.3 2.2 %long_grad.1 = (bf16[128,2048]{1,0:T(8,128)(2,1)S(1)}, bf16[128,2048]{1,0:T(8,128)(2,1)S(1)}) custom-call(f32[128,2048]{1,0:T(8,128)S(1)} %grad_local.1.refs_4_.refs_0_, f32[16,2048]{1,0:T(8,128)S(1)} %far_states.1.refs_1_, f32[16,2048]{1,0:T(8,128)S(1)} %get-tuple-element.64.refs_2_.refs_0_.refs_5_.refs_3_, ...), custom_call_target="tpu_custom_call" | custom-call | bytes 1024 | tf_op jit(solution)/shard_map/long_grad/pallas_call | solution.py:306
  25.4 1.5 %collective-permute-start.10 = (bf16[128,2048]{1,0:T(8,128)(2,1)S(1)}, bf16[128,2048]{1,0:T(8,128)(2,1)S(1)}, u32[]{:S(2)}, u32[]{:S(2)}) collective-permute-start(bf16[128,2048]{1,0:T(8,128)(2,1)S(1)} %get-tuple-element.79.refs_0_), channel_id=1, source_target_pairs={{4,0},{8,4},{12,8},{16,12},{20,16},{24,20},{28,24},{5,1},{9,5},{13... | collective-permute-start | bytes 1572872 | tf_op jit(solution)/shard_map/ppermute | solution.py:335
  26.9 1.7 %taps.1 = (f32[256,2048]{1,0:T(8,128)S(1)}, bf16[128,2048]{1,0:T(8,128)(2,1)S(1)}) custom-call(bf16[128,2048]{1,0:T(8,128)(2,1)S(1)} %get-tuple-element.79.refs_0_, f32[256,2048]{1,0:T(8,128)S(1)} %get-tuple-element.80.refs_1_, bf16[256,256]{1,0:T(8,128)(2,1)S(1)} %get-tuple-element.70.refs_3_.refs_2_, ...), custom_call_target="tpu_custom_call" | custom-call | bytes 1024 | tf_op jit(solution)/shard_map/taps/pallas_call | solution.py:306
  28.7 1.2 %collective-permute-start.5 = (bf16[128,256]{1,0:T(8,128)(2,1)S(1)}, bf16[128,256]{1,0:T(8,128)(2,1)S(1)}, u32[]{:S(2)}, u32[]{:S(2)}) collective-permute-start(bf16[128,256]{1,0:T(8,128)(2,1)S(1)} %get-tuple-element.85), channel_id=1, source_target_pairs={{0,4},{4,0},{8,12},{12,8},{16,20},{20,16},{24,28},{28,24},{1,5},{5... | collective-permute-start | bytes 196616 | tf_op jit(solution)/shard_map/ppermute | solution.py:340
  33.0 1.6 %collective-permute-start.12 = (bf16[128,640]{1,0:T(8,128)(2,1)S(1)}, bf16[128,640]{1,0:T(8,128)(2,1)S(1)}, u32[]{:S(2)}, u32[]{:S(2)}) collective-permute-start(bf16[128,640]{1,0:T(8,128)(2,1)S(1)} %get-tuple-element.96.refs_0_), channel_id=1, source_target_pairs={{0,16},{4,20},{8,24},{12,28},{16,0},{20,4},{24,8},{28,12},{1,17},{... | collective-permute-start | bytes 491528 | tf_op jit(solution)/shard_map/ppermute | solution.py:340
  34.6 2.5 %input_grad.1 = (bf16[128,2048]{1,0:T(8,128)(2,1)}, bf16[128,2048]{1,0:T(8,128)(2,1)}, f32[8,2048]{1,0:T(8,128)S(1)}) custom-call(bf16[128,2048]{1,0:T(8,128)(2,1)S(1)} %collective-permute-done.10.refs_0_, f32[256,2048]{1,0:T(8,128)S(1)} %get-tuple-element.91.refs_1_, f32[256,2048]{1,0:T(8,128)S(1)} %get-tuple-element.71.refs_5_.refs_2_, ...), custom_call_target="tpu_custom_call" | custom-call | bytes 1024 | tf_op jit(solution)/shard_map/input_grad/pallas_call | solution.py:306
  37.1 2.0 %collective-permute-done.9.refs_1_ = bf16[224,384]{1,0:T(8,128)(2,1)S(1)} collective-permute-done((bf16[224,384]{1,0:T(8,128)(2,1)S(1)}, bf16[224,384]{1,0:T(8,128)(2,1)S(1)}, u32[]{:S(2)}, u32[]{:S(2)}) %collective-permute-start.9) | collective-permute-done | bytes 172064 | tf_op jit(solution)/shard_map/ppermute | solution.py:340
  39.1 1.6 %collective-permute-start.11 = (bf16[224,384]{1,0:T(8,128)(2,1)S(1)}, bf16[224,384]{1,0:T(8,128)(2,1)S(1)}, u32[]{:S(2)}, u32[]{:S(2)}) collective-permute-start(bf16[224,384]{1,0:T(8,128)(2,1)S(1)} %get-tuple-element.95.refs_0_), channel_id=1, source_target_pairs={{0,16},{4,20},{8,24},{12,28},{16,0},{20,4},{24,8},{28,12},{1,17},{... | collective-permute-start | bytes 516104 | tf_op jit(solution)/shard_map/ppermute | solution.py:340
  40.8 1.3 %collective-permute-start.13 = (bf16[128,640]{1,0:T(8,128)(2,1)S(1)}, bf16[128,640]{1,0:T(8,128)(2,1)S(1)}, u32[]{:S(2)}, u32[]{:S(2)}) collective-permute-start(bf16[128,640]{1,0:T(8,128)(2,1)S(1)} %go_right.1.refs_2_), channel_id=1, source_target_pairs={{0,8},{4,12},{8,0},{12,4},{16,24},{20,28},{24,16},{28,20},{1,9},{5... | collective-permute-start | bytes 491528 | tf_op jit(solution)/shard_map/ppermute | solution.py:340
  42.1 1.7 %long_local.1.refs_7_.refs_2_ = f32[128,2048]{1,0:T(8,128)S(1)} custom-call(bf16[128,2048]{1,0:T(8,128)(2,1)S(1)} %get-tuple-element.99.refs_0_, f32[256,2048]{1,0:T(8,128)S(1)} %filter.1.refs_2_.refs_1_, bf16[256,256]{1,0:T(8,128)(2,1)S(1)} %get-tuple-element.70.refs_3_.refs_2_, bf16[256,256]{1,0:T(8,128)(2,1)S(1)} %get-tuple-element.68.refs_4_.refs_7_.refs_3_.refs_6_), custom_call_target="tpu_custom_call" | custom-call | bytes 1024 | tf_op jit(solution)/shard_map/long_local/pallas_call | solution.py:306
  43.7 1.1 %gates.1 = (bf16[128,2048]{1,0:T(8,128)(2,1)}, bf16[128,2048]{1,0:T(8,128)(2,1)}, f32[8,2048]{1,0:T(8,128)S(1)}) custom-call(bf16[128,2048]{1,0:T(8,128)(2,1)S(1)} %get-tuple-element.100.refs_0_, bf16[128,2048]{1,0:T(8,128)(2,1)S(1)} %get-tuple-element.76.refs_4_.refs_1_, bf16[128,2048]{1,0:T(8,128)(2,1)S(1)} %get-tuple-element.78.refs_4_.refs_2_, ...), custom_call_target="tpu_custom_call" | custom-call | bytes 1024 | tf_op jit(solution)/shard_map/gates/pallas_call | solution.py:306
  44.8 1.5 %collective-permute-done.13.refs_3_ = bf16[128,640]{1,0:T(8,128)(2,1)S(1)} collective-permute-done((bf16[128,640]{1,0:T(8,128)(2,1)S(1)}, bf16[128,640]{1,0:T(8,128)(2,1)S(1)}, u32[]{:S(2)}, u32[]{:S(2)}) %collective-permute-start.13) | collective-permute-done | bytes 163872 | tf_op jit(solution)/shard_map/ppermute | solution.py:340
  46.5 1.5 %gated_own.1 = (bf16[128,2048]{1,0:T(8,128)(2,1)}, bf16[128,2048]{1,0:T(8,128)(2,1)}) custom-call(f32[16,1024]{1,0:T(8,128)S(1)} %get-tuple-element.105.refs_0_, f32[16,2048]{1,0:T(8,128)S(1)} %get-tuple-element.104.refs_1_, f32[128,2048]{1,0:T(8,128)S(1)} %long_local.1.refs_7_.refs_2_, f32[16,2048]{1,0:T(8,128)S(1)} %get-tuple-element.64.refs_2_.refs_0_.refs_5_.refs_3_, ...), custom_call_target="tpu_custom_call" | custom-call | bytes 1024 | tf_op jit(solution)/shard_map/gated_own/pallas_call | solution.py:564
  48.1 1.6 %gated_other.1 = (bf16[128,2048]{1,0:T(8,128)(2,1)}, bf16[128,2048]{1,0:T(8,128)(2,1)}, f32[128,2048]{1,0:T(8,128)}) custom-call(bf16[160,1024]{1,0:T(8,128)(2,1)S(1)} %collective-permute-done.14.refs_0_, f32[16,2048]{1,0:T(8,128)S(1)} %get-tuple-element.104.refs_1_, ...), custom_call_target="tpu_custom_call", output_to_operand_aliasing={{0}: (8, {}), {1}: (9, {})} | custom-call | bytes 1024 | tf_op jit(solution)/shard_map/gated_other/pallas_call | solution.py:564
  (27 shorter events, 5.5 us)
Async XLA Ops:
  2.0 16.5 %collective-permute-start.3 = (bf16[128,2048]{1,0:T(8,128)(2,1)S(1)}, bf16[128,2048]{1,0:T(8,128)(2,1)S(1)}, u32[]{:S(2)}, u32[]{:S(2)}) collective-permute-start(bf16[128,2048]{1,0:T(8,128)(2,1)S(1)} %get-tuple-element.61.refs_11_.refs_1_), channel_id=1, source_target_pairs={{0,4},{4,8},{8,12},{12,16},{16,20},{20,24},{24,28},{1,5},{5,9},{9,... | collective-permute-start | bytes 1572872 | tf_op jit(solution)/shard_map/ppermute | solution.py:335
  7.4 3.6 %collective-permute-start = (f32[16,2048]{1,0:T(8,128)S(1)}, f32[16,2048]{1,0:T(8,128)S(1)}, u32[]{:S(2)}, u32[]{:S(2)}) collective-permute-start(f32[16,2048]{1,0:T(8,128)S(1)} %get-tuple-element.67.refs_0_), channel_id=1, source_target_pairs={{0,4},{4,0},{8,12},{12,8},{16,20},{20,16},{24,28},{28,24},{1,5},{5... | collective-permute-start | bytes 393224 | tf_op jit(solution)/shard_map/ppermute | solution.py:340
  11.1 6.5 %collective-permute-start.1 = (f32[16,2048]{1,0:T(8,128)S(1)}, f32[16,2048]{1,0:T(8,128)S(1)}, u32[]{:S(2)}, u32[]{:S(2)}) collective-permute-start(f32[16,2048]{1,0:T(8,128)S(1)} %chip_states.1.refs_3_.refs_0_), channel_id=1, source_target_pairs={{0,16},{4,20},{8,24},{12,28},{16,0},{20,4},{24,8},{28,12},{1,17},{... | collective-permute-start | bytes 393224 | tf_op jit(solution)/shard_map/ppermute | solution.py:340
  17.7 5.5 %collective-permute-start.2 = (f32[16,2048]{1,0:T(8,128)S(1)}, f32[16,2048]{1,0:T(8,128)S(1)}, u32[]{:S(2)}, u32[]{:S(2)}) collective-permute-start(f32[16,2048]{1,0:T(8,128)S(1)} %get-tuple-element.73.refs_8_), channel_id=1, source_target_pairs={{0,8},{4,12},{8,0},{12,4},{16,24},{20,28},{24,16},{28,20},{1,9},{5... | collective-permute-start | bytes 393224 | tf_op jit(solution)/shard_map/ppermute | solution.py:340
  25.4 9.1 %collective-permute-start.10 = (bf16[128,2048]{1,0:T(8,128)(2,1)S(1)}, bf16[128,2048]{1,0:T(8,128)(2,1)S(1)}, u32[]{:S(2)}, u32[]{:S(2)}) collective-permute-start(bf16[128,2048]{1,0:T(8,128)(2,1)S(1)} %get-tuple-element.79.refs_0_), channel_id=1, source_target_pairs={{4,0},{8,4},{12,8},{16,12},{20,16},{24,20},{28,24},{5,1},{9,5},{13... | collective-permute-start | bytes 1572872 | tf_op jit(solution)/shard_map/ppermute | solution.py:335
  28.7 2.1 %collective-permute-start.5 = (bf16[128,256]{1,0:T(8,128)(2,1)S(1)}, bf16[128,256]{1,0:T(8,128)(2,1)S(1)}, u32[]{:S(2)}, u32[]{:S(2)}) collective-permute-start(bf16[128,256]{1,0:T(8,128)(2,1)S(1)} %get-tuple-element.85), channel_id=1, source_target_pairs={{0,4},{4,0},{8,12},{12,8},{16,20},{20,16},{24,28},{28,24},{1,5},{5... | collective-permute-start | bytes 196616 | tf_op jit(solution)/shard_map/ppermute | solution.py:340
  29.9 2.2 %collective-permute-start.4 = (bf16[64,1024]{1,0:T(8,128)(2,1)S(1)}, bf16[64,1024]{1,0:T(8,128)(2,1)S(1)}, u32[]{:S(2)}, u32[]{:S(2)}) collective-permute-start(bf16[64,1024]{1,0:T(8,128)(2,1)S(1)} %get-tuple-element.84), channel_id=1, source_target_pairs={{0,4},{4,0},{8,12},{12,8},{16,20},{20,16},{24,28},{28,24},{1,5},{5... | collective-permute-start | bytes 393224 | tf_op jit(solution)/shard_map/ppermute | solution.py:340
  30.0 1.4 %collective-permute-start.6 = (bf16[128,256]{1,0:T(8,128)(2,1)S(1)}, bf16[128,256]{1,0:T(8,128)(2,1)S(1)}, u32[]{:S(2)}, u32[]{:S(2)}) collective-permute-start(bf16[128,256]{1,0:T(8,128)(2,1)S(1)} %get-tuple-element.86), channel_id=1, source_target_pairs={{0,4},{4,0},{8,12},{12,8},{16,20},{20,16},{24,28},{28,24},{1,5},{5... | collective-permute-start | bytes 196616 | tf_op jit(solution)/shard_map/ppermute | solution.py:340
  30.4 1.3 %collective-permute-start.7 = (bf16[128,256]{1,0:T(8,128)(2,1)S(1)}, bf16[128,256]{1,0:T(8,128)(2,1)S(1)}, u32[]{:S(2)}, u32[]{:S(2)}) collective-permute-start(bf16[128,256]{1,0:T(8,128)(2,1)S(1)} %get-tuple-element.87), channel_id=1, source_target_pairs={{0,4},{4,0},{8,12},{12,8},{16,20},{20,16},{24,28},{28,24},{1,5},{5... | collective-permute-start | bytes 196616 | tf_op jit(solution)/shard_map/ppermute | solution.py:340
  30.8 1.3 %collective-permute-start.8 = (bf16[128,256]{1,0:T(8,128)(2,1)S(1)}, bf16[128,256]{1,0:T(8,128)(2,1)S(1)}, u32[]{:S(2)}, u32[]{:S(2)}) collective-permute-start(bf16[128,256]{1,0:T(8,128)(2,1)S(1)} %get-tuple-element.88), channel_id=1, source_target_pairs={{0,4},{4,0},{8,12},{12,8},{16,20},{20,16},{24,28},{28,24},{1,5},{5... | collective-permute-start | bytes 196616 | tf_op jit(solution)/shard_map/ppermute | solution.py:340
  32.2 6.8 %collective-permute-start.9 = (bf16[224,384]{1,0:T(8,128)(2,1)S(1)}, bf16[224,384]{1,0:T(8,128)(2,1)S(1)}, u32[]{:S(2)}, u32[]{:S(2)}) collective-permute-start(bf16[224,384]{1,0:T(8,128)(2,1)S(1)} %get-tuple-element.89.refs_0_), channel_id=1, source_target_pairs={{0,8},{4,12},{8,0},{12,4},{16,24},{20,28},{24,16},{28,20},{1,9},{5... | collective-permute-start | bytes 516104 | tf_op jit(solution)/shard_map/ppermute | solution.py:340
  33.0 7.8 %collective-permute-start.12 = (bf16[128,640]{1,0:T(8,128)(2,1)S(1)}, bf16[128,640]{1,0:T(8,128)(2,1)S(1)}, u32[]{:S(2)}, u32[]{:S(2)}) collective-permute-start(bf16[128,640]{1,0:T(8,128)(2,1)S(1)} %get-tuple-element.96.refs_0_), channel_id=1, source_target_pairs={{0,16},{4,20},{8,24},{12,28},{16,0},{20,4},{24,8},{28,12},{1,17},{... | collective-permute-start | bytes 491528 | tf_op jit(solution)/shard_map/ppermute | solution.py:340
  39.1 7.2 %collective-permute-start.11 = (bf16[224,384]{1,0:T(8,128)(2,1)S(1)}, bf16[224,384]{1,0:T(8,128)(2,1)S(1)}, u32[]{:S(2)}, u32[]{:S(2)}) collective-permute-start(bf16[224,384]{1,0:T(8,128)(2,1)S(1)} %get-tuple-element.95.refs_0_), channel_id=1, source_target_pairs={{0,16},{4,20},{8,24},{12,28},{16,0},{20,4},{24,8},{28,12},{1,17},{... | collective-permute-start | bytes 516104 | tf_op jit(solution)/shard_map/ppermute | solution.py:340
  40.8 5.5 %collective-permute-start.13 = (bf16[128,640]{1,0:T(8,128)(2,1)S(1)}, bf16[128,640]{1,0:T(8,128)(2,1)S(1)}, u32[]{:S(2)}, u32[]{:S(2)}) collective-permute-start(bf16[128,640]{1,0:T(8,128)(2,1)S(1)} %go_right.1.refs_2_), channel_id=1, source_target_pairs={{0,8},{4,12},{8,0},{12,4},{16,24},{20,28},{24,16},{28,20},{1,9},{5... | collective-permute-start | bytes 491528 | tf_op jit(solution)/shard_map/ppermute | solution.py:340
  46.4 1.7 %collective-permute-start.14 = (bf16[160,1024]{1,0:T(8,128)(2,1)S(1)}, bf16[160,1024]{1,0:T(8,128)(2,1)S(1)}, u32[]{:S(2)}, u32[]{:S(2)}) collective-permute-start(bf16[160,1024]{1,0:T(8,128)(2,1)S(1)} %get-tuple-element.103.refs_7_), channel_id=1, source_target_pairs={{0,4},{4,0},{8,12},{12,8},{16,20},{20,16},{24,28},{28,24},{1,5},{5... | collective-permute-start | bytes 983048 | tf_op jit(solution)/shard_map/ppermute | solution.py:340
